TPU v7x, 32 devices: a whole 2x2x4 slice. The times are simulated.
32 devices in a mesh: seq: 4 (over y, x), ctx: 8 (over z, core).
Axes of the slice: x: 2, y: 2, z: 4, core: 2. Of those that a mesh axis runs over, the one named last changes fastest.
Arguments:
- tokens: bfloat16 [2, 4, 1024, 2048], P(None, 'seq', 'ctx'), may hold values from -6 to 6
- lengths: int32 [2, 4], P(None, 'seq'), may hold values from 256 to 1024, as said below
- cotangent: bfloat16 [2, 4, 1024, 2048], P(None, 'seq', 'ctx'), may hold values from -6 to 6
- attn_gain: bfloat16 [2048], P(('seq', 'ctx')), may hold values from 0.5 to 1.5
- w_query: bfloat16 [2048, 2048], P(('seq', 'ctx')), may hold values from -0.125 to 0.125
- w_key: bfloat16 [2048, 512], P(('seq', 'ctx')), may hold values from -0.125 to 0.125
- w_value: bfloat16 [2048, 512], P(('seq', 'ctx')), may hold values from -0.125 to 0.125
- w_out: bfloat16 [2048, 2048], P(('seq', 'ctx')), may hold values from -3 to 3
- mlp_gain: bfloat16 [2048], P(('seq', 'ctx')), may hold values from 0.5 to 1.5
- w_gate: bfloat16 [2048, 8192], P('seq', 'ctx'), may hold values from -0.125 to 0.125
- w_up: bfloat16 [2048, 8192], P('seq', 'ctx'), may hold values from -0.125 to 0.125
- w_down: bfloat16 [8192, 2048], P('ctx', 'seq'), may hold values from -0.0625 to 0.0625
Outputs:
- activations: bfloat16 [2, 4, 1024, 2048], P(None, 'seq', 'ctx')
- input_grad: float32 [2, 4, 1024, 2048], P(None, 'seq', 'ctx')
- grad_attn_gain: float32 [2048], P(('seq', 'ctx'))
- grad_query: float32 [2048, 2048], P(('seq', 'ctx'))
- grad_key: float32 [2048, 512], P(('seq', 'ctx'))
- grad_value: float32 [2048, 512], P(('seq', 'ctx'))
- grad_out: float32 [2048, 2048], P(('seq', 'ctx'))
- grad_mlp_gain: float32 [2048], P(('seq', 'ctx'))
- grad_gate: float32 [2048, 8192], P('seq', 'ctx')
- grad_up: float32 [2048, 8192], P('seq', 'ctx')
- grad_down: float32 [8192, 2048], P('ctx', 'seq')
Inputs may be any that keep to these rules, and one draw needn't show every extreme that they name: A sequence's valid slots are its first lengths slots; in every draw some sequence has exactly 1024.
All inputs are finite; a program needn't handle non-finite values.
Results may differ from a plain program's by a relative error of at most 0.015.
Values may be sent and summed in bfloat16 or wider, within the bound.
No kernel may reach another device: no remote copies, remote signals or barrier semaphores. Data moves between devices by JAX's collectives and lax.ppermute only.
A program may use at most 256 MiB of HBM per device.

v0:
```python
import math

import jax
import jax.numpy as jnp
from jax import lax
from jax.sharding import PartitionSpec as P

HEAD_DIM = 64


EPSILON = 1e-05
ROPE_BASE = 500000.0


def rms_parts(values, gain):
    inverse = lax.rsqrt(jnp.mean(values * values, axis=-1, keepdims=True) + EPSILON)
    plain = values * inverse
    return (plain * gain, plain, inverse)


def rms_back(grad_in, plain, inverse, gain):
    scaled = grad_in * gain
    back = inverse * (scaled - plain * jnp.mean(scaled * plain, axis=-1, keepdims=True))
    return (back, jnp.sum(grad_in * plain, axis=(0, 1)))


def scaled_frequency():
    half_dim = HEAD_DIM // 2
    base_freq = ROPE_BASE ** (-jnp.arange(half_dim, dtype=jnp.float32) * 2.0 / HEAD_DIM)
    wave = 2.0 * math.pi / base_freq
    smooth = (8192.0 / wave - 1.0) / 3.0
    middle = (1.0 - smooth) * base_freq / 32.0 + smooth * base_freq
    return jnp.where(wave < 2048.0, base_freq, jnp.where(wave > 8192.0, base_freq / 32.0, middle))


def rope_tables(first_slot, slot_count):
    frequency = scaled_frequency()
    positions = (first_slot + jnp.arange(slot_count)).astype(jnp.float32)
    angles = positions[:, None] * frequency[None, :]
    return (jnp.cos(angles), jnp.sin(angles))


def rotate(values, cosine, sine_table):
    half_dim = values.shape[-1] // 2
    first_half = values[..., :half_dim]
    second_half = values[..., half_dim:]
    cos_part = cosine[:, None, :]
    sin_part = sine_table[:, None, :]
    return jnp.concatenate(
        [
            first_half * cos_part - second_half * sin_part,
            second_half * cos_part + first_half * sin_part,
        ],
        axis=-1,
    )


def body(
    tokens,
    lengths,
    cotangent,
    attn_gain,
    w_query,
    w_key,
    w_value,
    w_out,
    mlp_gain,
    w_gate,
    w_up,
    w_down,
):
    batches = tokens.shape[0]
    slot_count = tokens.shape[2]
    model_width = tokens.shape[3]
    ctx_size = lax.axis_size("ctx")
    full_len = slot_count * ctx_size
    first_slot = lax.axis_index("ctx") * slot_count
    query_width = w_query.shape[1]
    kv_width = w_key.shape[1]
    heads_q = query_width // HEAD_DIM
    heads_kv = kv_width // HEAD_DIM
    per_kv = heads_q // heads_kv
    scaling = 1.0 / math.sqrt(HEAD_DIM)
    row_count = batches * slot_count
    inputs_f = tokens[:, 0].astype(jnp.float32)
    cot_f = cotangent[:, 0].astype(jnp.float32)
    seq_len = lengths[:, 0]
    slot_pos = first_slot + jnp.arange(slot_count)
    key_pos = jnp.arange(full_len)
    valid = (slot_pos[None, :] < seq_len[:, None]).astype(jnp.float32)[:, :, None]
    cosine, sine_table = rope_tables(first_slot, slot_count)
    limits = jnp.repeat(seq_len, heads_kv)

    def fetch_attention():
        return (
            lax.all_gather(attn_gain, ("seq", "ctx"), axis=0, tiled=True),
            lax.all_gather(w_query, ("seq", "ctx"), axis=0, tiled=True),
            lax.all_gather(w_key, ("seq", "ctx"), axis=0, tiled=True),
            lax.all_gather(w_value, ("seq", "ctx"), axis=0, tiled=True),
            lax.all_gather(w_out, ("seq", "ctx"), axis=0, tiled=True),
            lax.all_gather(mlp_gain, ("seq", "ctx"), axis=0, tiled=True),
        )

    def fetch_rows():
        return (
            lax.all_gather(w_gate, "seq", axis=0, tiled=True),
            lax.all_gather(w_up, "seq", axis=0, tiled=True),
            lax.all_gather(w_down, "seq", axis=1, tiled=True),
        )

    def head_scores(query_head, key_head, limit):
        allowed = (key_pos[None, :] <= slot_pos[:, None]) & (key_pos[None, :] < limit)
        scores = (
            jnp.einsum("igd,jd->gij", query_head, key_head, preferred_element_type=jnp.float32)
            * scaling
        )
        return jnp.where(allowed[None], scores, -1e30)

    def split_heads(array, length):
        return (
            array.reshape(batches, length, heads_kv, HEAD_DIM)
            .transpose(0, 2, 1, 3)
            .reshape(batches * heads_kv, length, HEAD_DIM)
        )

    def split_queries(array):
        return (
            array.reshape(batches, slot_count, heads_kv, per_kv, HEAD_DIM)
            .transpose(0, 2, 1, 3, 4)
            .reshape(batches * heads_kv, slot_count, per_kv, HEAD_DIM)
        )

    def join_queries(array):
        return (
            array.reshape(batches, heads_kv, slot_count, per_kv, HEAD_DIM)
            .transpose(0, 2, 1, 3, 4)
            .reshape(batches, slot_count, heads_q, HEAD_DIM)
        )

    def join_keys(array):
        return (
            array.reshape(batches, heads_kv, full_len, HEAD_DIM)
            .transpose(0, 2, 1, 3)
            .reshape(batches, full_len, kv_width)
        )

    gain_a, query_w, key_w, value_w, out_w, gain_m = fetch_attention()
    gain_af = gain_a.astype(jnp.float32)
    gain_mf = gain_m.astype(jnp.float32)
    normed_a, plain_a, inverse_a = rms_parts(inputs_f, gain_af)
    normed_low = normed_a.astype(jnp.bfloat16).reshape(row_count, model_width)
    query_raw = jnp.dot(normed_low, query_w, preferred_element_type=jnp.float32)
    key_raw = jnp.dot(normed_low, key_w, preferred_element_type=jnp.float32)
    value_raw = jnp.dot(normed_low, value_w, preferred_element_type=jnp.float32)
    queries = rotate(
        query_raw.reshape(batches, slot_count, heads_q, HEAD_DIM), cosine, sine_table
    ).astype(jnp.bfloat16)
    keys_rot = (
        rotate(key_raw.reshape(batches, slot_count, heads_kv, HEAD_DIM), cosine, sine_table)
        .astype(jnp.bfloat16)
        .reshape(batches, slot_count, kv_width)
    )
    values_low = value_raw.astype(jnp.bfloat16).reshape(batches, slot_count, kv_width)
    keys_all, values_all = (
        lax.all_gather(keys_rot, "ctx", axis=1, tiled=True),
        lax.all_gather(values_low, "ctx", axis=1, tiled=True),
    )
    query_items = split_queries(queries)
    key_items = split_heads(keys_all, full_len)
    value_items = split_heads(values_all, full_len)

    def forward_head(operands):
        query_head, key_head, value_head, limit = operands
        scores = head_scores(query_head, key_head, limit)
        row_max = jnp.max(scores, axis=-1, keepdims=True)
        shifted = jnp.exp(scores - row_max)
        row_total = jnp.sum(shifted, axis=-1, keepdims=True)
        attn_probs = (shifted / row_total).astype(jnp.bfloat16)
        head_out = jnp.einsum(
            "gij,jd->igd", attn_probs, value_head, preferred_element_type=jnp.float32
        )
        return (head_out, row_max + jnp.log(row_total))

    head_outs, log_sums = lax.map(forward_head, (query_items, key_items, value_items, limits))
    attended = join_queries(head_outs).reshape(row_count, query_width).astype(jnp.bfloat16)
    branch_a = jnp.dot(attended, out_w, preferred_element_type=jnp.float32)
    residual = inputs_f + branch_a.reshape(batches, slot_count, model_width)
    normed_m, plain_m, inverse_m = rms_parts(residual, gain_mf)
    mlp_in = normed_m.astype(jnp.bfloat16)
    gate_rows, up_rows, down_rows = fetch_rows()
    group_in = lax.all_gather(mlp_in, "ctx", axis=1, tiled=True).reshape(
        batches * full_len, model_width
    )
    gate_val = jnp.dot(group_in, gate_rows, preferred_element_type=jnp.float32)
    up_val = jnp.dot(group_in, up_rows, preferred_element_type=jnp.float32)
    sigmoid_g = 1.0 / (1.0 + jnp.exp(-gate_val))
    activated = gate_val * sigmoid_g
    slope = sigmoid_g * (1.0 + gate_val * (1.0 - sigmoid_g))
    hidden = (activated * up_val).astype(jnp.bfloat16)
    partial_out = jnp.dot(hidden, down_rows, preferred_element_type=jnp.float32).reshape(
        batches, full_len, model_width
    )
    branch_m = lax.psum_scatter(
        partial_out.astype(jnp.bfloat16), "ctx", scatter_dimension=1, tiled=True
    ).astype(jnp.float32)
    activations = (residual + branch_m).astype(jnp.bfloat16)[:, None]
    d_output = cot_f * valid
    d_branch = d_output.astype(jnp.bfloat16)
    gate_rows, up_rows, down_rows = fetch_rows()
    d_group = lax.all_gather(d_branch, "ctx", axis=1, tiled=True).reshape(
        batches * full_len, model_width
    )
    d_hidden = jnp.einsum("rd,fd->rf", d_group, down_rows, preferred_element_type=jnp.float32)
    d_gate = (d_hidden * up_val * slope).astype(jnp.bfloat16)
    d_up = (d_hidden * activated).astype(jnp.bfloat16)
    grad_gate = jnp.einsum("rd,rf->df", group_in, d_gate, preferred_element_type=jnp.float32)
    grad_up = jnp.einsum("rd,rf->df", group_in, d_up, preferred_element_type=jnp.float32)
    grad_down = jnp.einsum("rf,rd->fd", hidden, d_group, preferred_element_type=jnp.float32)
    partial_back = (
        jnp.einsum("rf,df->rd", d_gate, gate_rows, preferred_element_type=jnp.float32)
        + jnp.einsum("rf,df->rd", d_up, up_rows, preferred_element_type=jnp.float32)
    ).reshape(batches, full_len, model_width)
    d_normed_m = lax.psum_scatter(partial_back, "ctx", scatter_dimension=1, tiled=True)
    grad_gate, grad_up, grad_down = (
        lax.psum_scatter(
            grad_gate.astype(jnp.bfloat16), "seq", scatter_dimension=0, tiled=True
        ).astype(jnp.float32),
        lax.psum_scatter(
            grad_up.astype(jnp.bfloat16), "seq", scatter_dimension=0, tiled=True
        ).astype(jnp.float32),
        lax.psum_scatter(
            grad_down.astype(jnp.bfloat16), "seq", scatter_dimension=1, tiled=True
        ).astype(jnp.float32),
    )
    back_m, grad_gain_m = rms_back(d_normed_m, plain_m, inverse_m, gain_mf)
    d_resid = d_output + back_m
    gain_a, query_w, key_w, value_w, out_w, gain_m = fetch_attention()
    d_attn = d_resid.astype(jnp.bfloat16).reshape(row_count, model_width)
    grad_out = jnp.einsum("rh,rd->hd", attended, d_attn, preferred_element_type=jnp.float32)
    d_attended = jnp.einsum("rd,hd->rh", d_attn, out_w, preferred_element_type=jnp.float32).astype(
        jnp.bfloat16
    )
    d_items = split_queries(d_attended.reshape(batches, slot_count, heads_q, HEAD_DIM))

    def backward_head(operands):
        query_head, key_head, value_head, limit, log_sum, d_head = operands
        scores = head_scores(query_head, key_head, limit)
        attn_probs = jnp.exp(scores - log_sum)
        probs_low = attn_probs.astype(jnp.bfloat16)
        d_probs = jnp.einsum("igd,jd->gij", d_head, value_head, preferred_element_type=jnp.float32)
        d_scores = attn_probs * (d_probs - jnp.sum(d_probs * attn_probs, axis=-1, keepdims=True))
        d_scores_low = d_scores.astype(jnp.bfloat16)
        d_query = (
            jnp.einsum("gij,jd->igd", d_scores_low, key_head, preferred_element_type=jnp.float32)
            * scaling
        )
        d_key = (
            jnp.einsum("gij,igd->jd", d_scores_low, query_head, preferred_element_type=jnp.float32)
            * scaling
        )
        d_value = jnp.einsum("gij,igd->jd", probs_low, d_head, preferred_element_type=jnp.float32)
        return (d_query, d_key, d_value)

    d_query_items, d_key_items, d_value_items = lax.map(
        backward_head, (query_items, key_items, value_items, limits, log_sums, d_items)
    )
    key_sum, value_sum = (
        lax.psum_scatter(join_keys(d_key_items), "ctx", scatter_dimension=1, tiled=True),
        lax.psum_scatter(join_keys(d_value_items), "ctx", scatter_dimension=1, tiled=True),
    )
    query_grad = (
        rotate(join_queries(d_query_items), cosine, -sine_table)
        .astype(jnp.bfloat16)
        .reshape(row_count, query_width)
    )
    key_grad = (
        rotate(key_sum.reshape(batches, slot_count, heads_kv, HEAD_DIM), cosine, -sine_table)
        .astype(jnp.bfloat16)
        .reshape(row_count, kv_width)
    )
    value_grad = value_sum.astype(jnp.bfloat16).reshape(row_count, kv_width)
    grad_query = jnp.einsum("rd,rh->dh", normed_low, query_grad, preferred_element_type=jnp.float32)
    grad_key = jnp.einsum("rd,rh->dh", normed_low, key_grad, preferred_element_type=jnp.float32)
    grad_value = jnp.einsum("rd,rh->dh", normed_low, value_grad, preferred_element_type=jnp.float32)
    d_normed_a = jnp.einsum("rh,dh->rd", query_grad, query_w, preferred_element_type=jnp.float32)
    d_normed_a = d_normed_a + jnp.einsum(
        "rh,dh->rd", key_grad, key_w, preferred_element_type=jnp.float32
    )
    d_normed_a = d_normed_a + jnp.einsum(
        "rh,dh->rd", value_grad, value_w, preferred_element_type=jnp.float32
    )
    back_a, grad_gain_a = rms_back(
        d_normed_a.reshape(batches, slot_count, model_width), plain_a, inverse_a, gain_af
    )
    input_grad = (d_resid + back_a)[:, None]
    grad_gain_a, grad_query, grad_key, grad_value, grad_out, grad_gain_m = (
        lax.psum_scatter(grad_gain_a, ("seq", "ctx"), scatter_dimension=0, tiled=True),
        lax.psum_scatter(grad_query, ("seq", "ctx"), scatter_dimension=0, tiled=True),
        lax.psum_scatter(grad_key, ("seq", "ctx"), scatter_dimension=0, tiled=True),
        lax.psum_scatter(grad_value, ("seq", "ctx"), scatter_dimension=0, tiled=True),
        lax.psum_scatter(grad_out, ("seq", "ctx"), scatter_dimension=0, tiled=True),
        lax.psum_scatter(grad_gain_m, ("seq", "ctx"), scatter_dimension=0, tiled=True),
    )
    return (
        activations,
        input_grad,
        grad_gain_a,
        grad_query,
        grad_key,
        grad_value,
        grad_out,
        grad_gain_m,
        grad_gate,
        grad_up,
        grad_down,
    )


def solution(mesh):
    placed = (
        P(None, "seq", "ctx", None),
        P(None, "seq"),
        P(None, "seq", "ctx", None),
        P(("seq", "ctx")),
        P(("seq", "ctx"), None),
        P(("seq", "ctx"), None),
        P(("seq", "ctx"), None),
        P(("seq", "ctx"), None),
        P(("seq", "ctx")),
        P("seq", "ctx"),
        P("seq", "ctx"),
        P("ctx", "seq"),
    )
    return jax.shard_map(
        body,
        mesh=mesh,
        in_specs=placed,
        out_specs=(
            P(None, "seq", "ctx", None),
            P(None, "seq", "ctx", None),
            P(("seq", "ctx")),
            P(("seq", "ctx"), None),
            P(("seq", "ctx"), None),
            P(("seq", "ctx"), None),
            P(("seq", "ctx"), None),
            P(("seq", "ctx")),
            P("seq", "ctx"),
            P("seq", "ctx"),
            P("ctx", "seq"),
        ),
        check_vma=False,
    )
```

profile of v0, /device:TPU:0, one launch (start us, length us, event | category | flops | bytes accessed | tf_op | source)
XLA Modules:
  0.0 2098.4 jit_solution(12120319820817513001)
XLA Ops:
  11.2 42.1 %all-reduce.5 = (bf16[2048]{0:T(1024)(128)(2,1)S(1)}, bf16[2048]{0:T(1024)(128)(2,1)S(1)}) all-reduce(bf16[2048]{0:T(1024)(128)(2,1)S(1)} %dynamic-update-slice, bf16[2048]{0:T(1024)(128)(2,1)S(1)} %dynamic-update-slice.1), channel_id=1, replica_groups=mesh['seq'=4,'ctx'=8] {'seq','ctx'}, use_global_device_ids=true, to_apply=%add | all-reduce | flops 4096 | bytes 16384
  55.9 14.3 all-gather.16.cloned.1.call-done
  77.7 50.9 %all-gather.12.cloned.1.call-done = bf16[2048,512]{1,0:T(8,128)(2,1)} async-done(((bf16[64,512]{1,0:T(8,128)(2,1)}), bf16[2048,512]{1,0:T(8,128)(2,1)}) %all-gather.12.cloned.1.call-update) | async-done | bytes 2097168 | tf_op jit(solution)/shard_map/all_gather | solution.py:99
  134.5 73.3 %all-gather.20.cloned.1.call-done = bf16[2048,2048]{1,0:T(8,128)(2,1)} async-done(((bf16[64,2048]{1,0:T(8,128)(2,1)}), bf16[2048,2048]{1,0:T(8,128)(2,1)}) %all-gather.20.cloned.1.call-update) | async-done | bytes 8388624 | tf_op jit(solution)/shard_map/all_gather | solution.py:97
  239.4 31.9 %all-gather.14.cloned.1.call-done = bf16[2,1024,512]{1,2,0:T(8,128)(2,1)} async-done(((bf16[2,128,512]{1,2,0:T(8,128)(2,1)}), bf16[2,1024,512]{1,2,0:T(8,128)(2,1)}) %all-gather.14.cloned.1.call-update) | async-done | bytes 2097168 | tf_op jit(solution)/shard_map/all_gather | solution.py:166
  271.3 82.8 %while.32 = (s32[]{:T(128)}, bf16[16,128,4,64]{1,3,2,0:T(8,128)(2,1)}, f32[16,4,128,1]{2,1,3,0:T(4,128)S(1)}, bf16[16,1024,64]{1,2,0:T(8,128)(2,1)}, s32[16]{0:T...) while((s32[]{:T(128)}, ...), condition=%wide.region_4.5_spmd.clone.clone.clone, body=%wide.region_1.4_spmd.clone.clone.sunk.clone | while | flops 138674816 | bytes 7033965 | solution.py:184
  364.5 39.5 %all-gather.26.cloned.1.call-done = bf16[2048,1024]{1,0:T(8,128)(2,1)} async-done(((bf16[512,1024]{1,0:T(8,128)(2,1)}), bf16[2048,1024]{1,0:T(8,128)(2,1)}) %all-gather.26.cloned.1.call-update) | async-done | bytes 4194320 | tf_op jit(solution)/shard_map/all_gather | solution.py:106
  404.0 84.3 %all-gather.24.cloned.1.call-done = bf16[2,1024,2048]{2,1,0:T(8,128)(2,1)} async-done(((bf16[2,128,2048]{2,1,0:T(8,128)(2,1)}), bf16[2,1024,2048]{2,1,0:T(8,128)(2,1)}) %all-gather.24.cloned.1.call-update) | async-done | bytes 8388624 | tf_op jit(solution)/shard_map/all_gather | solution.py:191
  488.3 14.5 fusion.106
  502.8 38.6 %all-gather.28.cloned.1.call-done = bf16[2048,1024]{1,0:T(8,128)(2,1)} async-done(((bf16[512,1024]{1,0:T(8,128)(2,1)}), bf16[2048,1024]{1,0:T(8,128)(2,1)}) %all-gather.28.cloned.1.call-update) | async-done | bytes 4194320 | tf_op jit(solution)/shard_map/all_gather | solution.py:107
  541.4 14.4 fusion.107
  555.8 39.9 %all-gather.30.cloned.1.call-done = bf16[1024,2048]{1,0:T(8,128)(2,1)} async-done(((bf16[1024,512]{1,0:T(8,128)(2,1)}), bf16[1024,2048]{1,0:T(8,128)(2,1)}) %all-gather.30.cloned.1.call-update) | async-done | bytes 4194320 | tf_op jit(solution)/shard_map/all_gather | solution.py:108
  595.7 84.3 %all-gather.32.cloned.1.call-done = bf16[2,1024,2048]{2,1,0:T(8,128)(2,1)} async-done(((bf16[2,128,2048]{2,1,0:T(8,128)(2,1)}), bf16[2,1024,2048]{2,1,0:T(8,128)(2,1)}) %all-gather.32.cloned.1.call-update) | async-done | bytes 8388624 | tf_op jit(solution)/shard_map/all_gather | solution.py:210
  679.9 23.5 %multiply_convert_fusion = (bf16[2048,1024]{1,0:T(8,128)(2,1)}, bf16[2048,1024]{1,0:T(8,128)(2,1)}, bf16[2048,1024]{1,0:T(8,128)(2,1)}) fusion(f32[2048,1024]{1,0:T(8,128)} %fusion.106, f32[2048,1024]{1,0:T(8,128)} %fusion.107, bf16[2048,2048]{1,0:T(8,128)(2,1)} %bitcast.400, bf16[1024,2048]{1,0:T(8,128)(2,1)} %all-gather.30.cloned.1.call-done), kind=kOutput, calls=%fused_computation.70 | convolution fusion | flops 8621391872 | bytes 41943040 | tf_op jit(solution)/shard_map/rd,fd->rf/dot_general | solution.py:213
  703.4 15.5 fusion.108
  718.9 17.4 convolution_add_fusion
  736.4 166.9 %reduce-scatter.14.cloned.1.call-done = f32[2,128,2048]{2,1,0:T(8,128)} async-done(((f32[2,1024,2048]{2,1,0:T(8,128)}), f32[2,128,2048]{2,1,0:T(8,128)}) %reduce-scatter.14.cloned.1.call-update) | async-done | bytes 2097168 | tf_op jit(solution)/shard_map/reduce_scatter | solution.py:223
  918.2 156.2 %while.33 = (s32[]{:T(128)}, f32[16,128,4,64]{1,3,2,0:T(8,128)}, f32[16,1024,64]{1,2,0:T(8,128)}, f32[16,1024,64]{1,2,0:T(8,128)}, bf16[16,1024,64]{1,2,0:T(8,12...) while((s32[]{:T(128)}, f32[16,128,4,64]{1,3,2,0:T(8,128)}, ...), condition=%wide.region_11.12_spmd.clone.clone.clone, body=%wide.region_9.11_spmd.clone.clone.sunk.clone | while | flops 340624000 | bytes 17320068 | solution.py:264
  1075.0 14.5 convolution_convert_fusion.3
  1089.7 14.1 convolution_convert_fusion.2
  1103.9 14.4 convolution_convert_fusion.1
  1118.3 14.0 convolution_convert_fusion
  1137.3 35.9 %reduce-scatter.18.cloned.1.call-done = f32[2,128,512]{1,2,0:T(8,128)} async-done(((f32[2,1024,512]{1,2,0:T(8,128)}), f32[2,128,512]{1,2,0:T(8,128)}) %reduce-scatter.18.cloned.1.call-update) | async-done | bytes 524304 | tf_op jit(solution)/shard_map/reduce_scatter | solution.py:269
  1201.3 25.7 %reduce-scatter.28.cloned.1.call-done = bf16[512,1024]{1,0:T(8,128)(2,1)} async-done(((bf16[2048,1024]{1,0:T(8,128)(2,1)}), bf16[512,1024]{1,0:T(8,128)(2,1)}) %reduce-scatter.28.cloned.1.call-update) | async-done | bytes 1048592 | tf_op jit(solution)/shard_map/reduce_scatter | solution.py:225
  1229.7 53.0 %reduce-scatter.30.cloned.1.call-done = bf16[512,1024]{1,0:T(8,128)(2,1)} async-done(((bf16[2048,1024]{1,0:T(8,128)(2,1)}), bf16[512,1024]{1,0:T(8,128)(2,1)}) %reduce-scatter.30.cloned.1.call-update) | async-done | bytes 1048592 | tf_op jit(solution)/shard_map/reduce_scatter | solution.py:228
  1285.6 52.7 %reduce-scatter.32.cloned.1.call-done = bf16[1024,512]{1,0:T(8,128)(2,1)} async-done(((bf16[1024,2048]{1,0:T(8,128)(2,1)}), bf16[1024,512]{1,0:T(8,128)(2,1)}) %reduce-scatter.32.cloned.1.call-update) | async-done | bytes 1048592 | tf_op jit(solution)/shard_map/reduce_scatter | solution.py:231
  1355.5 41.3 %all-reduce.4 = (f32[2048]{0:T(1024)S(1)}, f32[2048]{0:T(1024)S(1)}) all-reduce(f32[2048]{0:T(1024)S(1)} %get-tuple-element.276, f32[2048]{0:T(1024)S(1)} %get-tuple-element.274), channel_id=6, replica_groups=mesh['seq'=4,'ctx'=8] {'seq','ctx'}, use_global_device_ids=true, to_apply=%region_16.17.clone | all-reduce | flops 4096 | bytes 32768
  1397.9 33.3 %reduce-scatter.12.cloned.1.call-done = bf16[2,128,2048]{2,1,0:T(8,128)(2,1)} async-done(((bf16[2,1024,2048]{2,1,0:T(8,128)(2,1)}), bf16[2,128,2048]{2,1,0:T(8,128)(2,1)}) %reduce-scatter.12.cloned.1.call-update) | async-done | bytes 1048592 | tf_op jit(solution)/shard_map/reduce_scatter | solution.py:203
  1437.0 137.8 %reduce-scatter.22.cloned.1.call-done = f32[64,512]{1,0:T(8,128)} async-done(((f32[2048,512]{1,0:T(8,128)}), f32[64,512]{1,0:T(8,128)}) %reduce-scatter.22.cloned.1.call-update) | async-done | bytes 131088 | tf_op jit(solution)/shard_map/reduce_scatter | solution.py:299
  1574.8 142.6 %reduce-scatter.24.cloned.1.call-done = f32[64,512]{1,0:T(8,128)} async-done(((f32[2048,512]{1,0:T(8,128)}), f32[64,512]{1,0:T(8,128)}) %reduce-scatter.24.cloned.1.call-update) | async-done | bytes 131088 | tf_op jit(solution)/shard_map/reduce_scatter | solution.py:300
  1717.5 186.5 %reduce-scatter.26.cloned.1.call-done = f32[64,2048]{1,0:T(8,128)} async-done(((f32[2048,2048]{1,0:T(8,128)}), f32[64,2048]{1,0:T(8,128)}) %reduce-scatter.26.cloned.1.call-update) | async-done | bytes 524304 | tf_op jit(solution)/shard_map/reduce_scatter | solution.py:301
  1904.0 187.4 %reduce-scatter.20.cloned.1.call-done = f32[64,2048]{1,0:T(8,128)} async-done(((f32[2048,2048]{1,0:T(8,128)}), f32[64,2048]{1,0:T(8,128)}) %reduce-scatter.20.cloned.1.call-update) | async-done | bytes 524304 | tf_op jit(solution)/shard_map/reduce_scatter | solution.py:298
  (467 shorter events, 377.7 us)
Async XLA Ops:
  7.2 48.4 %copy-start = (bf16[2,1,128,2048]{3,2,1,0:T(8,128)(2,1)S(1)}, bf16[2,1,128,2048]{3,2,1,0:T(8,128)(2,1)}, u32[]{:S(2)}) copy-start(bf16[2,1,128,2048]{3,2,1,0:T(8,128)(2,1)} %param.16) | copy-start | bytes 3145732
  7.2 63.1 %all-gather.16.cloned.1.call-start = ((), (), s32[]{:S(2)}) async-start(), calls=%async_computation.13 | async-start | bytes 2162688 | tf_op jit(solution)/shard_map/all_gather | solution.py:98
  7.9 120.7 %all-gather.12.cloned.1.call-start = ((), (), s32[]{:S(2)}) async-start(), calls=%async_computation.11 | async-start | bytes 2162688 | tf_op jit(solution)/shard_map/all_gather | solution.py:99
  8.7 199.2 %all-gather.20.cloned.1.call-start = ((), (), s32[]{:S(2)}) async-start(), calls=%async_computation.15 | async-start | bytes 8650752 | tf_op jit(solution)/shard_map/all_gather | solution.py:97
  9.4 230.0 %all-gather.18.cloned.1.call-start = ((), (), s32[]{:S(2)}) async-start(), calls=%async_computation.14 | async-start | bytes 2359296 | tf_op jit(solution)/shard_map/all_gather | solution.py:165
  53.3 24.1 %copy-start.14 = (f32[2048]{0:T(1024)}, f32[2048]{0:T(1024)S(1)}, u32[]{:S(2)}) copy-start(f32[2048]{0:T(1024)S(1)} %convert_element_type.199) | copy-start | bytes 24580
  54.8 19.3 copy-start.19
  54.9 22.5 %copy-start.21 = (f32[256]{0:T(256)}, f32[256]{0:T(256)S(1)}, u32[]{:S(2)}) copy-start(f32[256]{0:T(256)S(1)} %get-tuple-element.341) | copy-start | bytes 3076
  55.6 169.6 %copy-start.16 = (f32[128,32]{0,1:T(8,128)}, f32[128,32]{0,1:T(8,128)S(1)}, u32[]{:S(2)}) copy-start(f32[128,32]{0,1:T(8,128)S(1)} %get-tuple-element.339) | copy-start | bytes 49156
  55.9 164.3 %copy-start.3 = (bf16[2,1,128,2048]{3,2,0,1:T(8,128)(2,1)}, bf16[2,1,128,2048]{3,2,0,1:T(8,128)(2,1)S(1)}, u32[]{:S(2)}) copy-start(bf16[2,1,128,2048]{3,2,0,1:T(8,128)(2,1)S(1)} %fusion.76) | copy-start | bytes 3145732
  77.3 194.0 %all-gather.14.cloned.1.call-start = ((), (), s32[]{:S(2)}) async-start(), calls=%async_computation.12 | async-start | bytes 2359296 | tf_op jit(solution)/shard_map/all_gather | solution.py:166
  131.8 222.4 %all-gather.22.cloned.1.call-start = ((), (), s32[]{:S(2)}) async-start(), calls=%async_computation.16 | async-start | bytes 8650752 | tf_op jit(solution)/shard_map/all_gather | solution.py:100
  132.4 271.6 %all-gather.26.cloned.1.call-start = ((), (), s32[]{:S(2)}) async-start(), calls=%async_computation.18 | async-start | bytes 5242880 | tf_op jit(solution)/shard_map/all_gather | solution.py:106
  133.1 355.2 %all-gather.24.cloned.1.call-start = ((), (), s32[]{:S(2)}) async-start(), calls=%async_computation.17 | async-start | bytes 9437184 | tf_op jit(solution)/shard_map/all_gather | solution.py:191
  361.6 179.8 %all-gather.28.cloned.1.call-start = ((), (), s32[]{:S(2)}) async-start(), calls=%async_computation.19 | async-start | bytes 5242880 | tf_op jit(solution)/shard_map/all_gather | solution.py:107
  362.4 233.3 %all-gather.30.cloned.1.call-start = ((), (), s32[]{:S(2)}) async-start(), calls=%async_computation.20 | async-start | bytes 5242880 | tf_op jit(solution)/shard_map/all_gather | solution.py:108
  363.0 317.0 %all-gather.32.cloned.1.call-start = ((), (), s32[]{:S(2)}) async-start(), calls=%async_computation.22 | async-start | bytes 9437184 | tf_op jit(solution)/shard_map/all_gather | solution.py:210
  364.3 538.9 %reduce-scatter.14.cloned.1.call-start = ((), (), s32[]{:S(2)}) async-start(), calls=%async_computation.23 | async-start | bytes 18874368 | tf_op jit(solution)/shard_map/reduce_scatter | solution.py:223
  703.4 15.5 copy-start.24
  736.3 396.1 %reduce-scatter.16.cloned.1.call-start = ((), (), s32[]{:S(2)}) async-start(), calls=%async_computation.24 | async-start | bytes 4718592 | tf_op jit(solution)/shard_map/reduce_scatter | solution.py:268
  1074.4 98.8 %reduce-scatter.18.cloned.1.call-start = ((), (), s32[]{:S(2)}) async-start(), calls=%async_computation.25 | async-start | bytes 4718592 | tf_op jit(solution)/shard_map/reduce_scatter | solution.py:269
  1075.0 152.0 %reduce-scatter.28.cloned.1.call-start = ((), (), s32[]{:S(2)}) async-start(), calls=%async_computation.30 | async-start | bytes 5242880 | tf_op jit(solution)/shard_map/reduce_scatter | solution.py:225
  1089.6 193.2 %reduce-scatter.30.cloned.1.call-start = ((), (), s32[]{:S(2)}) async-start(), calls=%async_computation.31 | async-start | bytes 5242880 | tf_op jit(solution)/shard_map/reduce_scatter | solution.py:228
  1103.8 234.5 %reduce-scatter.32.cloned.1.call-start = ((), (), s32[]{:S(2)}) async-start(), calls=%async_computation.32 | async-start | bytes 5242880 | tf_op jit(solution)/shard_map/reduce_scatter | solution.py:231
  1118.2 313.0 %reduce-scatter.12.cloned.1.call-start = ((), (), s32[]{:S(2)}) async-start(), calls=%async_computation.21 | async-start | bytes 9437184 | tf_op jit(solution)/shard_map/reduce_scatter | solution.py:203
  1132.3 442.5 %reduce-scatter.22.cloned.1.call-start = ((), (), s32[]{:S(2)}) async-start(), calls=%async_computation.27 | async-start | bytes 4325376 | tf_op jit(solution)/shard_map/reduce_scatter | solution.py:299
  1137.3 37.8 %copy-start.1 = (bf16[2,1,128,2048]{3,2,1,0:T(8,128)(2,1)S(1)}, bf16[2,1,128,2048]{3,2,1,0:T(8,128)(2,1)}, u32[]{:S(2)}) copy-start(bf16[2,1,128,2048]{3,2,1,0:T(8,128)(2,1)} %param.16) | copy-start | bytes 3145732
  1137.3 37.8 %copy-start.15 = (f32[2048]{0:T(1024)S(1)}, f32[2048]{0:T(1024)}, u32[]{:S(2)}) copy-start(f32[2048]{0:T(1024)} %copy-done.14) | copy-start | bytes 24580
  1137.3 37.8 %copy-start.20 = (f32[2,128]{1,0:T(2,128)S(1)}, f32[2,128]{1,0:T(2,128)}, u32[]{:S(2)}) copy-start(f32[2,128]{1,0:T(2,128)} %copy-done.19) | copy-start | bytes 3076
  1137.3 580.2 %reduce-scatter.24.cloned.1.call-start = ((), (), s32[]{:S(2)}) async-start(), calls=%async_computation.28 | async-start | bytes 4325376 | tf_op jit(solution)/shard_map/reduce_scatter | solution.py:300
  1177.9 726.0 %reduce-scatter.26.cloned.1.call-start = ((), (), s32[]{:S(2)}) async-start(), calls=%async_computation.29 | async-start | bytes 17301504 | tf_op jit(solution)/shard_map/reduce_scatter | solution.py:301
  1188.6 902.8 %reduce-scatter.20.cloned.1.call-start = ((), (), s32[]{:S(2)}) async-start(), calls=%async_computation.26 | async-start | bytes 17301504 | tf_op jit(solution)/shard_map/reduce_scatter | solution.py:298
  (15 other events, 30.5 us)
Sparse Core Ops, SparseCore 0:
  11.0 59.1 all-gather.15
  73.2 55.3 all-gather.11
  131.6 76.2 all-gather.19
  209.9 29.4 all-gather.17
  241.4 29.8 all-gather.13
  274.1 76.5 all-gather.21
  352.6 51.3 all-gather.25
  406.2 82.0 all-gather.23
  490.1 51.2 all-gather.27
  543.1 52.5 all-gather.29
  597.8 82.0 all-gather.31
  736.4 166.7 reduce-scatter.13
  1074.5 48.3 reduce-scatter.15
  1125.1 48.1 reduce-scatter.17
  1176.1 50.8 reduce-scatter.27
  1230.1 52.6 reduce-scatter.29
  1285.6 52.6 reduce-scatter.31
  1340.5 90.6 reduce-scatter.11
  1434.2 140.6 reduce-scatter.21
  1577.6 139.8 reduce-scatter.23
  1720.5 183.4 reduce-scatter.25
  1906.9 184.3 reduce-scatter.19
where the time goes:
time: 2110 us; the launch traced here: 2100 us
  waiting for transfers between devices  1500 us (71%)
  matrix products  382 us (18%)
  blocking collectives  83.4 us (4%)
  other arithmetic  66.5 us (3%)
  local copies, waits for them, and re-layouts  52 us (2%)
    reduce_scatter x1, waiting for transfers between devices, body(): lax.psum_scatter(grad_query, ('seq', 'ctx'), scatter_dimension=0, tiled=T...  187 us
    reduce_scatter x1, waiting for transfers between devices, body(): lax.psum_scatter(grad_out, ('seq', 'ctx'), scatter_dimension=0, tiled=True)  186 us
    reduce_scatter x1, waiting for transfers between devices, body(): lax.psum_scatter(partial_back, 'ctx', scatter_dimension=1, tiled=True)  167 us
    reduce_scatter x1, waiting for transfers between devices, body(): lax.psum_scatter(grad_value, ('seq', 'ctx'), scatter_dimension=0, tiled=T...  143 us
    reduce_scatter x1, waiting for transfers between devices, body(): lax.psum_scatter(grad_key, ('seq', 'ctx'), scatter_dimension=0, tiled=True)  138 us
    all_gather x1, waiting for transfers between devices, body(): lax.all_gather(d_branch, 'ctx', axis=1, tiled=True)  84.3 us
    all_gather x1, waiting for transfers between devices, body(): lax.all_gather(mlp_in, 'ctx', axis=1, tiled=True)  84.3 us
    unnamed x2, blocking collectives  83.4 us
  transfers between devices with their start and end apart: 22, of which 20 were waited for; matrix products, arithmetic and copies ran while one was open for 13% of the time, Pallas kernels for 0%

commit v1 on v0

v1 whole, which is shorter than its diff:
```python
import functools
import math

import jax
import jax.numpy as jnp
from jax import lax
from jax.experimental import pallas as pl
from jax.experimental.pallas import tpu as pltpu
from jax.sharding import PartitionSpec as P

HEAD_DIM = 64
LANES = 128
EPSILON = 1e-05
ROPE_BASE = 500000.0
MASKED = -1e30
VMEM_LIMIT = 56 * 1024 * 1024
F32 = jnp.float32
BF16 = jnp.bfloat16


def folded_order(count):
    return list(range(0, count, 2)) + list(range(1, count, 2))[::-1]


def swap_core(array):
    ctx = lax.axis_size("ctx")
    return lax.ppermute(array, "ctx", [(i, i ^ 1) for i in range(ctx)])


def swap_seq(array, bit):
    seq = lax.axis_size("seq")
    return lax.ppermute(array, "seq", [(i, i ^ bit) for i in range(seq)])


def ring_step(array):
    chips = lax.axis_size("ctx") // 2
    order = folded_order(chips)
    pairs = [
        (order[i] * 2 + core, order[(i + 1) % chips] * 2 + core)
        for i in range(chips)
        for core in range(2)
    ]
    return lax.ppermute(array, "ctx", pairs)


def ring_gather(array):
    slots = [array]
    for _ in range(lax.axis_size("ctx") // 2 - 1):
        slots.append(ring_step(slots[-1]))
    return slots


def ring_scatter(parts):
    chips = len(parts)
    total = parts[1 % chips].astype(F32)
    for k in range(2, chips + 1):
        total = ring_step(total.astype(BF16)).astype(F32) + parts[k % chips].astype(F32)
    return total


def cube_gather(array):
    seq = lax.axis_size("seq")
    if seq == 4:
        half = array.shape[0] // 2
        first, second = swap_seq(array, 1), swap_seq(array, 2)
        return [
            [array],
            [first],
            [second],
            [swap_seq(first[:half], 2), swap_seq(second[half:], 1)],
        ]
    pieces = {0: array}
    bit = 1
    while bit < seq:
        pieces.update({r ^ bit: swap_seq(piece, bit) for r, piece in pieces.items()})
        bit *= 2
    return [[pieces[r]] for r in range(seq)]


def cube_scatter(chunks):
    seq = lax.axis_size("seq")
    if seq == 4:
        half = chunks[3].shape[0] // 2
        to_second = swap_seq(chunks[3][:half].astype(BF16), 1).astype(F32)
        to_first = swap_seq(chunks[3][half:].astype(BF16), 2).astype(F32)
        first = jnp.concatenate([chunks[1][:half], chunks[1][half:] + to_first])
        second = jnp.concatenate([chunks[2][:half] + to_second, chunks[2][half:]])
        return (
            chunks[0]
            + swap_seq(first.astype(BF16), 1).astype(F32)
            + swap_seq(second.astype(BF16), 2).astype(F32)
        )
    held = dict(enumerate(chunks))
    bit = seq // 2
    while bit >= 1:
        held = {
            r: held[r] + swap_seq(held[r | bit].astype(BF16), bit).astype(F32)
            for r in held
            if not r & bit
        }
        bit //= 2
    return held[0]


def scaled_frequency():
    half_dim = HEAD_DIM // 2
    base_freq = ROPE_BASE ** (-jnp.arange(half_dim, dtype=F32) * 2.0 / HEAD_DIM)
    wave = 2.0 * math.pi / base_freq
    smooth = (8192.0 / wave - 1.0) / 3.0
    middle = (1.0 - smooth) * base_freq / 32.0 + smooth * base_freq
    return jnp.where(wave < 2048.0, base_freq, jnp.where(wave > 8192.0, base_freq / 32.0, middle))


def rope_tables(positions):
    angles = positions.astype(F32)[:, None] * scaled_frequency()[None, :]
    cosine, sine = jnp.cos(angles), jnp.sin(angles)
    return (
        jnp.concatenate([cosine] * 4, axis=1),
        jnp.concatenate([-sine, sine, -sine, sine], axis=1),
    )


def rotate_lanes(values, cosine, sine):
    lane = lax.broadcasted_iota(jnp.int32, values.shape, 1)
    partner = jnp.where(
        (lane % HEAD_DIM) < HEAD_DIM // 2,
        pltpu.roll(values, LANES - HEAD_DIM // 2, 1),
        pltpu.roll(values, HEAD_DIM // 2, 1),
    )
    return values * cosine + partner * sine


def qkv_kernel(query_blocks, rope_blocks, x_ref, w_ref, cos_ref, sin_ref, out_ref):
    block = pl.program_id(0)
    raw = jnp.dot(x_ref[...], w_ref[...], preferred_element_type=F32)
    scale = jnp.where(block < query_blocks, 1.0 / math.sqrt(HEAD_DIM), 1.0)
    for at in range(raw.shape[1] // LANES):
        part = raw[:, at * LANES : (at + 1) * LANES]
        turned = rotate_lanes(part, cos_ref[...], sin_ref[...]) * scale
        out_ref[:, at * LANES : (at + 1) * LANES] = jnp.where(
            block < rope_blocks, turned, part
        ).astype(BF16)


def project_qkv(x, weights, cosine, sine, query_width, kv_width):
    rows, depth = x.shape
    width = query_width + 2 * kv_width
    block = 256
    return pl.pallas_call(
        functools.partial(qkv_kernel, query_width // block, (query_width + kv_width) // block),
        grid=(width // block,),
        in_specs=[
            pl.BlockSpec((rows, depth), lambda j: (0, 0)),
            pl.BlockSpec((depth, block), lambda j: (0, j)),
            pl.BlockSpec((rows, LANES), lambda j: (0, 0)),
            pl.BlockSpec((rows, LANES), lambda j: (0, 0)),
        ],
        out_specs=pl.BlockSpec((rows, block), lambda j: (0, j)),
        out_shape=jax.ShapeDtypeStruct((rows, width), BF16),
        compiler_params=pltpu.CompilerParams(vmem_limit_bytes=VMEM_LIMIT),
        cost_estimate=pl.CostEstimate(
            flops=2 * rows * depth * width,
            bytes_accessed=2 * (rows * depth + depth * width + rows * width),
            transcendentals=0,
        ),
    )(x, weights, cosine, sine)


def transposed(values):
    return values.astype(F32).T.astype(BF16)


def attend_kernel(limit_ref, kpos_ref, qpos_ref, q_ref, k_ref, v_ref, out_ref, lse_ref, bias):
    @pl.when(pl.program_id(0) == 0)
    def _():
        allowed = (kpos_ref[...] <= qpos_ref[...]) & (kpos_ref[...] < limit_ref[0])
        bias[...] = jnp.where(allowed, 0.0, MASKED)

    heads = q_ref.shape[1] // HEAD_DIM
    q_t = transposed(q_ref[...])
    v_t = transposed(v_ref[...])
    outs = []
    for h in range(heads):
        a = h * 2 // heads
        k_h = k_ref[:, a * HEAD_DIM : (a + 1) * HEAD_DIM]
        scores = (
            jnp.dot(k_h, q_t[h * HEAD_DIM : (h + 1) * HEAD_DIM], preferred_element_type=F32)
            + bias[...]
        )
        top = jnp.max(scores, axis=0, keepdims=True)
        shifted = jnp.exp(scores - top)
        total = jnp.sum(shifted, axis=0, keepdims=True)
        out_t = jnp.dot(
            v_t[a * HEAD_DIM : (a + 1) * HEAD_DIM],
            shifted.astype(BF16),
            preferred_element_type=F32,
        )
        outs.append(out_t / total)
        lse_ref[h : h + 1, :] = top + jnp.log(total)
    out_ref[...] = jnp.concatenate(outs, axis=0).T.astype(BF16)


def attend(qkv, part, kv, limit, kpos, qpos, query_width, kv_width):
    rows, keys = qpos.shape[1], kv.shape[0]
    pairs = kv_width // LANES
    width = query_width // pairs
    heads = width // HEAD_DIM
    grid_spec = pltpu.PrefetchScalarGridSpec(
        num_scalar_prefetch=1,
        grid=(pairs,),
        in_specs=[
            pl.BlockSpec((keys, 1), lambda i, n: (0, 0)),
            pl.BlockSpec((1, rows), lambda i, n: (0, 0)),
            pl.BlockSpec((rows, width), lambda i, n: (part, i)),
            pl.BlockSpec((keys, LANES), lambda i, n: (0, i)),
            pl.BlockSpec((keys, LANES), lambda i, n: (0, pairs + i)),
        ],
        out_specs=[
            pl.BlockSpec((rows, width), lambda i, n: (0, i)),
            pl.BlockSpec((heads, rows), lambda i, n: (i, 0)),
        ],
        scratch_shapes=[pltpu.VMEM((keys, rows), F32)],
    )
    return pl.pallas_call(
        attend_kernel,
        grid_spec=grid_spec,
        out_shape=[
            jax.ShapeDtypeStruct((rows, query_width), BF16),
            jax.ShapeDtypeStruct((query_width // HEAD_DIM, rows), F32),
        ],
        compiler_params=pltpu.CompilerParams(vmem_limit_bytes=VMEM_LIMIT),
        cost_estimate=pl.CostEstimate(
            flops=16 * rows * keys * query_width,
            bytes_accessed=4 * rows * query_width + 4 * keys * kv_width,
            transcendentals=rows * keys * query_width // HEAD_DIM,
        ),
    )(limit, kpos, qpos, qkv, kv, kv)


def attend_back_kernel(
    limit_ref, kpos_ref, qpos_ref, q_ref, k_ref, v_ref, do_ref, lse_ref, cos_ref, sin_ref,
    dq_ref, dk_ref, dv_ref, bias,
):
    @pl.when(pl.program_id(0) == 0)
    def _():
        allowed = (kpos_ref[...] <= qpos_ref[...]) & (kpos_ref[...] < limit_ref[0])
        bias[...] = jnp.where(allowed, 0.0, MASKED)

    heads = q_ref.shape[1] // HEAD_DIM
    per_kv = heads // 2
    q_t = transposed(q_ref[...])
    do_t = transposed(do_ref[...])
    k_t = transposed(k_ref[...])
    lane = lax.broadcasted_iota(jnp.int32, (k_ref.shape[0], LANES), 1)
    d_queries = []
    d_keys, d_values = [], []
    for a in range(2):
        k_h = k_ref[:, a * HEAD_DIM : (a + 1) * HEAD_DIM]
        v_h = v_ref[:, a * HEAD_DIM : (a + 1) * HEAD_DIM]
        dk_sum, dv_sum = [None, None], [None, None]
        for g in range(per_kv):
            h = a * per_kv + g
            rows = slice(h * HEAD_DIM, (h + 1) * HEAD_DIM)
            pair = slice((h // 2) * LANES, (h // 2 + 1) * LANES)
            scores = jnp.dot(k_h, q_t[rows], preferred_element_type=F32) + bias[...]
            probs = jnp.exp(scores - lse_ref[h : h + 1, :])
            d_probs = jnp.dot(v_h, do_t[rows], preferred_element_type=F32)
            mean = jnp.sum(d_probs * probs, axis=0, keepdims=True)
            d_scores = (probs * (d_probs - mean)).astype(BF16)
            probs_low = probs.astype(BF16)
            d_queries.append(
                jnp.dot(
                    k_t[a * HEAD_DIM : (a + 1) * HEAD_DIM], d_scores, preferred_element_type=F32
                )
            )
            dk_term = jnp.dot(d_scores, q_ref[:, pair], preferred_element_type=F32)
            dv_term = jnp.dot(probs_low, do_ref[:, pair], preferred_element_type=F32)
            e = h % 2
            dk_sum[e] = dk_term if dk_sum[e] is None else dk_sum[e] + dk_term
            dv_sum[e] = dv_term if dv_sum[e] is None else dv_sum[e] + dv_term
        for sums, kept in ((dk_sum, d_keys), (dv_sum, d_values)):
            mixed = jnp.where(lane < HEAD_DIM, sums[0], sums[1])
            kept.append(mixed + pltpu.roll(mixed, HEAD_DIM, 1))
    dk_ref[...] = jnp.where(lane < HEAD_DIM, d_keys[0], d_keys[1])
    dv_ref[...] = jnp.where(lane < HEAD_DIM, d_values[0], d_values[1])
    d_query = jnp.concatenate(d_queries, axis=0).T
    for at in range(d_query.shape[1] // LANES):
        cut = slice(at * LANES, (at + 1) * LANES)
        dq_ref[:, cut] = (
            rotate_lanes(d_query[:, cut], cos_ref[...], -sin_ref[...]) / math.sqrt(HEAD_DIM)
        ).astype(BF16)


def attend_back(qkv, part, kv, d_out, lse, limit, kpos, qpos, cosine, sine, query_width, kv_width):
    rows, keys = qpos.shape[1], kv.shape[0]
    pairs = kv_width // LANES
    width = query_width // pairs
    heads = width // HEAD_DIM
    grid_spec = pltpu.PrefetchScalarGridSpec(
        num_scalar_prefetch=1,
        grid=(pairs,),
        in_specs=[
            pl.BlockSpec((keys, 1), lambda i, n: (0, 0)),
            pl.BlockSpec((1, rows), lambda i, n: (0, 0)),
            pl.BlockSpec((rows, width), lambda i, n: (part, i)),
            pl.BlockSpec((keys, LANES), lambda i, n: (0, i)),
            pl.BlockSpec((keys, LANES), lambda i, n: (0, pairs + i)),
            pl.BlockSpec((rows, width), lambda i, n: (0, i)),
            pl.BlockSpec((heads, rows), lambda i, n: (i, 0)),
            pl.BlockSpec((rows, LANES), lambda i, n: (0, 0)),
            pl.BlockSpec((rows, LANES), lambda i, n: (0, 0)),
        ],
        out_specs=[
            pl.BlockSpec((rows, width), lambda i, n: (0, i)),
            pl.BlockSpec((keys, LANES), lambda i, n: (0, i)),
            pl.BlockSpec((keys, LANES), lambda i, n: (0, i)),
        ],
        scratch_shapes=[pltpu.VMEM((keys, rows), F32)],
    )
    return pl.pallas_call(
        attend_back_kernel,
        grid_spec=grid_spec,
        out_shape=[
            jax.ShapeDtypeStruct((rows, query_width), BF16),
            jax.ShapeDtypeStruct((keys, kv_width), F32),
            jax.ShapeDtypeStruct((keys, kv_width), F32),
        ],
        compiler_params=pltpu.CompilerParams(vmem_limit_bytes=VMEM_LIMIT),
        cost_estimate=pl.CostEstimate(
            flops=40 * rows * keys * query_width,
            bytes_accessed=6 * rows * query_width + 12 * keys * kv_width,
            transcendentals=rows * keys * query_width // HEAD_DIM,
        ),
    )(limit, kpos, qpos, qkv, kv, kv, d_out, lse, cosine, sine)


def unrotate_kernel(x_ref, cos_ref, sin_ref, out_ref):
    for at in range(x_ref.shape[1] // LANES):
        cut = slice(at * LANES, (at + 1) * LANES)
        out_ref[:, cut] = rotate_lanes(x_ref[:, cut], cos_ref[...], -sin_ref[...]).astype(BF16)


def unrotate(x, cosine, sine):
    return pl.pallas_call(
        unrotate_kernel,
        out_shape=jax.ShapeDtypeStruct(x.shape, BF16),
    )(x, cosine, sine)


def rms_inverse(values):
    return lax.rsqrt(jnp.mean(values * values, axis=-1, keepdims=True) + EPSILON)


def rms_back(grad_in, plain, inverse, gain):
    scaled = grad_in * gain
    back = inverse * (scaled - plain * jnp.mean(scaled * plain, axis=-1, keepdims=True))
    return (back, jnp.sum(grad_in * plain, axis=0))


def body(
    tokens,
    lengths,
    cotangent,
    attn_gain,
    w_query,
    w_key,
    w_value,
    w_out,
    mlp_gain,
    w_gate,
    w_up,
    w_down,
):
    batches, _, slot_count, model_width = tokens.shape
    seq_size, ctx_size = lax.axis_size("seq"), lax.axis_size("ctx")
    chips = ctx_size // 2
    seq_at, ctx_at = lax.axis_index("seq"), lax.axis_index("ctx")
    chip_at, core = ctx_at // 2, ctx_at % 2
    order = folded_order(chips)
    shard = w_query.shape[0]
    query_half, kv_half = w_query.shape[1] // 2, w_key.shape[1] // 2
    out_half = model_width // 2
    chip_rows = 2 * slot_count
    attn_width = query_half + 2 * kv_half
    hidden_width = w_gate.shape[1]

    def chip_back(k):
        index = jnp.int32(0)
        for place, chip in enumerate(order):
            index = jnp.where(chip_at == chip, order[(place - k) % chips], index)
        return index

    slot_chip = [chip_back(k) for k in range(chips)]

    def half(array, which, axis):
        size = array.shape[axis] // 2
        return lax.dynamic_slice_in_dim(array, which * size, size, axis)

    def mine(array, axis):
        return half(array, core, axis)

    def others(array, axis):
        return half(array, 1 - core, axis)

    def by_core(own, other, axis):
        return jnp.where(
            core == 0,
            jnp.concatenate([own, other], axis),
            jnp.concatenate([other, own], axis),
        )

    def turn_blocks(array):
        block = array.shape[-1] // seq_size
        bit = 1
        while bit < seq_size:
            turned = jnp.concatenate(
                [
                    array[..., (r ^ bit) * block : ((r ^ bit) + 1) * block]
                    for r in range(seq_size)
                ],
                axis=-1,
            )
            array = jnp.where((seq_at & bit) != 0, turned, array)
            bit *= 2
        return array

    def block_row(r, k):
        return ((seq_at ^ r) * chips + slot_chip[k]) * (2 * shard)

    def plane_gather(piece, rotation):
        total = 2 * shard * seq_size * chips
        out = jnp.zeros((total, piece.shape[1]), BF16)
        for k, slot in enumerate(ring_gather(piece)):
            for r, blocks in enumerate(cube_gather(slot)):
                at = (block_row(r, k) + rotation) % total
                for block in blocks:
                    out = lax.dynamic_update_slice(out, block, (at, 0))
                    at = at + block.shape[0]
        return out

    def plane_scatter(partial, rotation):
        total = partial.shape[0]
        summed = []
        for k in range(chips):
            chunks = [
                lax.dynamic_slice_in_dim(
                    partial, (block_row(r, k % chips) + rotation) % total, 2 * shard, 0
                )
                for r in range(seq_size)
            ]
            summed.append(cube_scatter(chunks))
        return ring_scatter(summed)

    gains = jnp.concatenate(
        [attn_gain[:, None], mlp_gain[:, None], jnp.zeros((shard, LANES - 2), BF16)], axis=1
    )
    piece_a = by_core(
        jnp.concatenate([mine(w_query, 1), mine(w_key, 1), mine(w_value, 1), gains], 1),
        swap_core(
            jnp.concatenate([others(w_query, 1), others(w_key, 1), others(w_value, 1), gains], 1)
        ),
        0,
    )
    piece_o = by_core(mine(w_out, 1), swap_core(others(w_out, 1)), 0)
    x_own = tokens[:, 0]
    x_chip = by_core(x_own, swap_core(x_own), 1)
    attn_w = plane_gather(piece_a, 0)
    out_rotation = core * query_half
    out_w = plane_gather(piece_o, out_rotation)
    gate_w = jnp.concatenate([b for blocks in cube_gather(w_gate) for b in blocks], 0)
    up_w = jnp.concatenate([b for blocks in cube_gather(w_up) for b in blocks], 0)
    down_w = jnp.concatenate(
        [jnp.concatenate(blocks, 0) for blocks in cube_gather(w_down)], axis=1
    )

    first_row = chip_at * chip_rows
    q_positions = first_row + jnp.arange(chip_rows)
    cosine, sine = rope_tables(q_positions)
    cosine_all, sine_all = jnp.tile(cosine, (batches, 1)), jnp.tile(sine, (batches, 1))
    qpos = q_positions[None, :]
    kpos = jnp.concatenate([slot_chip[k] * chip_rows + jnp.arange(chip_rows) for k in range(chips)])
    kpos = kpos[:, None]
    own_pos = ctx_at * slot_count + jnp.arange(slot_count)
    gain_table = attn_w[:, attn_width : attn_width + 2].astype(F32).T
    gain_a, gain_m = gain_table[0], gain_table[1]

    x_rows = x_chip.reshape(batches * chip_rows, model_width).astype(F32)
    inverse_rows = rms_inverse(x_rows)
    normed_a = (x_rows * inverse_rows * gain_a).astype(BF16)
    qkv = project_qkv(normed_a, attn_w, cosine_all, sine_all, query_half, kv_half)
    kv_all, outs, lses, attended = [], [], [], []
    for b in range(batches):
        kv = qkv[b * chip_rows : (b + 1) * chip_rows, query_half:]
        kv_all.append(jnp.concatenate(ring_gather(kv), 0))
    for b in range(batches):
        out, lse = attend(qkv, b, kv_all[b], lengths[b], kpos, qpos, query_half, kv_half)
        outs.append(out)
        lses.append(lse)
        attended.append(jnp.concatenate([out, swap_core(out)], axis=1))

    residual, plain_m, inverse_m, group_in, group_d, d_own = [], [], [], [], [], []

    def group_rows(own):
        slots = ring_gather(own)
        return jnp.concatenate(slots + [swap_core(slot) for slot in slots], 0)

    for b in range(batches):
        valid = (own_pos < lengths[b, 0]).astype(F32)[:, None]
        d_output = cotangent[b, 0].astype(F32) * valid
        d_own.append(d_output)
        group_d.append(group_rows(turn_blocks(d_output.astype(BF16))))
    for b in range(batches):
        branch = jnp.dot(attended[b], out_w, preferred_element_type=F32)
        branch = by_core(mine(branch, 0), swap_core(others(branch, 0)), 1)
        res = x_own[b].astype(F32) + branch
        inverse = rms_inverse(res)
        plain = res * inverse
        residual.append(res)
        inverse_m.append(inverse)
        plain_m.append(plain)
        group_in.append(group_rows(turn_blocks((plain * gain_m).astype(BF16))))

    def back_to_owner(partial):
        rows = chips * slot_count
        received = swap_core(partial[rows:].astype(BF16)).astype(F32)
        own = partial[:rows] + received
        return turn_blocks(
            ring_scatter([own[k * slot_count : (k + 1) * slot_count] for k in range(chips)])
        )

    activations, hiddens, d_gates, d_ups, d_normed = [], [], [], [], []
    for b in range(batches):
        gate_val = jnp.dot(group_in[b], gate_w, preferred_element_type=F32)
        up_val = jnp.dot(group_in[b], up_w, preferred_element_type=F32)
        d_hidden = jnp.einsum("rd,fd->rf", group_d[b], down_w, preferred_element_type=F32)
        sigmoid_g = 1.0 / (1.0 + jnp.exp(-gate_val))
        activated = gate_val * sigmoid_g
        slope = sigmoid_g * (1.0 + gate_val * (1.0 - sigmoid_g))
        d_gate = (d_hidden * up_val * slope).astype(BF16)
        d_up = (d_hidden * activated).astype(BF16)
        hidden = (activated * up_val).astype(BF16)
        hiddens.append(hidden)
        d_gates.append(d_gate)
        d_ups.append(d_up)
        partial_back = jnp.einsum(
            "rf,df->rd", d_gate, gate_w, preferred_element_type=F32
        ) + jnp.einsum("rf,df->rd", d_up, up_w, preferred_element_type=F32)
        d_normed.append(back_to_owner(partial_back))
    for b in range(batches):
        partial_out = jnp.dot(hiddens[b], down_w, preferred_element_type=F32)
        activations.append((residual[b] + back_to_owner(partial_out)).astype(BF16))

    d_resid, gain_m_parts, d_half, d_queries, d_kvs = [], [], [], [], []
    for b in range(batches):
        back_m, gain_part = rms_back(d_normed[b], plain_m[b], inverse_m[b], gain_m)
        gain_m_parts.append(gain_part)
        d_res = d_own[b] + back_m
        d_resid.append(d_res)
        d_low = d_res.astype(BF16)
        d_half.append(by_core(mine(d_low, 1), swap_core(others(d_low, 1)), 0))
        d_att = jnp.einsum("rd,hd->rh", d_half[b], out_w, preferred_element_type=F32)
        d_att = (d_att[:, :query_half] + swap_core(d_att[:, query_half:])).astype(BF16)
        d_query, d_key, d_value = attend_back(
            qkv, b, kv_all[b], d_att, lses[b], lengths[b], kpos, qpos, cosine, sine,
            query_half, kv_half,
        )
        d_queries.append(d_query)
        slots = [
            jnp.concatenate([d[k * chip_rows : (k + 1) * chip_rows] for d in (d_key, d_value)], 1)
            for k in range(chips)
        ]
        d_kvs.append(ring_scatter(slots))

    group_in_all = jnp.concatenate(group_in, 0)
    group_d_all = jnp.concatenate(group_d, 0)
    grad_gate = jnp.einsum(
        "rd,rf->df", group_in_all, jnp.concatenate(d_gates, 0), preferred_element_type=F32
    )
    grad_up = jnp.einsum(
        "rd,rf->df", group_in_all, jnp.concatenate(d_ups, 0), preferred_element_type=F32
    )
    grad_down = jnp.einsum(
        "rf,rd->fd", jnp.concatenate(hiddens, 0), group_d_all, preferred_element_type=F32
    )
    depth = w_gate.shape[0]
    grad_gate = cube_scatter([grad_gate[r * depth : (r + 1) * depth] for r in range(seq_size)])
    grad_up = cube_scatter([grad_up[r * depth : (r + 1) * depth] for r in range(seq_size)])
    depth = w_down.shape[1]
    grad_down = cube_scatter(
        [grad_down[:, r * depth : (r + 1) * depth] for r in range(seq_size)]
    )
    grad_out = jnp.einsum(
        "rh,rd->hd",
        jnp.concatenate(attended, 0),
        jnp.concatenate(d_half, 0),
        preferred_element_type=F32,
    )
    grad_out = plane_scatter(grad_out, out_rotation)

    d_qkv = []
    for b in range(batches):
        d_key = unrotate(d_kvs[b][:, :kv_half], cosine, sine)
        d_value = d_kvs[b][:, kv_half:].astype(BF16)
        d_qkv.append(jnp.concatenate([d_queries[b], d_key, d_value], 1))
    d_qkv = jnp.concatenate(d_qkv, 0)
    grad_attn = jnp.einsum("rd,rh->dh", normed_a, d_qkv, preferred_element_type=F32)
    d_normed_a = jnp.einsum(
        "rh,dh->rd", d_qkv, attn_w[:, :attn_width], preferred_element_type=F32
    ).reshape(batches, chip_rows, model_width)
    d_normed_a = mine(d_normed_a, 1) + swap_core(others(d_normed_a, 1))
    x_own_f = x_own.astype(F32)
    inverse_a = rms_inverse(x_own_f)
    plain_a = x_own_f * inverse_a
    gain_a_part, input_grad = 0.0, []
    for b in range(batches):
        back_a, gain_part = rms_back(d_normed_a[b], plain_a[b], inverse_a[b], gain_a)
        gain_a_part = gain_a_part + gain_part
        input_grad.append(d_resid[b] + back_a)
    gain_parts = jnp.stack([gain_a_part, sum(gain_m_parts)], 1)
    gain_parts = jnp.pad(gain_parts, ((0, 0), (0, LANES - 2)))
    grad_attn = plane_scatter(jnp.concatenate([grad_attn, gain_parts], 1), 0)

    received = swap_core(others(jnp.concatenate([grad_attn, grad_out], 1), 0))
    grad_attn, grad_out = mine(grad_attn, 0), mine(grad_out, 0)
    edges = [0, query_half, query_half + kv_half, attn_width]
    grad_query, grad_key, grad_value = (
        by_core(grad_attn[:, lo:hi], received[:, lo:hi], 1)
        for lo, hi in zip(edges[:-1], edges[1:])
    )
    grad_gains = grad_attn[:, attn_width:] + received[:, attn_width : attn_width + LANES]
    grad_out = by_core(grad_out, received[:, attn_width + LANES :], 1)
    return (
        jnp.stack(activations)[:, None],
        jnp.stack(input_grad)[:, None],
        grad_gains[:, 0],
        grad_query,
        grad_key,
        grad_value,
        grad_out,
        grad_gains[:, 1],
        grad_gate,
        grad_up,
        grad_down,
    )


def solution(mesh):
    rows = P(None, "seq", "ctx", None)
    spread = P(("seq", "ctx"))
    spread_rows = P(("seq", "ctx"), None)
    return jax.shard_map(
        body,
        mesh=mesh,
        in_specs=(
            rows,
            P(None, "seq"),
            rows,
            spread,
            spread_rows,
            spread_rows,
            spread_rows,
            spread_rows,
            spread,
            P("seq", "ctx"),
            P("seq", "ctx"),
            P("ctx", "seq"),
        ),
        out_specs=(
            rows,
            rows,
            spread,
            spread_rows,
            spread_rows,
            spread_rows,
            spread_rows,
            spread,
            P("seq", "ctx"),
            P("seq", "ctx"),
            P("ctx", "seq"),
        ),
        check_vma=False,
    )
```

time: 2110 us -> 1080 us (0.51)
  waiting for transfers between devices: 1500 us -> 410 us
  matrix products: 382 us -> 162 us
  starting transfers between devices: 1.27 us -> 199 us
  blocking collectives: 83.4 us -> 0 us
  Pallas kernels: 0 us -> 79.8 us
  local copies, waits for them, and re-layouts: 52 us -> 131 us
    reduce_scatter x11 -> x0, waiting for transfers between devices: 1020 us -> none  [the longest x1 187 us: body(): lax.psum_scatter(grad_query, ('seq', 'ctx'), scatter_dimension=0, tiled=T...]
    all_gather x11 -> x0, waiting for transfers between devices: 470 us -> none  [the longest x1 84.3 us: body(): lax.all_gather(d_branch, 'ctx', axis=1, tiled=True)]
    ppermute x0 -> x169, waiting for transfers between devices: none -> 410 us  [the longest x48 205 us: ring_step(): return lax.ppermute(array, 'ctx', pairs)]
    dot_general x133 -> x22, matrix products: 382 us -> 162 us  [the longest x2 20.2 us: body(): jnp.einsum('rd,fd->rf', group_d[b], down_w, preferred_element_type=F32)]
    ppermute x0 -> x169, starting transfers between devices: none -> 199 us  [the longest x88 97 us: swap_seq(): return lax.ppermute(array, 'seq', [(i, i ^ bit) for i in range(seq)])]
    unnamed x2 -> x0, blocking collectives: 83.4 us -> none
    pallas_call x0 -> x7, Pallas kernels: none -> 79.8 us  [the longest x2 37.7 us: attend_back(): pl.pallas_call(attend_back_kernel, grid_spec=grid_spec, out_shape=[jax.Sh...]
    unnamed x56 -> x208, local copies, waits for them, and re-layouts: 6.22 us -> 54.6 us
  transfers between devices with their start and end apart: 22 -> 169, of which waited for: 20 -> 78; matrix products, arithmetic and copies ran while one was open for 13% -> 27% of each run, Pallas kernels for 0% -> 7%
where the time goes in v1:
time: 1080 us; the launch traced here: 1070 us
  waiting for transfers between devices  410 us (38%)
  starting transfers between devices  199 us (18%)
  matrix products  162 us (15%)
  local copies, waits for them, and re-layouts  131 us (12%)
  other arithmetic  86.6 us (8%)
  Pallas kernels  79.8 us (7%)
    ppermute x48, waiting for transfers between devices, ring_step(): return lax.ppermute(array, 'ctx', pairs)  205 us
    ppermute x88, waiting for transfers between devices, swap_seq(): return lax.ppermute(array, 'seq', [(i, i ^ bit) for i in range(seq)])  204 us
    ppermute x88, starting transfers between devices, swap_seq(): return lax.ppermute(array, 'seq', [(i, i ^ bit) for i in range(seq)])  97 us
    ppermute x48, starting transfers between devices, ring_step(): return lax.ppermute(array, 'ctx', pairs)  95.6 us
    unnamed x208, local copies, waits for them, and re-layouts  54.6 us
    pallas_call x2, Pallas kernels, attend_back(): pl.pallas_call(attend_back_kernel, grid_spec=grid_spec, out_shape=[jax.Sh...  37.7 us
    pallas_call x2, Pallas kernels, attend(): pl.pallas_call(attend_kernel, grid_spec=grid_spec, out_shape=[jax.ShapeDt...  29 us
  transfers between devices with their start and end apart: 169, of which 78 were waited for; matrix products, arithmetic and copies ran while one was open for 27% of the time, Pallas kernels for 7%

profile of v1, /device:TPU:0, one launch (start us, length us, event | category | flops | bytes accessed | tf_op | source)
XLA Modules:
  0.0 1071.5 jit_solution(9156338439170051543)
XLA Ops:
  107.3 38.8 %collective-permute-done.38 = bf16[64,1024]{1,0:T(8,128)(2,1)S(1)} collective-permute-done((bf16[64,1024]{1,0:T(8,128)(2,1)S(1)}, bf16[64,1024]{1,0:T(8,128)(2,1)S(1)}, u32[]{:S(2)}, u32[]{:S(2)}) %collective-permute-start.38) | collective-permute-done | bytes 131104 | tf_op jit(solution)/shard_map/ppermute | solution.py:32
  153.2 19.2 %collective-permute-done.39 = bf16[64,1024]{1,0:T(8,128)(2,1)S(1)} collective-permute-done((bf16[64,1024]{1,0:T(8,128)(2,1)S(1)}, bf16[64,1024]{1,0:T(8,128)(2,1)S(1)}, u32[]{:S(2)}, u32[]{:S(2)}) %collective-permute-start.39) | collective-permute-done | bytes 131104 | tf_op jit(solution)/shard_map/ppermute | solution.py:32
  202.1 7.9 collective-permute-done.9
  258.8 9.3 shard_map.203.q_ref
  304.1 14.3 %shard_map.204 = (bf16[256,1024]{1,0:T(8,128)(2,1)}, f32[16,256]{1,0:T(8,128)}) custom-call(s32[1]{0:T(128)} %bitcast.1.limit_ref, s32[1024,1]{1,0:T(8,128)} %copy.120.kpos_ref, s32[1,256]{1,0:T(1,128)} %iota_add_fusion.qpos_ref, bf16[512,1536]{1,0:T(8,128)(2,1)} %shard_map.203.q_ref, bf16[1024,512]{1,0:T(8,128)(2,1)} %pad_maximum_fusion.k_ref.v_ref, ...), custom_call_target="tpu_custom_call" | custom-call | flops 4294967296 | bytes 2097152 | tf_op jit(solution)/shard_map/pallas_call | solution.py:224
  322.3 14.7 %shard_map.205 = (bf16[256,1024]{1,0:T(8,128)(2,1)}, f32[16,256]{1,0:T(8,128)}) custom-call(s32[1]{0:T(128)} %bitcast.12.limit_ref, s32[1024,1]{1,0:T(8,128)} %copy.120.kpos_ref, s32[1,256]{1,0:T(1,128)} %iota_add_fusion.qpos_ref, bf16[512,1536]{1,0:T(8,128)(2,1)} %shard_map.203.q_ref, bf16[1024,512]{1,0:T(8,128)(2,1)} %pad_maximum_fusion.1.k_ref.v_ref, ...), custom_call_target="tpu_custom_call" | custom-call | flops 4294967296 | bytes 2097152 | tf_op jit(solution)/shard_map/pallas_call | solution.py:224
  358.1 10.0 collective-permute-done.46
  370.3 10.1 fusion.107
  381.5 9.1 collective-permute-done.47
  395.2 17.4 %collective-permute-done.48 = bf16[128,2048]{1,0:T(8,128)(2,1)S(1)} collective-permute-done((bf16[128,2048]{1,0:T(8,128)(2,1)S(1)}, bf16[128,2048]{1,0:T(8,128)(2,1)S(1)}, u32[]{:S(2)}, u32[]{:S(2)}) %collective-permute-start.48) | collective-permute-done | bytes 524320 | tf_op jit(solution)/shard_map/ppermute | solution.py:43
  423.3 9.8 multiply_convert_fusion.3
  463.1 9.6 collective-permute-done.103
  481.1 10.7 %collective-permute-done.93 = bf16[128,2048]{1,0:T(8,128)(2,1)S(1)} collective-permute-done((bf16[128,2048]{1,0:T(8,128)(2,1)S(1)}, bf16[128,2048]{1,0:T(8,128)(2,1)S(1)}, u32[]{:S(2)}, u32[]{:S(2)}) %collective-permute-start.93) | collective-permute-done | bytes 524320 | tf_op jit(solution)/shard_map/ppermute | solution.py:43
  495.9 11.4 %collective-permute-done.66 = bf16[128,2048]{1,0:T(8,128)(2,1)S(1)} collective-permute-done((bf16[128,2048]{1,0:T(8,128)(2,1)S(1)}, bf16[128,2048]{1,0:T(8,128)(2,1)S(1)}, u32[]{:S(2)}, u32[]{:S(2)}) %collective-permute-start.66) | collective-permute-done | bytes 524320 | tf_op jit(solution)/shard_map/ppermute | solution.py:43
  522.0 7.7 collective-permute-done.67
  533.3 7.7 collective-permute-done.95
  541.5 9.2 collective-permute-done.68
  570.2 10.1 fusion.106
  584.9 10.2 collective-permute-done.76
  604.1 9.6 multiply_convert_fusion.1
  620.5 14.1 %fusion.153 = (bf16[2048,1024]{1,0:T(8,128)(2,1)}, f32[2048,1024]{1,0:T(8,128)}) fusion(bf16[2048,2048]{1,0:T(8,128)(2,1)S(1)} %copy-done.55, bf16[1024,1024]{1,0:T(8,128)(2,1)} %copy-done.79, bf16[1024,1024]{1,0:T(8,128)(2,1)} %copy-done.77), kind=kOutput, calls=%fused_computation.536 | convolution fusion | flops 8600420352 | bytes 25165824 | tf_op jit(solution)/shard_map/rd,rf->df/dot_general | solution.py:579
  634.6 12.6 %fusion.152 = (bf16[2048,1024]{1,0:T(8,128)(2,1)}, f32[2048,1024]{1,0:T(8,128)}) fusion(bf16[2048,2048]{1,0:T(8,128)(2,1)S(1)} %copy-done.55, bf16[1024,1024]{1,0:T(8,128)(2,1)S(1)} %copy-done.78, bf16[1024,1024]{1,0:T(8,128)(2,1)S(1)} %copy-done.76), kind=kOutput, calls=%fused_computation.535 | convolution fusion | flops 8600420352 | bytes 25165824 | tf_op jit(solution)/shard_map/rd,rf->df/dot_general | solution.py:576
  671.0 16.1 %fusion.154 = (bf16[1024,2048]{1,0:T(8,128)(2,1)}, f32[1024,2048]{1,0:T(8,128)}) fusion(bf16[2048,2048]{1,0:T(8,128)(2,1)} %get-tuple-element.226, bf16[1024,1024]{1,0:T(8,128)(2,1)} %get-tuple-element.155, bf16[1024,1024]{1,0:T(8,128)(2,1)} %get-tuple-element.152), kind=kOutput, calls=%fused_computation.537 | convolution fusion | flops 8600420352 | bytes 25165824 | tf_op jit(solution)/shard_map/rf,rd->fd/dot_general | solution.py:582
  724.4 11.4 %collective-permute-done.109 = bf16[128,2048]{1,0:T(8,128)(2,1)S(1)} collective-permute-done((bf16[128,2048]{1,0:T(8,128)(2,1)S(1)}, bf16[128,2048]{1,0:T(8,128)(2,1)S(1)}, u32[]{:S(2)}, u32[]{:S(2)}) %collective-permute-start.109) | collective-permute-done | bytes 524320 | tf_op jit(solution)/shard_map/ppermute | solution.py:43
  739.1 7.9 collective-permute-done.82
  747.7 7.8 collective-permute-done.110
  762.2 8.1 collective-permute-done.83
  773.0 8.5 collective-permute-done.111
  841.8 18.7 %shard_map.208 = (bf16[256,1024]{1,0:T(8,128)(2,1)}, f32[1024,256]{1,0:T(8,128)}, f32[1024,256]{1,0:T(8,128)}) custom-call(s32[1]{0:T(128)} %bitcast.12.limit_ref, s32[1024,1]{1,0:T(8,128)} %copy.120.kpos_ref, s32[1,256]{1,0:T(1,128)} %iota_add_fusion.qpos_ref, bf16[512,1536]{1,0:T(8,128)(2,1)} %shard_map.203.q_ref, ...), custom_call_target="tpu_custom_call" | custom-call | flops 10737418240 | bytes 4718592 | tf_op jit(solution)/shard_map/pallas_call | solution.py:320
  867.0 18.9 %shard_map.206 = (bf16[256,1024]{1,0:T(8,128)(2,1)}, f32[1024,256]{1,0:T(8,128)}, f32[1024,256]{1,0:T(8,128)}) custom-call(s32[1]{0:T(128)} %bitcast.1.limit_ref, s32[1024,1]{1,0:T(8,128)} %copy.120.kpos_ref, s32[1,256]{1,0:T(1,128)} %iota_add_fusion.qpos_ref, bf16[512,1536]{1,0:T(8,128)(2,1)} %shard_map.203.q_ref, ...), custom_call_target="tpu_custom_call" | custom-call | flops 10737418240 | bytes 4718592 | tf_op jit(solution)/shard_map/pallas_call | solution.py:320
  971.3 8.9 collective-permute-done.120
  985.5 7.8 collective-permute-done.121
  (834 shorter events, 679.9 us)
Async XLA Ops:
  6.1 34.4 %collective-permute-start.1 = (bf16[64,1664]{1,0:T(8,128)(2,1)}, bf16[64,1664]{1,0:T(8,128)(2,1)}, u32[]{:S(2)}, u32[]{:S(2)}) collective-permute-start(bf16[64,1664]{1,0:T(8,128)(2,1)} %concatenate.332), channel_id=1, source_target_pairs={{0,1},{1,0},{2,3},{3,2},{4,5},{5,4},{6,7},{7,6},{8,9},{9,8},{10,11... | collective-permute-start | bytes 638984 | tf_op jit(solution)/shard_map/ppermute | solution.py:27
  14.5 46.6 %collective-permute-start.85 = (bf16[128,2048]{1,0:T(8,128)(2,1)}, bf16[128,2048]{1,0:T(8,128)(2,1)}, u32[]{:S(2)}, u32[]{:S(2)}) collective-permute-start(bf16[128,2048]{1,0:T(8,128)(2,1)} %get-tuple-element.90), channel_id=1, source_target_pairs={{0,4},{1,5},{4,6},{5,7},{6,2},{7,3},{2,0},{3,1},{8,12},{9,13},{12,... | collective-permute-start | bytes 1572872 | tf_op jit(solution)/shard_map/ppermute | solution.py:43
  18.5 128.6 %collective-permute-start.57 = (bf16[512,1024]{1,0:T(8,128)(2,1)}, bf16[512,1024]{1,0:T(8,128)(2,1)S(1)}, u32[]{:S(2)}, u32[]{:S(2)}) collective-permute-start(bf16[512,1024]{1,0:T(8,128)(2,1)} %param.22), channel_id=1, source_target_pairs={{0,8},{8,0},{16,24},{24,16},{1,9},{9,1},{17,25},{25,17},{2,10},{10... | collective-permute-start | bytes 3145736 | tf_op jit(solution)/shard_map/ppermute | solution.py:32
  57.5 45.7 %collective-permute-start = (bf16[2,128,2048]{2,1,0:T(8,128)(2,1)S(1)}, bf16[2,128,2048]{2,1,0:T(8,128)(2,1)S(1)}, u32[]{:S(2)}, u32[]{:S(2)}) collective-permute-start(bf16[2,128,2048]{2,1,0:T(8,128)(2,1)S(1)} %bitcast.136), channel_id=1, source_target_pairs={{0,1},{1,0},{2,3},{3,2},{4,5},{5,4},{6,7},{7,6},{8,9},{9,8},{10,11... | collective-permute-start | bytes 3145736 | tf_op jit(solution)/shard_map/ppermute | solution.py:27
  96.1 54.9 %collective-permute-start.58 = (bf16[512,1024]{1,0:T(8,128)(2,1)S(1)}, bf16[512,1024]{1,0:T(8,128)(2,1)S(1)}, u32[]{:S(2)}, u32[]{:S(2)}) collective-permute-start(bf16[512,1024]{1,0:T(8,128)(2,1)S(1)} %copy-done.15), channel_id=1, source_target_pairs={{0,16},{8,24},{16,0},{24,8},{1,17},{9,25},{17,1},{25,9},{2,18},{10... | collective-permute-start | bytes 3145736 | tf_op jit(solution)/shard_map/ppermute | solution.py:32
  100.0 74.2 %collective-permute-start.53 = (bf16[512,1024]{1,0:T(8,128)(2,1)S(1)}, bf16[512,1024]{1,0:T(8,128)(2,1)S(1)}, u32[]{:S(2)}, u32[]{:S(2)}) collective-permute-start(bf16[512,1024]{1,0:T(8,128)(2,1)S(1)} %copy-done.16), channel_id=1, source_target_pairs={{0,8},{8,0},{16,24},{24,16},{1,9},{9,1},{17,25},{25,17},{2,10},{10... | collective-permute-start | bytes 3145736 | tf_op jit(solution)/shard_map/ppermute | solution.py:32
  103.3 78.1 %collective-permute-start.62 = (bf16[1024,512]{1,0:T(8,128)(2,1)S(1)}, bf16[1024,512]{1,0:T(8,128)(2,1)S(1)}, u32[]{:S(2)}, u32[]{:S(2)}) collective-permute-start(bf16[1024,512]{1,0:T(8,128)(2,1)S(1)} %copy-done.64), channel_id=1, source_target_pairs={{0,16},{8,24},{16,0},{24,8},{1,17},{9,25},{17,1},{25,9},{2,18},{10... | collective-permute-start | bytes 3145736 | tf_op jit(solution)/shard_map/ppermute | solution.py:32
  106.1 40.0 %collective-permute-start.38 = (bf16[64,1024]{1,0:T(8,128)(2,1)S(1)}, bf16[64,1024]{1,0:T(8,128)(2,1)S(1)}, u32[]{:S(2)}, u32[]{:S(2)}) collective-permute-start(bf16[64,1024]{1,0:T(8,128)(2,1)S(1)} %slice.1004), channel_id=1, source_target_pairs={{0,16},{8,24},{16,0},{24,8},{1,17},{9,25},{17,1},{25,9},{2,18},{10... | collective-permute-start | bytes 393224 | tf_op jit(solution)/shard_map/ppermute | solution.py:32
  146.1 37.1 %collective-permute-start.61 = (bf16[1024,512]{1,0:T(8,128)(2,1)S(1)}, bf16[1024,512]{1,0:T(8,128)(2,1)S(1)}, u32[]{:S(2)}, u32[]{:S(2)}) collective-permute-start(bf16[1024,512]{1,0:T(8,128)(2,1)S(1)} %copy-done.64), channel_id=1, source_target_pairs={{0,8},{8,0},{16,24},{24,16},{1,9},{9,1},{17,25},{25,17},{2,10},{10... | collective-permute-start | bytes 3145736 | tf_op jit(solution)/shard_map/ppermute | solution.py:32
  147.1 36.7 %collective-permute-start.54 = (bf16[512,1024]{1,0:T(8,128)(2,1)S(1)}, bf16[512,1024]{1,0:T(8,128)(2,1)S(1)}, u32[]{:S(2)}, u32[]{:S(2)}) collective-permute-start(bf16[512,1024]{1,0:T(8,128)(2,1)S(1)} %copy-done.16), channel_id=1, source_target_pairs={{0,16},{8,24},{16,0},{24,8},{1,17},{9,25},{17,1},{25,9},{2,18},{10... | collective-permute-start | bytes 3145736 | tf_op jit(solution)/shard_map/ppermute | solution.py:32
  185.4 89.0 %collective-permute-start.59 = (bf16[256,1024]{1,0:T(8,128)(2,1)S(1)}, bf16[256,1024]{1,0:T(8,128)(2,1)}, u32[]{:S(2)}, u32[]{:S(2)}) collective-permute-start(bf16[256,1024]{1,0:T(8,128)(2,1)S(1)} %slice.1017), channel_id=1, source_target_pairs={{0,16},{8,24},{16,0},{24,8},{1,17},{9,25},{17,1},{25,9},{2,18},{10... | collective-permute-start | bytes 1572872 | tf_op jit(solution)/shard_map/ppermute | solution.py:32
  191.6 84.7 %collective-permute-start.60 = (bf16[256,1024]{1,0:T(8,128)(2,1)S(1)}, bf16[256,1024]{1,0:T(8,128)(2,1)S(1)}, u32[]{:S(2)}, u32[]{:S(2)}) collective-permute-start(bf16[256,1024]{1,0:T(8,128)(2,1)S(1)} %slice.1018), channel_id=1, source_target_pairs={{0,8},{8,0},{16,24},{24,16},{1,9},{9,1},{17,25},{25,17},{2,10},{10... | collective-permute-start | bytes 1572872 | tf_op jit(solution)/shard_map/ppermute | solution.py:32
  192.6 87.0 %collective-permute-start.87 = (bf16[128,2048]{1,0:T(8,128)(2,1)S(1)}, bf16[128,2048]{1,0:T(8,128)(2,1)S(1)}, u32[]{:S(2)}, u32[]{:S(2)}) collective-permute-start(bf16[128,2048]{1,0:T(8,128)(2,1)S(1)} %collective-permute-done.86), channel_id=1, source_target_pairs={{0,4},{1,5},{4,6},{5,7},{6,2},{7,3},{2,0},{3,1},{8,12},{9,13},{12,... | collective-permute-start | bytes 1572872 | tf_op jit(solution)/shard_map/ppermute | solution.py:43
  279.5 68.6 %collective-permute-start.89 = (bf16[128,2048]{1,0:T(8,128)(2,1)}, bf16[128,2048]{1,0:T(8,128)(2,1)S(1)}, u32[]{:S(2)}, u32[]{:S(2)}) collective-permute-start(bf16[128,2048]{1,0:T(8,128)(2,1)} %collective-permute-done.85), channel_id=1, source_target_pairs={{0,1},{1,0},{2,3},{3,2},{4,5},{5,4},{6,7},{7,6},{8,9},{9,8},{10,11... | collective-permute-start | bytes 1572872 | tf_op jit(solution)/shard_map/ppermute | solution.py:27
  282.0 88.3 %collective-permute-start.64 = (bf16[512,512]{1,0:T(8,128)(2,1)S(1)}, bf16[512,512]{1,0:T(8,128)(2,1)}, u32[]{:S(2)}, u32[]{:S(2)}) collective-permute-start(bf16[512,512]{1,0:T(8,128)(2,1)S(1)} %slice.1020), channel_id=1, source_target_pairs={{0,8},{8,0},{16,24},{24,16},{1,9},{9,1},{17,25},{25,17},{2,10},{10... | collective-permute-start | bytes 1572872 | tf_op jit(solution)/shard_map/ppermute | solution.py:32
  292.8 54.7 %collective-permute-start.56 = (bf16[256,1024]{1,0:T(8,128)(2,1)S(1)}, bf16[256,1024]{1,0:T(8,128)(2,1)S(1)}, u32[]{:S(2)}, u32[]{:S(2)}) collective-permute-start(bf16[256,1024]{1,0:T(8,128)(2,1)S(1)} %slice.1016), channel_id=1, source_target_pairs={{0,8},{8,0},{16,24},{24,16},{1,9},{9,1},{17,25},{25,17},{2,10},{10... | collective-permute-start | bytes 1572872 | tf_op jit(solution)/shard_map/ppermute | solution.py:32
  296.6 53.7 %collective-permute-start.90 = (bf16[128,2048]{1,0:T(8,128)(2,1)S(1)}, bf16[128,2048]{1,0:T(8,128)(2,1)S(1)}, u32[]{:S(2)}, u32[]{:S(2)}) collective-permute-start(bf16[128,2048]{1,0:T(8,128)(2,1)S(1)} %collective-permute-done.86), channel_id=1, source_target_pairs={{0,1},{1,0},{2,3},{3,2},{4,5},{5,4},{6,7},{7,6},{8,9},{9,8},{10,11... | collective-permute-start | bytes 1572872 | tf_op jit(solution)/shard_map/ppermute | solution.py:27
  380.4 77.9 %collective-permute-start.102 = (bf16[128,2048]{1,0:T(8,128)(2,1)S(1)}, bf16[128,2048]{1,0:T(8,128)(2,1)S(1)}, u32[]{:S(2)}, u32[]{:S(2)}) collective-permute-start(bf16[128,2048]{1,0:T(8,128)(2,1)S(1)} %collective-permute-done.101), channel_id=1, source_target_pairs={{0,4},{1,5},{4,6},{5,7},{6,2},{7,3},{2,0},{3,1},{8,12},{9,13},{12,... | collective-permute-start | bytes 1572872 | tf_op jit(solution)/shard_map/ppermute | solution.py:43
  460.7 34.3 %collective-permute-start.104 = (bf16[128,2048]{1,0:T(8,128)(2,1)S(1)}, bf16[128,2048]{1,0:T(8,128)(2,1)S(1)}, u32[]{:S(2)}, u32[]{:S(2)}) collective-permute-start(bf16[128,2048]{1,0:T(8,128)(2,1)S(1)} %get-tuple-element.88), channel_id=1, source_target_pairs={{0,1},{1,0},{2,3},{3,2},{4,5},{5,4},{6,7},{7,6},{8,9},{9,8},{10,11... | collective-permute-start | bytes 1572872 | tf_op jit(solution)/shard_map/ppermute | solution.py:27
  460.8 96.4 %collective-permute-start.105 = (bf16[128,2048]{1,0:T(8,128)(2,1)S(1)}, bf16[128,2048]{1,0:T(8,128)(2,1)}, u32[]{:S(2)}, u32[]{:S(2)}) collective-permute-start(bf16[128,2048]{1,0:T(8,128)(2,1)S(1)} %collective-permute-done.101), channel_id=1, source_target_pairs={{0,1},{1,0},{2,3},{3,2},{4,5},{5,4},{6,7},{7,6},{8,9},{9,8},{10,11... | collective-permute-start | bytes 1572872 | tf_op jit(solution)/shard_map/ppermute | solution.py:27
  472.7 86.5 %collective-permute-start.106 = (bf16[128,2048]{1,0:T(8,128)(2,1)S(1)}, bf16[128,2048]{1,0:T(8,128)(2,1)}, u32[]{:S(2)}, u32[]{:S(2)}) collective-permute-start(bf16[128,2048]{1,0:T(8,128)(2,1)S(1)} %collective-permute-done.102), channel_id=1, source_target_pairs={{0,1},{1,0},{2,3},{3,2},{4,5},{5,4},{6,7},{7,6},{8,9},{9,8},{10,11... | collective-permute-start | bytes 1572872 | tf_op jit(solution)/shard_map/ppermute | solution.py:27
  475.6 85.5 %collective-permute-start.107 = (bf16[128,2048]{1,0:T(8,128)(2,1)S(1)}, bf16[128,2048]{1,0:T(8,128)(2,1)}, u32[]{:S(2)}, u32[]{:S(2)}) collective-permute-start(bf16[128,2048]{1,0:T(8,128)(2,1)S(1)} %collective-permute-done.103), channel_id=1, source_target_pairs={{0,1},{1,0},{2,3},{3,2},{4,5},{5,4},{6,7},{7,6},{8,9},{9,8},{10,11... | collective-permute-start | bytes 1572872 | tf_op jit(solution)/shard_map/ppermute | solution.py:27
  655.9 62.3 %collective-permute-start.108 = (bf16[512,2048]{1,0:T(8,128)(2,1)}, bf16[512,2048]{1,0:T(8,128)(2,1)}, u32[]{:S(2)}, u32[]{:S(2)}) collective-permute-start(bf16[512,2048]{1,0:T(8,128)(2,1)} %slice.1323), channel_id=1, source_target_pairs={{0,1},{1,0},{2,3},{3,2},{4,5},{5,4},{6,7},{7,6},{8,9},{9,8},{10,11... | collective-permute-start | bytes 6291464 | tf_op jit(solution)/shard_map/ppermute | solution.py:27
  664.7 57.4 %collective-permute-start.81 = (bf16[512,2048]{1,0:T(8,128)(2,1)}, bf16[512,2048]{1,0:T(8,128)(2,1)S(1)}, u32[]{:S(2)}, u32[]{:S(2)}) collective-permute-start(bf16[512,2048]{1,0:T(8,128)(2,1)} %slice.1325), channel_id=1, source_target_pairs={{0,1},{1,0},{2,3},{3,2},{4,5},{5,4},{6,7},{7,6},{8,9},{9,8},{10,11... | collective-permute-start | bytes 6291464 | tf_op jit(solution)/shard_map/ppermute | solution.py:27
  703.8 53.0 %collective-permute-start.160 = (bf16[512,1024]{1,0:T(8,128)(2,1)}, bf16[512,1024]{1,0:T(8,128)(2,1)}, u32[]{:S(2)}, u32[]{:S(2)}) collective-permute-start(bf16[512,1024]{1,0:T(8,128)(2,1)} %pad_maximum_fusion.3), channel_id=1, source_target_pairs={{0,16},{8,24},{16,0},{24,8},{1,17},{9,25},{17,1},{25,9},{2,18},{10... | collective-permute-start | bytes 3145736 | tf_op jit(solution)/shard_map/ppermute | solution.py:32
  709.1 49.0 %collective-permute-start.158 = (bf16[512,1024]{1,0:T(8,128)(2,1)}, bf16[512,1024]{1,0:T(8,128)(2,1)}, u32[]{:S(2)}, u32[]{:S(2)}) collective-permute-start(bf16[512,1024]{1,0:T(8,128)(2,1)} %pad_maximum_fusion.2), channel_id=1, source_target_pairs={{0,8},{8,0},{16,24},{24,16},{1,9},{9,1},{17,25},{25,17},{2,10},{10... | collective-permute-start | bytes 3145736 | tf_op jit(solution)/shard_map/ppermute | solution.py:32
  715.0 75.8 %collective-permute-start.164 = (bf16[512,1024]{1,0:T(8,128)(2,1)}, bf16[512,1024]{1,0:T(8,128)(2,1)S(1)}, u32[]{:S(2)}, u32[]{:S(2)}) collective-permute-start(bf16[512,1024]{1,0:T(8,128)(2,1)} %pad_maximum_fusion.5), channel_id=1, source_target_pairs={{0,16},{8,24},{16,0},{24,8},{1,17},{9,25},{17,1},{25,9},{2,18},{10... | collective-permute-start | bytes 3145736 | tf_op jit(solution)/shard_map/ppermute | solution.py:32
  747.0 43.8 %collective-permute-start.162 = (bf16[512,1024]{1,0:T(8,128)(2,1)S(1)}, bf16[512,1024]{1,0:T(8,128)(2,1)S(1)}, u32[]{:S(2)}, u32[]{:S(2)}) collective-permute-start(bf16[512,1024]{1,0:T(8,128)(2,1)S(1)} %copy-done.17), channel_id=1, source_target_pairs={{0,8},{8,0},{16,24},{24,16},{1,9},{9,1},{17,25},{25,17},{2,10},{10... | collective-permute-start | bytes 3145736 | tf_op jit(solution)/shard_map/ppermute | solution.py:32
  828.1 122.8 %collective-permute-start.168 = (bf16[1024,512]{1,0:T(8,128)(2,1)S(1)}, bf16[1024,512]{1,0:T(8,128)(2,1)}, u32[]{:S(2)}, u32[]{:S(2)}) collective-permute-start(bf16[1024,512]{1,0:T(8,128)(2,1)S(1)} %pad_maximum_fusion.7), channel_id=1, source_target_pairs={{0,16},{8,24},{16,0},{24,8},{1,17},{9,25},{17,1},{25,9},{2,18},{10... | collective-permute-start | bytes 3145736 | tf_op jit(solution)/shard_map/ppermute | solution.py:32
  832.4 32.4 %collective-permute-start.97 = (f32[256,1024]{1,0:T(8,128)S(1)}, f32[256,1024]{1,0:T(8,128)}, u32[]{:S(2)}, u32[]{:S(2)}) collective-permute-start(f32[256,1024]{1,0:T(8,128)S(1)} %slice.1071), channel_id=1, source_target_pairs={{0,1},{1,0},{2,3},{3,2},{4,5},{5,4},{6,7},{7,6},{8,9},{9,8},{10,11... | collective-permute-start | bytes 3145736 | tf_op jit(solution)/shard_map/ppermute | solution.py:27
  834.7 85.8 %collective-permute-start.145 = (bf16[128,1024]{0,1:T(8,128)(2,1)}, bf16[128,1024]{0,1:T(8,128)(2,1)}, u32[]{:S(2)}, u32[]{:S(2)}) collective-permute-start(bf16[128,1024]{0,1:T(8,128)(2,1)} %pad_maximum_fusion.21), channel_id=1, source_target_pairs={{0,16},{8,24},{16,0},{24,8},{1,17},{9,25},{17,1},{25,9},{2,18},{10... | collective-permute-start | bytes 786440 | tf_op jit(solution)/shard_map/ppermute | solution.py:32
  835.9 68.8 %collective-permute-start.140 = (bf16[128,1024]{0,1:T(8,128)(2,1)S(1)}, bf16[128,1024]{0,1:T(8,128)(2,1)S(1)}, u32[]{:S(2)}, u32[]{:S(2)}) collective-permute-start(bf16[128,1024]{0,1:T(8,128)(2,1)S(1)} %pad_maximum_fusion.19), channel_id=1, source_target_pairs={{0,16},{8,24},{16,0},{24,8},{1,17},{9,25},{17,1},{25,9},{2,18},{10... | collective-permute-start | bytes 786440 | tf_op jit(solution)/shard_map/ppermute | solution.py:32
  (217 other events, 3151.3 us)

commit v2 on v1

v2 whole, which is shorter than its diff:
```python
import functools
import math

import jax
import jax.numpy as jnp
from jax import lax
from jax.experimental import pallas as pl
from jax.experimental.pallas import tpu as pltpu
from jax.sharding import PartitionSpec as P

HEAD_DIM = 64
LANES = 128
EPSILON = 1e-05
ROPE_BASE = 500000.0
MASKED = -1e30
VMEM_LIMIT = 56 * 1024 * 1024
F32 = jnp.float32
BF16 = jnp.bfloat16


def folded_order(count):
    return list(range(0, count, 2)) + list(range(1, count, 2))[::-1]


def swap_core(array):
    ctx = lax.axis_size("ctx")
    return lax.ppermute(array, "ctx", [(i, i ^ 1) for i in range(ctx)])


def swap_seq(array, bit):
    seq = lax.axis_size("seq")
    return lax.ppermute(array, "seq", [(i, i ^ bit) for i in range(seq)])


def ring_step(array):
    chips = lax.axis_size("ctx") // 2
    order = folded_order(chips)
    pairs = [
        (order[i] * 2 + core, order[(i + 1) % chips] * 2 + core)
        for i in range(chips)
        for core in range(2)
    ]
    return lax.ppermute(array, "ctx", pairs)


def ring_gather(array):
    slots = [array]
    for _ in range(lax.axis_size("ctx") // 2 - 1):
        slots.append(ring_step(slots[-1]))
    return slots


def ring_scatter(parts):
    chips = len(parts)
    total = parts[1 % chips].astype(F32)
    for k in range(2, chips + 1):
        total = ring_step(total.astype(BF16)).astype(F32) + parts[k % chips].astype(F32)
    return total


def cube_gather(array, route):
    seq = lax.axis_size("seq")
    bits = [1 << i for i in range(seq.bit_length() - 1)]
    pieces = {0: array}
    for bit in bits if route == 0 else bits[::-1]:
        pieces.update({r ^ bit: swap_seq(piece, bit) for r, piece in pieces.items()})
    return [pieces[r] for r in range(seq)]


def cube_scatter(chunks, route):
    seq = lax.axis_size("seq")
    bits = [1 << i for i in range(seq.bit_length() - 1)]
    held = dict(enumerate(chunks))
    for bit in bits if route == 0 else bits[::-1]:
        held = {
            r: held[r].astype(F32) + swap_seq(held[r ^ bit].astype(BF16), bit).astype(F32)
            for r in held
            if not r & bit
        }
    return held[0]


def after(array, *others):
    return lax.optimization_barrier((array, *others))[0]


def scaled_frequency():
    half_dim = HEAD_DIM // 2
    base_freq = ROPE_BASE ** (-jnp.arange(half_dim, dtype=F32) * 2.0 / HEAD_DIM)
    wave = 2.0 * math.pi / base_freq
    smooth = (8192.0 / wave - 1.0) / 3.0
    middle = (1.0 - smooth) * base_freq / 32.0 + smooth * base_freq
    return jnp.where(wave < 2048.0, base_freq, jnp.where(wave > 8192.0, base_freq / 32.0, middle))


def rope_tables(positions):
    angles = positions.astype(F32)[:, None] * scaled_frequency()[None, :]
    cosine, sine = jnp.cos(angles), jnp.sin(angles)
    return (
        jnp.concatenate([cosine] * 4, axis=1),
        jnp.concatenate([-sine, sine, -sine, sine], axis=1),
    )


def rotate_lanes(values, cosine, sine):
    lane = lax.broadcasted_iota(jnp.int32, values.shape, 1)
    partner = jnp.where(
        (lane % HEAD_DIM) < HEAD_DIM // 2,
        pltpu.roll(values, LANES - HEAD_DIM // 2, 1),
        pltpu.roll(values, HEAD_DIM // 2, 1),
    )
    return values * cosine + partner * sine


SMEM = pltpu.SMEM
ANYWHERE = pl.BlockSpec(memory_space=pl.ANY)
SCALARS = pl.BlockSpec(memory_space=pltpu.SMEM)
PARAMS = pltpu.CompilerParams(vmem_limit_bytes=VMEM_LIMIT)
NT = (((1,), (1,)), ((), ()))


def cost(flops, nbytes, transcendentals=0):
    return pl.CostEstimate(
        flops=int(flops), bytes_accessed=int(nbytes), transcendentals=int(transcendentals)
    )


def dot(left, right):
    return jnp.dot(left, right, preferred_element_type=F32)


def dot_nt(left, right):
    return lax.dot_general(left, right, NT, preferred_element_type=F32)


def transposed(values):
    return values.astype(F32).T.astype(BF16)


def pack_kernel(kv_half, core_ref, wq, wk, wv, wo, gains, mine, other):
    def fill(out, which):
        at = 0
        half = wq.shape[1] // 2
        out[:, at : at + half] = wq[:, which * half : (which + 1) * half]
        at += half
        for i in range(kv_half // LANES):
            for source in (wk, wv):
                lo = which * kv_half + i * LANES
                out[:, at : at + LANES] = source[:, lo : lo + LANES]
                at += LANES
        out[:, at : at + LANES] = gains[...]
        at += LANES
        half = wo.shape[1] // 2
        out[:, at : at + half] = wo[:, which * half : (which + 1) * half]

    for core in range(2):

        @pl.when(core_ref[0] == core)
        def _():
            fill(mine, core)
            fill(other, 1 - core)


def pack(core, wq, wk, wv, wo, gains):
    rows = wq.shape[0]
    width = (wq.shape[1] + wk.shape[1] + wv.shape[1] + wo.shape[1]) // 2 + LANES
    shape = jax.ShapeDtypeStruct((rows, width), BF16)
    whole = [pl.BlockSpec(memory_space=pltpu.VMEM)] * 5
    return pl.pallas_call(
        functools.partial(pack_kernel, wk.shape[1] // 2),
        in_specs=[SCALARS] + whole,
        out_shape=[shape, shape],
        compiler_params=PARAMS,
        cost_estimate=cost(0, 8 * rows * width),
    )(core, wq, wk, wv, wo, gains)


def stack_kernel(cut, core_ref, mine, other, left, right):
    rows = mine.shape[0]
    for core in range(2):

        @pl.when(core_ref[0] == core)
        def _():
            for source, at in ((mine, core), (other, 1 - core)):
                left[at * rows : (at + 1) * rows] = source[:, :cut]
                right[at * rows : (at + 1) * rows] = source[:, cut:]


def stack_pieces(core, mine, other, cut):
    rows, width = mine.shape
    return pl.pallas_call(
        functools.partial(stack_kernel, cut),
        in_specs=[SCALARS] + [pl.BlockSpec(memory_space=pltpu.VMEM)] * 2,
        out_shape=[
            jax.ShapeDtypeStruct((2 * rows, cut), BF16),
            jax.ShapeDtypeStruct((2 * rows, width - cut), BF16),
        ],
        compiler_params=PARAMS,
        cost_estimate=cost(0, 8 * rows * width),
    )(core, mine, other)


def qkv_kernel(count, batches, query_blocks, *refs):
    core_ref, starts, x_own, x_oth, cos_ref, sin_ref = refs[:6]
    pieces = refs[6 : 6 + count]
    q_ref, kv_ref, normed, gains_ref, w_out, w, sems, out_sem = refs[6 + count :]
    step = pl.program_id(0)
    rows, depth = normed.shape
    slots = rows // (2 * batches)

    def arriving(i):
        start = pl.multiple_of(starts[i], 16)
        return pltpu.make_async_copy(
            pieces[i], w.at[pl.ds(start, pieces[i].shape[0])], sems.at[i]
        )

    @pl.when(step == 0)
    def _():
        for i in range(count):
            arriving(i).start()
        for i in range(count):
            arriving(i).wait()
        pltpu.make_async_copy(w, w_out, out_sem.at[0]).start()
        table = w[:, w.shape[1] - LANES :].astype(F32).T
        gains_ref[...] = table[:8]
        for source, which in ((x_own, core_ref[0]), (x_oth, 1 - core_ref[0])):
            for b in range(batches):
                x = source[b * slots : (b + 1) * slots].astype(F32)
                inverse = lax.rsqrt(jnp.mean(x * x, axis=-1, keepdims=True) + EPSILON)
                at = pl.multiple_of((2 * b + which) * slots, slots)
                normed[pl.ds(at, slots)] = (x * inverse * table[:1]).astype(BF16)

    block = 2 * LANES
    at = pl.multiple_of(step * block, block)
    raw = dot(normed[...], w[:, pl.ds(at, block)])
    left = rotate_lanes(raw[:, :LANES], cos_ref[...], sin_ref[...])

    @pl.when(step < query_blocks)
    def _():
        right = rotate_lanes(raw[:, LANES:], cos_ref[...], sin_ref[...])
        scale = 1.0 / math.sqrt(HEAD_DIM)
        q_ref[:, :LANES] = (left * scale).astype(BF16)
        q_ref[:, LANES:] = (right * scale).astype(BF16)

    @pl.when(step >= query_blocks)
    def _():
        kv_ref[:, :LANES] = left.astype(BF16)
        kv_ref[:, LANES:] = raw[:, LANES:].astype(BF16)

    @pl.when(step == pl.num_programs(0) - 1)
    def _():
        pltpu.make_async_copy(w, w_out, out_sem.at[0]).wait()


def project_qkv(core, starts, x_own, x_oth, cosine, sine, pieces, batches, query_width, kv_width):
    rows, depth = 2 * x_own.shape[0], x_own.shape[1]
    block = 2 * LANES
    query_blocks = query_width // block
    width = pieces[0].shape[1]
    count = len(pieces)

    def whole(shape):
        return pl.BlockSpec(shape, lambda j: (0, 0))

    return pl.pallas_call(
        functools.partial(qkv_kernel, count, batches, query_blocks),
        grid=((query_width + 2 * kv_width) // block,),
        in_specs=[SCALARS, SCALARS, whole(x_own.shape), whole(x_own.shape)]
        + [whole((rows, LANES))] * 2
        + [ANYWHERE] * count,
        out_specs=[
            pl.BlockSpec((rows, block), lambda j: (0, jnp.minimum(j, query_blocks - 1))),
            pl.BlockSpec((rows, block), lambda j: (0, jnp.maximum(j - query_blocks, 0))),
            whole((rows, depth)),
            whole((8, depth)),
            ANYWHERE,
        ],
        out_shape=[
            jax.ShapeDtypeStruct((rows, query_width), BF16),
            jax.ShapeDtypeStruct((rows, 2 * kv_width), BF16),
            jax.ShapeDtypeStruct((rows, depth), BF16),
            jax.ShapeDtypeStruct((8, depth), F32),
            jax.ShapeDtypeStruct((depth, width), BF16),
        ],
        scratch_shapes=[
            pltpu.VMEM((depth, width), BF16),
            pltpu.SemaphoreType.DMA((count,)),
            pltpu.SemaphoreType.DMA((1,)),
        ],
        compiler_params=PARAMS,
        cost_estimate=cost(2 * rows * depth * width, 4 * rows * depth + 4 * depth * width),
    )(core, starts, x_own, x_oth, cosine, sine, *pieces)


def set_bias(limit_ref, kpos_ref, qpos_ref, bias):
    @pl.when(pl.program_id(1) == 0)
    def _():
        limit = limit_ref[pl.program_id(0)]
        allowed = (kpos_ref[...] <= qpos_ref[...]) & (kpos_ref[...] < limit)
        bias[...] = jnp.where(allowed, 0.0, MASKED)


def attend_kernel(chips, limit_ref, kpos_ref, qpos_ref, q_ref, *refs):
    slots, (out_ref, lse_ref, bias) = refs[:chips], refs[chips:]
    set_bias(limit_ref, kpos_ref, qpos_ref, bias)
    heads = q_ref.shape[1] // HEAD_DIM
    kv = jnp.concatenate([slot[...] for slot in slots], axis=0)
    q_t = transposed(q_ref[...])
    v_t = transposed(kv[:, LANES:])
    outs = []
    for h in range(heads):
        a = h * 2 // heads
        k_h = kv[:, a * HEAD_DIM : (a + 1) * HEAD_DIM]
        scores = dot(k_h, q_t[h * HEAD_DIM : (h + 1) * HEAD_DIM]) + bias[...]
        top = jnp.max(scores, axis=0, keepdims=True)
        shifted = jnp.exp(scores - top)
        total = jnp.sum(shifted, axis=0, keepdims=True)
        out_t = dot(v_t[a * HEAD_DIM : (a + 1) * HEAD_DIM], shifted.astype(BF16))
        outs.append(out_t / total)
        lse_ref[h : h + 1, :] = top + jnp.log(total)
    out_ref[...] = jnp.concatenate(outs, axis=0).T.astype(BF16)


def attention_specs(batches, chips, rows, keys, width, heads, pairs):
    def at(shape):
        return pl.BlockSpec(shape, lambda b, i, n: (b, i))

    return (
        [
            pl.BlockSpec((keys, 1), lambda b, i, n: (0, 0)),
            pl.BlockSpec((1, rows), lambda b, i, n: (0, 0)),
            at((rows, width)),
        ]
        + [at((rows, 2 * LANES))] * chips,
        at((rows, width)),
        pl.BlockSpec((heads, rows), lambda b, i, n: (b * pairs + i, 0)),
    )


def attend(q, kv_slots, limits, kpos, qpos):
    rows, keys, batches, chips = qpos.shape[1], kpos.shape[0], limits.shape[0], len(kv_slots)
    pairs = kv_slots[0].shape[1] // (2 * LANES)
    width = q.shape[1] // pairs
    heads = width // HEAD_DIM
    ins, out, lse = attention_specs(batches, chips, rows, keys, width, heads, pairs)
    return pl.pallas_call(
        functools.partial(attend_kernel, chips),
        grid_spec=pltpu.PrefetchScalarGridSpec(
            num_scalar_prefetch=1,
            grid=(batches, pairs),
            in_specs=ins,
            out_specs=[out, lse],
            scratch_shapes=[pltpu.VMEM((keys, rows), F32)],
        ),
        out_shape=[
            jax.ShapeDtypeStruct(q.shape, BF16),
            jax.ShapeDtypeStruct((batches * pairs * heads, rows), F32),
        ],
        compiler_params=PARAMS,
        cost_estimate=cost(
            16 * batches * rows * keys * q.shape[1],
            4 * q.size + 2 * chips * kv_slots[0].size,
            batches * rows * keys * q.shape[1] // HEAD_DIM,
        ),
    )(limits, kpos, qpos, q, *kv_slots)


def attend_back_kernel(chips, limit_ref, kpos_ref, qpos_ref, q_ref, *refs):
    slots = refs[:chips]
    do_mine, do_other, lse_ref, cos_ref, sin_ref, dq_ref = refs[chips : chips + 6]
    d_slots, bias = refs[chips + 6 : 2 * chips + 6], refs[2 * chips + 6]
    set_bias(limit_ref, kpos_ref, qpos_ref, bias)
    rows, width = q_ref.shape
    heads = width // HEAD_DIM
    per_kv = heads // 2
    kv = jnp.concatenate([slot[...] for slot in slots], axis=0)
    d_out = (do_mine[...] + do_other[...].astype(F32)).astype(BF16)
    q_t = transposed(q_ref[...])
    do_t = transposed(d_out)
    k_t = transposed(kv[:, :LANES])
    lane = lax.broadcasted_iota(jnp.int32, (kv.shape[0], LANES), 1)
    d_queries = []
    d_keys, d_values = [], []
    for a in range(2):
        k_h = kv[:, a * HEAD_DIM : (a + 1) * HEAD_DIM]
        v_h = kv[:, LANES + a * HEAD_DIM : LANES + (a + 1) * HEAD_DIM]
        dk_sum, dv_sum = [None, None], [None, None]
        for g in range(per_kv):
            h = a * per_kv + g
            head = slice(h * HEAD_DIM, (h + 1) * HEAD_DIM)
            pair = slice((h // 2) * LANES, (h // 2 + 1) * LANES)
            scores = dot(k_h, q_t[head]) + bias[...]
            probs = jnp.exp(scores - lse_ref[h : h + 1, :])
            d_probs = dot(v_h, do_t[head])
            mean = jnp.sum(d_probs * probs, axis=0, keepdims=True)
            d_scores = (probs * (d_probs - mean)).astype(BF16)
            d_queries.append(dot(k_t[a * HEAD_DIM : (a + 1) * HEAD_DIM], d_scores))
            dk_term = dot(d_scores, q_ref[:, pair])
            dv_term = dot(probs.astype(BF16), d_out[:, pair])
            e = h % 2
            dk_sum[e] = dk_term if dk_sum[e] is None else dk_sum[e] + dk_term
            dv_sum[e] = dv_term if dv_sum[e] is None else dv_sum[e] + dv_term
        for sums, kept in ((dk_sum, d_keys), (dv_sum, d_values)):
            mixed = jnp.where(lane < HEAD_DIM, sums[0], sums[1])
            kept.append(mixed + pltpu.roll(mixed, HEAD_DIM, 1))
    d_key = jnp.where(lane < HEAD_DIM, d_keys[0], d_keys[1])
    d_value = jnp.where(lane < HEAD_DIM, d_values[0], d_values[1])
    for k, d_slot in enumerate(d_slots):
        d_slot[:, :LANES] = d_key[k * rows : (k + 1) * rows].astype(BF16)
        d_slot[:, LANES:] = d_value[k * rows : (k + 1) * rows].astype(BF16)
    d_query = jnp.concatenate(d_queries, axis=0).T
    for at in range(width // LANES):
        cut = slice(at * LANES, (at + 1) * LANES)
        turned = rotate_lanes(d_query[:, cut], cos_ref[...], -sin_ref[...])
        dq_ref[:, cut] = (turned / math.sqrt(HEAD_DIM)).astype(BF16)


def attend_back(q, kv_slots, do_mine, do_other, lse, limits, kpos, qpos, cosine, sine):
    rows, keys, batches, chips = qpos.shape[1], kpos.shape[0], limits.shape[0], len(kv_slots)
    pairs = kv_slots[0].shape[1] // (2 * LANES)
    width = q.shape[1] // pairs
    heads = width // HEAD_DIM
    ins, out, lse_spec = attention_specs(batches, chips, rows, keys, width, heads, pairs)
    table = pl.BlockSpec((rows, LANES), lambda b, i, n: (0, 0))
    return pl.pallas_call(
        functools.partial(attend_back_kernel, chips),
        grid_spec=pltpu.PrefetchScalarGridSpec(
            num_scalar_prefetch=1,
            grid=(batches, pairs),
            in_specs=ins + [out, out, lse_spec, table, table],
            out_specs=[out] + ins[3 : 3 + chips],
            scratch_shapes=[pltpu.VMEM((keys, rows), F32)],
        ),
        out_shape=[jax.ShapeDtypeStruct(q.shape, BF16)]
        + [jax.ShapeDtypeStruct(slot.shape, BF16) for slot in kv_slots],
        compiler_params=PARAMS,
        cost_estimate=cost(
            40 * batches * rows * keys * q.shape[1],
            10 * q.size + 4 * chips * kv_slots[0].size,
            batches * rows * keys * q.shape[1] // HEAD_DIM,
        ),
    )(limits, kpos, qpos, q, *kv_slots, do_mine, do_other, lse, cosine, sine)


def unrotate_kernel(last_ref, own_ref, cos_ref, sin_ref, out_ref):
    total = last_ref[...].astype(F32) + own_ref[...].astype(F32)
    for at in range(total.shape[1] // LANES):
        cut = slice(at * LANES, (at + 1) * LANES)
        part = total[:, cut]
        if at % 2 == 0:
            part = rotate_lanes(part, cos_ref[...], -sin_ref[...])
        out_ref[:, cut] = part.astype(BF16)


def unrotate(last, own, cosine, sine):
    return pl.pallas_call(
        unrotate_kernel,
        out_shape=jax.ShapeDtypeStruct(own.shape, BF16),
        compiler_params=PARAMS,
        cost_estimate=cost(0, 6 * own.size),
    )(last, own, cosine, sine)


def split_rows(batches, core_ref, acc, own, other):
    slots = acc.shape[0] // (2 * batches)
    for out, which in ((own, core_ref[0]), (other, 1 - core_ref[0])):
        for b in range(batches):
            at = pl.multiple_of((2 * b + which) * slots, slots)
            out[b * slots : (b + 1) * slots] = acc[pl.ds(at, slots)].astype(out.dtype)


def out_kernel(batches, chips, core_ref, starts, o_mine, o_other, *refs):
    count = len(refs) - 6
    pieces = refs[:count]
    own, other, w_out, w, acc, sems = refs[count:]
    shard = pieces[0].shape[0] // chips
    half = o_mine.shape[1]
    arriving = [
        pltpu.make_async_copy(
            pieces[r].at[pl.ds(k * shard, shard)],
            w.at[pl.ds(pl.multiple_of(starts[r * chips + k], 16), shard)],
            sems.at[r * chips + k],
        )
        for r in range(count)
        for k in range(chips)
    ]
    for copy in arriving:
        copy.start()
    for copy in arriving:
        copy.wait()
    leaving = pltpu.make_async_copy(w, w_out, sems.at[count * chips])
    leaving.start()
    block = 2 * LANES

    @pl.loop(0, w.shape[1] // block)
    def _(j):
        cut = pl.ds(pl.multiple_of(j * block, block), block)
        acc[:, cut] = dot(o_mine[...], w[:half, cut]) + dot(o_other[...], w[half:, cut])

    split_rows(batches, core_ref, acc, own, other)
    leaving.wait()


def project_out(core, starts, o_mine, o_other, pieces, batches, chips):
    rows, half = o_mine.shape
    width = pieces[0].shape[1]
    count = len(pieces)
    vmem = pl.BlockSpec(memory_space=pltpu.VMEM)
    part = jax.ShapeDtypeStruct((rows // 2, width), F32)
    return pl.pallas_call(
        functools.partial(out_kernel, batches, chips),
        in_specs=[SCALARS, SCALARS, vmem, vmem] + [ANYWHERE] * count,
        out_specs=[vmem, vmem, ANYWHERE],
        out_shape=[part, part, jax.ShapeDtypeStruct((2 * half, width), BF16)],
        scratch_shapes=[
            pltpu.VMEM((2 * half, width), BF16),
            pltpu.VMEM((rows, width), F32),
            pltpu.SemaphoreType.DMA((count * chips + 1,)),
        ],
        compiler_params=PARAMS,
        cost_estimate=cost(4 * rows * half * width, 8 * half * width + 12 * rows * width),
    )(core, starts, o_mine, o_other, *pieces)


def mlp_kernel(seq, filled, *refs):
    x_mine, x_other, d_mine, d_other = refs[:4]
    gates, ups, downs = (refs[4 + i * seq : 4 + (i + 1) * seq] for i in range(3))
    refs = refs[4 + 3 * seq + filled :]
    xs, ds = refs[:seq], refs[seq : 2 * seq]
    hidden_ref, d_gate_ref, d_up_ref = refs[2 * seq : 2 * seq + 3]
    rows = x_mine.shape[0]
    block = x_mine.shape[1] // seq

    @pl.when(pl.program_id(0) == 0)
    def _():
        for r in range(seq):
            cut = slice(r * block, (r + 1) * block)
            xs[r][:rows] = x_mine[:, cut]
            xs[r][rows:] = x_other[:, cut]
            ds[r][:rows] = d_mine[:, cut]
            ds[r][rows:] = d_other[:, cut]

    gate_val = sum(dot(xs[r][...], gates[r][...]) for r in range(seq))
    up_val = sum(dot(xs[r][...], ups[r][...]) for r in range(seq))
    d_hidden = sum(dot_nt(ds[r][...], downs[r][...]) for r in range(seq))
    sigmoid_g = 1.0 / (1.0 + jnp.exp(-gate_val))
    activated = gate_val * sigmoid_g
    slope = sigmoid_g * (1.0 + gate_val * (1.0 - sigmoid_g))
    hidden_ref[...] = (activated * up_val).astype(BF16)
    d_gate_ref[...] = (d_hidden * up_val * slope).astype(BF16)
    d_up_ref[...] = (d_hidden * activated).astype(BF16)


def mlp_slot(slot, slots, x_mine, x_other, d_mine, d_other, gates, ups, downs, kept):
    seq = len(gates)
    rows, width = x_mine.shape
    block = width // seq
    hidden_width = gates[0].shape[1]
    tile = 2 * LANES

    def whole(shape):
        return pl.BlockSpec(shape, lambda j: (0, 0))

    wide = [jax.ShapeDtypeStruct((2 * rows * slots, block), BF16)] * (2 * seq)
    narrow = [jax.ShapeDtypeStruct((2 * rows * slots, hidden_width), BF16)] * 3
    filled = 0 if kept is None else 2 * seq + 3
    first = 4 + 3 * seq
    return pl.pallas_call(
        functools.partial(mlp_kernel, seq, filled),
        grid=(hidden_width // tile,),
        in_specs=[whole((rows, width))] * 4
        + [pl.BlockSpec((block, tile), lambda j: (0, j))] * (2 * seq)
        + [pl.BlockSpec((tile, block), lambda j: (j, 0))] * seq
        + [ANYWHERE] * filled,
        out_specs=[pl.BlockSpec((2 * rows, block), lambda j: (slot, 0))] * (2 * seq)
        + [pl.BlockSpec((2 * rows, tile), lambda j: (slot, j))] * 3,
        out_shape=wide + narrow,
        input_output_aliases={first + i: i for i in range(filled)},
        compiler_params=PARAMS,
        cost_estimate=cost(
            12 * rows * width * hidden_width,
            6 * width * hidden_width + 24 * rows * width,
            2 * rows * hidden_width,
        ),
    )(x_mine, x_other, d_mine, d_other, *gates, *ups, *downs, *([] if kept is None else kept))


def mlp_back_kernel(seq, hidden, d_gate, d_up, *refs):
    weights = refs[: 3 * seq]
    back_mine, back_other, out_mine, out_other = refs[3 * seq : 3 * seq + 4]
    held, sems = refs[3 * seq + 4 : -1], refs[-1]
    rows = back_mine.shape[0]
    block = back_mine.shape[1] // seq
    copies = [pltpu.make_async_copy(weights[i], held[i], sems.at[i]) for i in range(3 * seq)]
    for r in range(seq):
        for i in range(3):
            copies[i * seq + r].start()
    for r in range(seq):
        cut = slice(r * block, (r + 1) * block)
        for i in range(3):
            copies[i * seq + r].wait()
        back = dot_nt(d_gate[...], held[r][...]) + dot_nt(d_up[...], held[seq + r][...])
        back_mine[:, cut] = back[:rows].astype(BF16)
        back_other[:, cut] = back[rows:].astype(BF16)
        out = dot(hidden[...], held[2 * seq + r][...])
        out_mine[:, cut] = out[:rows].astype(BF16)
        out_other[:, cut] = out[rows:].astype(BF16)


def mlp_back(slot, slots, hidden, d_gate, d_up, gates, ups, downs):
    seq = len(gates)
    rows, width = hidden.shape[0] // (2 * slots), gates[0].shape[0] * seq
    hidden_width = hidden.shape[1]
    weights = [*gates, *ups, *downs]
    return pl.pallas_call(
        functools.partial(mlp_back_kernel, seq),
        grid=(1,),
        in_specs=[pl.BlockSpec((2 * rows, hidden_width), lambda j: (slot, 0))] * 3
        + [ANYWHERE] * (3 * seq),
        out_specs=[pl.BlockSpec((rows, width), lambda j: (0, 0))] * 4,
        out_shape=[jax.ShapeDtypeStruct((rows, width), BF16)] * 4,
        scratch_shapes=[pltpu.VMEM(w.shape, BF16) for w in weights]
        + [pltpu.SemaphoreType.DMA((3 * seq,))],
        compiler_params=PARAMS,
        cost_estimate=cost(
            12 * rows * width * hidden_width, 6 * width * hidden_width + 14 * rows * width
        ),
    )(hidden, d_gate, d_up, *weights)


def d_attended_kernel(batches, other_blocks, core_ref, d_own, d_oth, w_ref, mine, other, d_rows):
    step = pl.program_id(0)
    slots = d_own.shape[0] // batches

    @pl.when(step == 0)
    def _():
        for source, which in ((d_own, core_ref[0]), (d_oth, 1 - core_ref[0])):
            for b in range(batches):
                at = pl.multiple_of((2 * b + which) * slots, slots)
                d_rows[pl.ds(at, slots)] = source[b * slots : (b + 1) * slots]

    term = dot_nt(d_rows[...], w_ref[...])

    @pl.when(step < other_blocks)
    def _():
        other[...] = term.astype(BF16)

    @pl.when(step >= other_blocks)
    def _():
        mine[...] = term


def d_attended(core, d_own, d_oth, w, batches):
    rows, width = 2 * d_own.shape[0], d_own.shape[1]
    heads_width = w.shape[0]
    block = 2 * LANES
    blocks = heads_width // 2 // block

    def whole(shape):
        return pl.BlockSpec(shape, lambda j: (0, 0))

    return pl.pallas_call(
        functools.partial(d_attended_kernel, batches, blocks),
        grid=(2 * blocks,),
        in_specs=[
            SCALARS,
            whole(d_own.shape),
            whole(d_own.shape),
            pl.BlockSpec((block, width), lambda j: ((j + blocks) % (2 * blocks), 0)),
        ],
        out_specs=[
            pl.BlockSpec((rows, block), lambda j: (0, jnp.maximum(j - blocks, 0))),
            pl.BlockSpec((rows, block), lambda j: (0, jnp.minimum(j, blocks - 1))),
            whole((rows, width)),
        ],
        out_shape=[
            jax.ShapeDtypeStruct((rows, heads_width // 2), F32),
            jax.ShapeDtypeStruct((rows, heads_width // 2), BF16),
            jax.ShapeDtypeStruct((rows, width), BF16),
        ],
        compiler_params=PARAMS,
        cost_estimate=cost(
            2 * rows * width * heads_width, 2 * width * heads_width + 6 * rows * heads_width
        ),
    )(core, d_own, d_oth, w)


def grad_kernel(count, parts, chips, starts, *refs):
    sources, right, outs, turned = refs[:count], refs[count], refs[count + 1 : -1], refs[-1]
    shard = turned.shape[0] // (parts * chips)
    at = 0
    for source in sources:
        for lo in range(0, source.shape[1], 4 * LANES):
            turned[at : at + 4 * LANES] = transposed(source[:, lo : lo + 4 * LANES])
            at += 4 * LANES
    for r in range(parts):
        left = jnp.concatenate(
            [
                turned[pl.ds(pl.multiple_of(starts[r * chips + k], 16), shard)]
                for k in range(chips)
            ],
            axis=0,
        )
        outs[r][...] = dot(left, right[...]).astype(BF16)


def grad_chunks(starts, sources, right, parts, chips):
    rows = right.shape[0]
    depth = sum(source.shape[1] for source in sources)
    shape = jax.ShapeDtypeStruct((depth // parts, right.shape[1]), BF16)
    vmem = pl.BlockSpec(memory_space=pltpu.VMEM)
    return pl.pallas_call(
        functools.partial(grad_kernel, len(sources), parts, chips),
        in_specs=[SCALARS] + [vmem] * (len(sources) + 1),
        out_shape=[shape] * parts,
        scratch_shapes=[pltpu.VMEM((depth, rows), BF16)],
        compiler_params=PARAMS,
        cost_estimate=cost(
            2 * rows * depth * right.shape[1], 2 * rows * depth + 2 * depth * right.shape[1]
        ),
    )(starts, *sources, right)


def d_normed_kernel(batches, core_ref, dq_ref, dkv_ref, w_ref, own, other, acc):
    width = dq_ref.shape[1]
    acc[...] = dot_nt(dq_ref[...], w_ref[:, :width]) + dot_nt(
        dkv_ref[...], w_ref[:, width : width + dkv_ref.shape[1]]
    )
    split_rows(batches, core_ref, acc, own, other)


def d_normed_rows(core, dq, dkv, w, batches):
    rows = dq.shape[0]
    depth, width = w.shape
    block = 4 * LANES

    def whole(shape):
        return pl.BlockSpec(shape, lambda j: (0, 0))

    part = pl.BlockSpec((rows // 2, block), lambda j: (0, j))
    return pl.pallas_call(
        functools.partial(d_normed_kernel, batches),
        grid=(depth // block,),
        in_specs=[
            SCALARS,
            whole(dq.shape),
            whole(dkv.shape),
            pl.BlockSpec((block, width), lambda j: (j, 0)),
        ],
        out_specs=[part, part],
        out_shape=[jax.ShapeDtypeStruct((rows // 2, depth), F32)] * 2,
        scratch_shapes=[pltpu.VMEM((rows, block), F32)],
        compiler_params=PARAMS,
        cost_estimate=cost(2 * rows * depth * width, 2 * depth * width + 4 * rows * depth),
    )(core, dq, dkv, w)


def rms_inverse(values):
    return lax.rsqrt(jnp.mean(values * values, axis=-1, keepdims=True) + EPSILON)


def rms_back(grad_in, plain, inverse, gain):
    scaled = grad_in * gain
    back = inverse * (scaled - plain * jnp.mean(scaled * plain, axis=-1, keepdims=True))
    return (back, jnp.sum(grad_in * plain, axis=0, keepdims=True))


def body(
    tokens,
    lengths,
    cotangent,
    attn_gain,
    w_query,
    w_key,
    w_value,
    w_out,
    mlp_gain,
    w_gate,
    w_up,
    w_down,
):
    batches, _, slot_count, model_width = tokens.shape
    seq_size, ctx_size = lax.axis_size("seq"), lax.axis_size("ctx")
    chips = ctx_size // 2
    seq_at, ctx_at = lax.axis_index("seq"), lax.axis_index("ctx")
    chip_at, core = ctx_at // 2, ctx_at % 2
    core_ref = core.reshape(1).astype(jnp.int32)
    order = folded_order(chips)
    shard = w_query.shape[0]
    query_half, kv_half = w_query.shape[1] // 2, w_key.shape[1] // 2
    chip_rows = 2 * slot_count
    own_rows = batches * slot_count
    attn_width = query_half + 2 * kv_half
    limits = lengths[:, 0]

    def chip_back(k):
        index = jnp.int32(0)
        for place, chip in enumerate(order):
            index = jnp.where(chip_at == chip, order[(place - k) % chips], index)
        return index

    slot_chip = jnp.stack([chip_back(k) for k in range(chips)])
    rank = (seq_at ^ jnp.arange(seq_size))[:, None] * chips + slot_chip[None, :]
    starts = (rank * (2 * shard)).reshape(-1).astype(jnp.int32)
    out_starts = (starts + core * query_half) % (2 * query_half)

    def half(array, which, axis):
        size = array.shape[axis] // 2
        return lax.dynamic_slice_in_dim(array, which * size, size, axis)

    def mine(array, axis):
        return half(array, core, axis)

    def others(array, axis):
        return half(array, 1 - core, axis)

    def by_core(own, other, axis):
        return jnp.where(
            core == 0,
            jnp.concatenate([own, other], axis),
            jnp.concatenate([other, own], axis),
        )

    def turn_blocks(array):
        block = array.shape[-1] // seq_size
        bit = 1
        while bit < seq_size:
            turned = jnp.concatenate(
                [
                    array[..., (r ^ bit) * block : ((r ^ bit) + 1) * block]
                    for r in range(seq_size)
                ],
                axis=-1,
            )
            array = jnp.where((seq_at & bit) != 0, turned, array)
            bit *= 2
        return array

    gains = jnp.concatenate(
        [attn_gain[:, None], mlp_gain[:, None], jnp.zeros((shard, LANES - 2), BF16)], axis=1
    )
    packed, to_other = pack(core_ref, w_query, w_key, w_value, w_out, gains)
    piece_a, piece_o = stack_pieces(
        core_ref, packed, swap_core(to_other), attn_width + LANES
    )
    ring_a = ring_gather(piece_a)
    cubes_a = [cube_gather(slot, k % 2) for k, slot in enumerate(ring_a)]
    x_own = tokens.reshape(own_rows, model_width)
    x_oth = swap_core(x_own)
    ring_o = jnp.concatenate(ring_gather(after(piece_o, ring_a[-1])), 0)
    cube_o = cube_gather(after(ring_o, cubes_a[-1][1], cubes_a[-1][2]), 0)
    gates = cube_gather(after(w_gate, cube_o[1], cube_o[2]), 1)
    ups = cube_gather(after(w_up, gates[1], gates[2]), 0)
    downs = cube_gather(after(w_down, ups[1], ups[2]), 1)

    q_positions = chip_at * chip_rows + jnp.arange(chip_rows)
    cosine, sine = rope_tables(q_positions)
    cosine_all, sine_all = jnp.tile(cosine, (batches, 1)), jnp.tile(sine, (batches, 1))
    qpos = q_positions[None, :]
    kpos = (slot_chip[:, None] * chip_rows + jnp.arange(chip_rows)[None, :]).reshape(-1, 1)
    own_pos = ctx_at * slot_count + jnp.arange(slot_count)
    valid = (own_pos[None, :] < limits[:, None]).astype(F32).reshape(own_rows, 1)
    d_output = cotangent.reshape(own_rows, model_width).astype(F32) * valid
    d_turned = turn_blocks(d_output.astype(BF16))

    flat_a = [cubes_a[k][r] for r in range(seq_size) for k in range(chips)]
    q, kv, normed_a, gain_rows, attn_w = project_qkv(
        core_ref, starts, x_own, x_oth, cosine_all, sine_all, flat_a, batches, query_half, kv_half
    )
    gain_a, gain_m = gain_rows[0:1], gain_rows[1:2]
    kv_slots = ring_gather(kv)
    d_slots = ring_gather(after(d_turned, ring_o))
    d_pairs = [(slot, swap_core(slot)) for slot in d_slots]
    attended, lse = attend(q, kv_slots, limits, kpos, qpos)
    attended_oth = swap_core(attended)
    branch, branch_oth, out_w = project_out(
        core_ref, out_starts, attended, attended_oth, cube_o, batches, chips
    )

    residual = x_own.astype(F32) + by_core(branch, swap_core(branch_oth), 1)
    inverse_m = rms_inverse(residual)
    x_slots = ring_gather(turn_blocks((residual * inverse_m * gain_m).astype(BF16)))
    kept = None
    back_parts, out_parts = [None] * chips, [None] * chips
    for k in range(chips):
        kept = mlp_slot(
            k, chips, x_slots[k], swap_core(x_slots[k]), *d_pairs[k], gates, ups, downs, kept
        )
        parts = mlp_back(k, chips, *kept[2 * seq_size :], gates, ups, downs)
        back_parts[k] = (parts[0], swap_core(parts[1]))
        out_parts[k] = (parts[2], parts[3])
    d_normed = turn_blocks(
        ring_scatter([own.astype(F32) + oth.astype(F32) for own, oth in back_parts])
    )
    xs, ds = kept[:seq_size], kept[seq_size : 2 * seq_size]
    hidden, d_gate, d_up = kept[2 * seq_size :]

    def rows_product(left, right):
        return jnp.einsum("ri,rj->ij", left, right, preferred_element_type=F32).astype(BF16)

    grad_gate = cube_scatter([rows_product(x, d_gate) for x in xs], 0)
    grad_up = cube_scatter([rows_product(x, d_up) for x in xs], 1)
    grad_down = cube_scatter([rows_product(hidden, d) for d in ds], 0)

    plain_m = residual * inverse_m
    back_m, gain_m_part = rms_back(d_normed, plain_m, inverse_m, gain_m)
    d_resid = d_output + back_m
    d_low = d_resid.astype(BF16)
    do_mine, do_other, d_half = d_attended(
        core_ref, mine(d_low, 1), swap_core(others(d_low, 1)), out_w, batches
    )
    d_query, *d_kv_slots = attend_back(
        q, kv_slots, do_mine, swap_core(do_other), lse, limits, kpos, qpos, cosine, sine
    )

    def owner_sum(chunks, route):
        summed = cube_scatter(chunks, route)
        rows = 2 * shard
        return ring_scatter([summed[k * rows : (k + 1) * rows] for k in range(chips)])

    def own_shard(summed, lanes):
        received = swap_core(others(summed, 0))
        kept_rows = mine(summed, 0)
        edges = [sum(lanes[:i]) for i in range(len(lanes) + 1)]
        return [
            by_core(kept_rows[:, lo:hi], received[:, lo:hi], 1)
            for lo, hi in zip(edges[:-1], edges[1:])
        ]

    grad_out = owner_sum(
        grad_chunks(out_starts, [attended, attended_oth], d_half, seq_size, chips), 1
    )
    (grad_out,) = own_shard(grad_out, [model_width // 2])
    grad_query = owner_sum(grad_chunks(starts, [normed_a], d_query, seq_size, chips), 0)
    (grad_query,) = own_shard(grad_query, [query_half])
    last = d_kv_slots[1 % chips]
    for k in range(2, chips):
        last = (ring_step(last).astype(F32) + d_kv_slots[k].astype(F32)).astype(BF16)
    d_kv = unrotate(ring_step(last), d_kv_slots[0], cosine_all, sine_all)
    grad_kv = owner_sum(grad_chunks(starts, [normed_a], d_kv, seq_size, chips), 1)
    kv_parts = own_shard(grad_kv, [LANES] * (2 * kv_half // LANES))
    grad_kv = [
        jnp.concatenate(
            [part[:, :LANES] for part in kv_parts[i::2]]
            + [part[:, LANES:] for part in kv_parts[i::2]],
            axis=1,
        )
        for i in range(2)
    ]
    d_normed_a, d_normed_oth = d_normed_rows(core_ref, d_query, d_kv, attn_w, batches)
    d_normed_a = d_normed_a + swap_core(d_normed_oth)
    x_own_f = x_own.astype(F32)
    inverse_a = rms_inverse(x_own_f)
    back_a, gain_a_part = rms_back(d_normed_a, x_own_f * inverse_a, inverse_a, gain_a)
    input_grad = d_resid + back_a
    gain_sum = jnp.concatenate([gain_a_part, gain_m_part], 0)
    gain_sum = gain_sum + swap_core(gain_sum)
    bit = 1
    while bit < seq_size:
        gain_sum = gain_sum + swap_seq(gain_sum, bit)
        bit *= 2
    passing = gain_sum
    for _ in range(chips - 1):
        passing = ring_step(passing)
        gain_sum = gain_sum + passing
    gain_sum = lax.dynamic_slice_in_dim(gain_sum, (seq_at * ctx_size + ctx_at) * shard, shard, 1)

    out_parts = [(own, swap_core(oth)) for own, oth in out_parts]
    branch_m = ring_scatter([own.astype(F32) + oth.astype(F32) for own, oth in out_parts])
    activations = (residual + turn_blocks(branch_m)).astype(BF16)
    return (
        activations.reshape(tokens.shape),
        input_grad.reshape(tokens.shape),
        gain_sum[0],
        grad_query,
        grad_kv[0],
        grad_kv[1],
        grad_out,
        gain_sum[1],
        grad_gate,
        grad_up,
        grad_down,
    )


def solution(mesh):
    rows = P(None, "seq", "ctx", None)
    spread = P(("seq", "ctx"))
    spread_rows = P(("seq", "ctx"), None)
    return jax.shard_map(
        body,
        mesh=mesh,
        in_specs=(
            rows,
            P(None, "seq"),
            rows,
            spread,
            spread_rows,
            spread_rows,
            spread_rows,
            spread_rows,
            spread,
            P("seq", "ctx"),
            P("seq", "ctx"),
            P("ctx", "seq"),
        ),
        out_specs=(
            rows,
            rows,
            spread,
            spread_rows,
            spread_rows,
            spread_rows,
            spread_rows,
            spread,
            P("seq", "ctx"),
            P("seq", "ctx"),
            P("ctx", "seq"),
        ),
        check_vma=False,
    )
```

time: 1080 us -> 821 us (0.76)
  Pallas kernels: 79.8 us -> 227 us
  matrix products: 162 us -> 42.1 us
  local copies, waits for them, and re-layouts: 131 us -> 22.7 us
  starting transfers between devices: 199 us -> 122 us
  waiting for transfers between devices: 410 us -> 344 us
  other arithmetic: 86.6 us -> 54.5 us
    pallas_call x7 -> x20, Pallas kernels: 79.8 us -> 227 us  [the longest x4 53 us: mlp_slot(): pl.pallas_call(functools.partial(mlp_kernel, seq, filled), grid=(hidden_w...]
    dot_general x22 -> x12, matrix products: 162 us -> 42.1 us  [rows_product(): jnp.einsum('ri,rj->ij', left, right, preferred_element_type=F32)]
    ppermute x88 -> x44, starting transfers between devices: 97 us -> 46.8 us  [swap_seq(): return lax.ppermute(array, 'seq', [(i, i ^ bit) for i in range(seq)])]
    ppermute x48 -> x36, waiting for transfers between devices: 205 us -> 160 us  [ring_step(): return lax.ppermute(array, 'ctx', pairs)]
    unnamed x208 -> x161, local copies, waits for them, and re-layouts: 54.6 us -> 13.8 us
    slice x71 -> x10, local copies, waits for them, and re-layouts: 31.1 us -> 1.74 us  [the longest x1 1.61 us: body(): gain_a, gain_m = (gain_rows[0:1], gain_rows[1:2])]
    ppermute x48 -> x36, starting transfers between devices: 95.6 us -> 69.6 us  [ring_step(): return lax.ppermute(array, 'ctx', pairs)]
    ppermute x88 -> x44, waiting for transfers between devices: 204 us -> 180 us  [swap_seq(): return lax.ppermute(array, 'seq', [(i, i ^ bit) for i in range(seq)])]
  transfers between devices with their start and end apart: 169 -> 107, of which waited for: 78 -> 51; matrix products, arithmetic and copies ran while one was open for 27% -> 13% of each run, Pallas kernels for 7% -> 27%
where the time goes in v2:
time: 821 us; the launch traced here: 814 us
  waiting for transfers between devices  344 us (42%)
  Pallas kernels  227 us (28%)
  starting transfers between devices  122 us (15%)
  other arithmetic  54.5 us (7%)
  matrix products  42.1 us (5%)
  local copies, waits for them, and re-layouts  22.7 us (3%)
    ppermute x44, waiting for transfers between devices, swap_seq(): return lax.ppermute(array, 'seq', [(i, i ^ bit) for i in range(seq)])  180 us
    ppermute x36, waiting for transfers between devices, ring_step(): return lax.ppermute(array, 'ctx', pairs)  160 us
    ppermute x36, starting transfers between devices, ring_step(): return lax.ppermute(array, 'ctx', pairs)  69.6 us
    pallas_call x4, Pallas kernels, mlp_slot(): pl.pallas_call(functools.partial(mlp_kernel, seq, filled), grid=(hidden_w...  53 us
    pallas_call x4, Pallas kernels, mlp_back(): pl.pallas_call(functools.partial(mlp_back_kernel, seq), grid=(1,), in_spe...  51.6 us
    ppermute x44, starting transfers between devices, swap_seq(): return lax.ppermute(array, 'seq', [(i, i ^ bit) for i in range(seq)])  46.8 us
    dot_general x12, matrix products, rows_product(): jnp.einsum('ri,rj->ij', left, right, preferred_element_type=F32)  42.1 us
    pallas_call x1, Pallas kernels, attend_back(): pl.pallas_call(functools.partial(attend_back_kernel, chips), grid_spec=pl...  34.9 us
  transfers between devices with their start and end apart: 107, of which 51 were waited for; matrix products, arithmetic and copies ran while one was open for 13% of the time, Pallas kernels for 27%

profile of v2, /device:TPU:0, one launch (start us, length us, event | category | flops | bytes accessed | tf_op | source)
XLA Modules:
  0.0 814.3 jit_solution(18338085551955473135)
XLA Ops:
  13.6 9.7 %collective-permute-done.2.refs_7_ = bf16[128,1664]{1,0:T(8,128)(2,1)S(1)} collective-permute-done((bf16[128,1664]{1,0:T(8,128)(2,1)}, bf16[128,1664]{1,0:T(8,128)(2,1)S(1)}, u32[]{:S(2)}, u32[]{:S(2)}) %collective-permute-start.2) | collective-permute-done | bytes 426016 | tf_op jit(solution)/shard_map/ppermute | solution.py:43
  90.1 13.3 %shard_map.205 = (bf16[512,1024]{1,0:T(8,128)(2,1)}, bf16[512,512]{1,0:T(8,128)(2,1)}, bf16[512,2048]{1,0:T(8,128)(2,1)}, f32[8,2048]{1,0:T(8,128)}, bf16[2048,1664]{1,0:T(8,128)(2,1)}) custom-call(s32[1]{0:T(128)} %bitcast.1.core_ref.refs_0_, s32[16]{0:T(128)} %mul.185.refs_1_.starts, bf16[256,2048]{1,0:T(8,128)(2,1)} %bitcast.81, ...), custom_call_target="tpu_custom_call" | custom-call | flops 3489660928 | bytes 17825792 | tf_op jit(solution)/shard_map/pallas_call | solution.py:265
  108.8 9.7 %collective-permute-done.17.refs_1_ = bf16[512,512]{1,0:T(8,128)(2,1)S(1)} collective-permute-done((bf16[512,512]{1,0:T(8,128)(2,1)}, bf16[512,512]{1,0:T(8,128)(2,1)S(1)}, u32[]{:S(2)}, u32[]{:S(2)}) %collective-permute-start.17) | collective-permute-done | bytes 524320 | tf_op jit(solution)/shard_map/ppermute | solution.py:43
  137.6 10.2 %collective-permute-done.24.refs_1_ = bf16[512,1024]{1,0:T(8,128)(2,1)} collective-permute-done((bf16[512,1024]{1,0:T(8,128)(2,1)}, bf16[512,1024]{1,0:T(8,128)(2,1)}, u32[]{:S(2)}, u32[]{:S(2)}) %collective-permute-start.24) | collective-permute-done | bytes 1048608 | tf_op jit(solution)/shard_map/ppermute | solution.py:32
  152.2 26.1 %shard_map.206 = (bf16[512,1024]{1,0:T(8,128)(2,1)}, f32[32,256]{1,0:T(8,128)}) custom-call(s32[2]{0:T(128)} %bitcast.106, s32[1024,1]{1,0:T(8,128)} %bitcast.89, s32[1,256]{1,0:T(1,128)} %iota_add_fusion.qpos_ref, bf16[512,1024]{1,0:T(8,128)(2,1)} %get-tuple-element.116.q_ref, bf16[512,512]{1,0:T(8,128)(2,1)} %get-tuple-element.117.refs_0_, ...), custom_call_target="tpu_custom_call" | custom-call | flops 8589934592 | bytes 4194304 | tf_op jit(solution)/shard_map/pallas_call | solution.py:346
  184.5 8.2 %shard_map.207 = (f32[256,1024]{1,0:T(8,128)}, f32[256,1024]{1,0:T(8,128)}, bf16[2048,1024]{1,0:T(8,128)(2,1)}) custom-call(s32[1]{0:T(128)} %bitcast.1.core_ref.refs_0_, s32[16]{0:T(128)} %and_select_fusion.starts, bf16[512,1024]{1,0:T(8,128)(2,1)} %get-tuple-element.118.o_mine.refs_0_, bf16[512,1024]{1,0:T(8,128)(2,1)} %collective-permute-done.20.o_other.refs_1_, ...), custom_call_target="tpu_custom_call" | custom-call | flops 2147483648 | bytes 14680064 | tf_op jit(solution)/shard_map/pallas_call | solution.py:510
  194.9 9.8 %collective-permute-done.47.refs_2_ = bf16[256,2048]{1,0:T(8,128)(2,1)} collective-permute-done((bf16[256,2048]{1,0:T(8,128)(2,1)}, bf16[256,2048]{1,0:T(8,128)(2,1)}, u32[]{:S(2)}, u32[]{:S(2)}) %collective-permute-start.47) | collective-permute-done | bytes 1048608 | tf_op jit(solution)/shard_map/ppermute | solution.py:43
  220.3 10.6 %collective-permute-done.34.refs_7_.refs_3_ = bf16[512,1024]{1,0:T(8,128)(2,1)S(1)} collective-permute-done((bf16[512,1024]{1,0:T(8,128)(2,1)}, bf16[512,1024]{1,0:T(8,128)(2,1)S(1)}, u32[]{:S(2)}, u32[]{:S(2)}) %collective-permute-start.34) | collective-permute-done | bytes 1048608 | tf_op jit(solution)/shard_map/ppermute | solution.py:32
  236.6 19.7 %collective-permute-done.37.refs_11_.refs_7_ = bf16[512,1024]{1,0:T(8,128)(2,1)} collective-permute-done((bf16[512,1024]{1,0:T(8,128)(2,1)S(1)}, bf16[512,1024]{1,0:T(8,128)(2,1)}, u32[]{:S(2)}, u32[]{:S(2)}) %collective-permute-start.37) | collective-permute-done | bytes 1048608 | tf_op jit(solution)/shard_map/ppermute | solution.py:32
  257.3 17.4 %collective-permute-done.40.refs_15_.refs_11_ = bf16[1024,512]{1,0:T(8,128)(2,1)} collective-permute-done((bf16[1024,512]{1,0:T(8,128)(2,1)S(1)}, bf16[1024,512]{1,0:T(8,128)(2,1)}, u32[]{:S(2)}, u32[]{:S(2)}) %collective-permute-start.40) | collective-permute-done | bytes 1048608 | tf_op jit(solution)/shard_map/ppermute | solution.py:32
  278.2 12.9 %shard_map.208 = (bf16[2048,512]{1,0:T(8,128)(2,1)}, bf16[2048,512]{1,0:T(8,128)(2,1)}, bf16[2048,512]{1,0:T(8,128)(2,1)}, bf16[2048,512]{1,0:T(8,128)(2,1)}, bf...) custom-call(bf16[256,2048]{1,0:T(8,128)(2,1)} %maximum_select_fusion, ...), custom_call_target="tpu_custom_call" | custom-call | flops 6442450944 | bytes 25165824 | tf_op jit(solution)/shard_map/pallas_call | solution.py:568
  291.0 12.6 %shard_map.215 = (bf16[256,2048]{1,0:T(8,128)(2,1)}, bf16[256,2048]{1,0:T(8,128)(2,1)}, bf16[256,2048]{1,0:T(8,128)(2,1)}, bf16[256,2048]{1,0:T(8,128)(2,1)}) custom-call(bf16[2048,1024]{1,0:T(8,128)(2,1)} %get-tuple-element.137.refs_24_.hidden, bf16[2048,1024]{1,0:T(8,128)(2,1)} %get-tuple-element.138.refs_25_.d_gate, ...), custom_call_target="tpu_custom_call" | custom-call | flops 6442450944 | bytes 19922944 | tf_op jit(solution)/shard_map/pallas_call | solution.py:615
  305.3 13.3 %shard_map.209 = (bf16[2048,512]{1,0:T(8,128)(2,1)}, bf16[2048,512]{1,0:T(8,128)(2,1)}, bf16[2048,512]{1,0:T(8,128)(2,1)}, bf16[2048,512]{1,0:T(8,128)(2,1)}, bf...) custom-call(bf16[256,2048]{1,0:T(8,128)(2,1)} %collective-permute-do, ...), custom_call_target="tpu_custom_call", output_to_operand_aliasing={{0}: (16, {}), {1}: (17, {}), {2}: (18, {}), {3}: (19, {}),... | custom-call | flops 6442450944 | bytes 25165824 | tf_op jit(solution)/shard_map/pallas_call | solution.py:568
  318.6 12.6 %shard_map.210 = (bf16[256,2048]{1,0:T(8,128)(2,1)}, bf16[256,2048]{1,0:T(8,128)(2,1)}, bf16[256,2048]{1,0:T(8,128)(2,1)}, bf16[256,2048]{1,0:T(8,128)(2,1)}) custom-call(bf16[2048,1024]{1,0:T(8,128)(2,1)} %get-tuple-element.140.hidden.refs_24_, bf16[2048,1024]{1,0:T(8,128)(2,1)} %get-tuple-element.141.d_gate.refs_25_, ...), custom_call_target="tpu_custom_call" | custom-call | flops 6442450944 | bytes 19922944 | tf_op jit(solution)/shard_map/pallas_call | solution.py:615
  332.7 13.5 %shard_map.211 = (bf16[2048,512]{1,0:T(8,128)(2,1)}, bf16[2048,512]{1,0:T(8,128)(2,1)}, bf16[2048,512]{1,0:T(8,128)(2,1)}, bf16[2048,512]{1,0:T(8,128)(2,1)}, bf...) custom-call(bf16[256,2048]{1,0:T(8,128)(2,1)} %copy-done.39, ...), custom_call_target="tpu_custom_call", output_to_operand_aliasing={{0}: (16, {}), {1}: (17, {}), {2}: (18, {}), {3}: (19, {}),... | custom-call | flops 6442450944 | bytes 25165824 | tf_op jit(solution)/shard_map/pallas_call | solution.py:568
  346.2 12.6 %shard_map.212 = (bf16[256,2048]{1,0:T(8,128)(2,1)}, bf16[256,2048]{1,0:T(8,128)(2,1)}, bf16[256,2048]{1,0:T(8,128)(2,1)}, bf16[256,2048]{1,0:T(8,128)(2,1)}) custom-call(bf16[2048,1024]{1,0:T(8,128)(2,1)} %get-tuple-element.153.hidden.refs_24_, bf16[2048,1024]{1,0:T(8,128)(2,1)} %get-tuple-element.154.d_gate.refs_25_, ...), custom_call_target="tpu_custom_call" | custom-call | flops 6442450944 | bytes 19922944 | tf_op jit(solution)/shard_map/pallas_call | solution.py:615
  364.0 13.5 %shard_map.213 = (bf16[2048,512]{1,0:T(8,128)(2,1)}, bf16[2048,512]{1,0:T(8,128)(2,1)}, bf16[2048,512]{1,0:T(8,128)(2,1)}, bf16[2048,512]{1,0:T(8,128)(2,1)}, bf...) custom-call(bf16[256,2048]{1,0:T(8,128)(2,1)} %copy-done.41, ...), custom_call_target="tpu_custom_call", output_to_operand_aliasing={{0}: (16, {}), {1}: (17, {}), {2}: (18, {}), {3}: (19, {}),... | custom-call | flops 6442450944 | bytes 25165824 | tf_op jit(solution)/shard_map/pallas_call | solution.py:568
  400.6 13.9 %shard_map.214 = (bf16[256,2048]{1,0:T(8,128)(2,1)}, bf16[256,2048]{1,0:T(8,128)(2,1)}, bf16[256,2048]{1,0:T(8,128)(2,1)}, bf16[256,2048]{1,0:T(8,128)(2,1)}) custom-call(bf16[2048,1024]{1,0:T(8,128)(2,1)} %get-tuple-element.166.hidden, bf16[2048,1024]{1,0:T(8,128)(2,1)} %get-tuple-element.167.d_gate, bf16[2048,1024]{1,0:T(8,128)(2,1)} %get-tuple-element.168.d_up, ...), custom_call_target="tpu_custom_call" | custom-call | flops 6442450944 | bytes 19922944 | tf_op jit(solution)/shard_map/pallas_call | solution.py:615
  426.4 16.6 %collective-permute-done.44 = bf16[256,2048]{1,0:T(8,128)(2,1)S(1)} collective-permute-done((bf16[256,2048]{1,0:T(8,128)(2,1)S(1)}, bf16[256,2048]{1,0:T(8,128)(2,1)S(1)}, u32[]{:S(2)}, u32[]{:S(2)}) %collective-permute-start.44) | collective-permute-done | bytes 1048608 | tf_op jit(solution)/shard_map/ppermute | solution.py:43
  449.9 15.5 %collective-permute-done.61 = bf16[256,2048]{1,0:T(8,128)(2,1)S(1)} collective-permute-done((bf16[256,2048]{1,0:T(8,128)(2,1)S(1)}, bf16[256,2048]{1,0:T(8,128)(2,1)S(1)}, u32[]{:S(2)}, u32[]{:S(2)}) %collective-permute-start.61) | collective-permute-done | bytes 1048608 | tf_op jit(solution)/shard_map/ppermute | solution.py:43
  472.2 15.8 %collective-permute-done.50 = bf16[256,2048]{1,0:T(8,128)(2,1)S(1)} collective-permute-done((bf16[256,2048]{1,0:T(8,128)(2,1)S(1)}, bf16[256,2048]{1,0:T(8,128)(2,1)S(1)}, u32[]{:S(2)}, u32[]{:S(2)}) %collective-permute-start.50) | collective-permute-done | bytes 1048608 | tf_op jit(solution)/shard_map/ppermute | solution.py:43
  491.8 18.1 %collective-permute-done.63 = bf16[256,2048]{1,0:T(8,128)(2,1)S(1)} collective-permute-done((bf16[256,2048]{1,0:T(8,128)(2,1)S(1)}, bf16[256,2048]{1,0:T(8,128)(2,1)S(1)}, u32[]{:S(2)}, u32[]{:S(2)}) %collective-permute-start.63) | collective-permute-done | bytes 1048608 | tf_op jit(solution)/shard_map/ppermute | solution.py:43
  517.5 17.8 %collective-permute-done.56 = bf16[256,2048]{1,0:T(8,128)(2,1)S(1)} collective-permute-done((bf16[256,2048]{1,0:T(8,128)(2,1)S(1)}, bf16[256,2048]{1,0:T(8,128)(2,1)S(1)}, u32[]{:S(2)}, u32[]{:S(2)}) %collective-permute-start.56) | collective-permute-done | bytes 1048608 | tf_op jit(solution)/shard_map/ppermute | solution.py:43
  547.3 9.0 %shard_map.216 = (f32[512,1024]{1,0:T(8,128)}, bf16[512,1024]{1,0:T(8,128)(2,1)}, bf16[512,1024]{1,0:T(8,128)(2,1)}) custom-call(s32[1]{0:T(128)} %bitcast.1.core_ref.refs_0_, bf16[256,1024]{1,0:T(8,128)(2,1)} %get-tuple-element.275.d_own, bf16[256,1024]{1,0:T(8,128)(2,1)} %copy-done.74, bf16[2048,1024]{1,0:T(8,128)(2,1)} %get-tuple-element.181.w_ref), custom_call_target="tpu_custom_call" | custom-call | flops 2147483648 | bytes 10485760 | tf_op jit(solution)/shard_map/pallas_call | solution.py:662
  570.5 34.9 %shard_map.217 = (bf16[512,1024]{1,0:T(8,128)(2,1)}, bf16[512,512]{1,0:T(8,128)(2,1)}, bf16[512,512]{1,0:T(8,128)(2,1)}, bf16[512,512]{1,0:T(8,128)(2,1)}, bf16[512,512]{1,0:T(8,128)(2,1)}) custom-call(s32[2]{0:T(128)} %bitcast.107, s32[1024,1]{1,0:T(8,128)} %bitcast.90, s32[1,256]{1,0:T(1,128)} %iota_add_fusion.qpos_ref, ...), custom_call_target="tpu_custom_call" | custom-call | flops 21474836480 | bytes 9437184 | tf_op jit(solution)/shard_map/pallas_call | solution.py:425
  609.6 10.8 %collective-permute-done.67 = bf16[512,512]{1,0:T(8,128)(2,1)} collective-permute-done((bf16[512,512]{1,0:T(8,128)(2,1)}, bf16[512,512]{1,0:T(8,128)(2,1)}, u32[]{:S(2)}, u32[]{:S(2)}) %collective-permute-start.67) | collective-permute-done | bytes 524320 | tf_op jit(solution)/shard_map/ppermute | solution.py:43
  637.8 8.8 %collective-permute-done.103 = bf16[512,1024]{1,0:T(8,128)(2,1)S(1)} collective-permute-done((bf16[512,1024]{1,0:T(8,128)(2,1)S(1)}, bf16[512,1024]{1,0:T(8,128)(2,1)S(1)}, u32[]{:S(2)}, u32[]{:S(2)}) %collective-permute-start.103) | collective-permute-done | bytes 1048608 | tf_op jit(solution)/shard_map/ppermute | solution.py:32
  650.6 18.4 %collective-permute-done.78 = bf16[512,1024]{1,0:T(8,128)(2,1)S(1)} collective-permute-done((bf16[512,1024]{1,0:T(8,128)(2,1)}, bf16[512,1024]{1,0:T(8,128)(2,1)S(1)}, u32[]{:S(2)}, u32[]{:S(2)}) %collective-permute-start.78) | collective-permute-done | bytes 1048608 | tf_op jit(solution)/shard_map/ppermute | solution.py:32
  671.5 20.0 %collective-permute-done.93 = bf16[512,1024]{1,0:T(8,128)(2,1)S(1)} collective-permute-done((bf16[512,1024]{1,0:T(8,128)(2,1)S(1)}, bf16[512,1024]{1,0:T(8,128)(2,1)S(1)}, u32[]{:S(2)}, u32[]{:S(2)}) %collective-permute-start.93) | collective-permute-done | bytes 1048608 | tf_op jit(solution)/shard_map/ppermute | solution.py:32
  692.6 21.3 %collective-permute-done.104 = bf16[1024,512]{1,0:T(8,128)(2,1)S(1)} collective-permute-done((bf16[1024,512]{1,0:T(8,128)(2,1)S(1)}, bf16[1024,512]{1,0:T(8,128)(2,1)S(1)}, u32[]{:S(2)}, u32[]{:S(2)}) %collective-permute-start.104) | collective-permute-done | bytes 1048608 | tf_op jit(solution)/shard_map/ppermute | solution.py:32
  727.3 8.1 shard_map.219
  757.2 8.3 %collective-permute-done.84 = bf16[512,512]{1,0:T(8,128)(2,1)S(1)} collective-permute-done((bf16[512,512]{1,0:T(8,128)(2,1)}, bf16[512,512]{1,0:T(8,128)(2,1)S(1)}, u32[]{:S(2)}, u32[]{:S(2)}) %collective-permute-start.84) | collective-permute-done | bytes 524320 | tf_op jit(solution)/shard_map/ppermute | solution.py:32
  (479 shorter events, 349.1 us)
Async XLA Ops:
  53.3 35.3 %collective-permute-start.14 = (bf16[128,1664]{1,0:T(8,128)(2,1)}, bf16[128,1664]{1,0:T(8,128)(2,1)}, u32[]{:S(2)}, u32[]{:S(2)}) collective-permute-start(bf16[128,1664]{1,0:T(8,128)(2,1)} %collective-permute-done.10.refs_15_), channel_id=1, source_target_pairs={{0,8},{8,0},{16,24},{24,16},{1,9},{9,1},{17,25},{25,17},{2,10},{10... | collective-permute-start | bytes 1277960 | tf_op jit(solution)/shard_map/ppermute | solution.py:32
  136.6 42.2 %collective-permute-start.30 = (bf16[256,2048]{1,0:T(8,128)(2,1)}, bf16[256,2048]{1,0:T(8,128)(2,1)}, u32[]{:S(2)}, u32[]{:S(2)}) collective-permute-start(bf16[256,2048]{1,0:T(8,128)(2,1)} %maximum_select_fusion.9.refs_2_), channel_id=1, source_target_pairs={{0,4},{1,5},{4,6},{5,7},{6,2},{7,3},{2,0},{3,1},{8,12},{9,13},{12,... | collective-permute-start | bytes 3145736 | tf_op jit(solution)/shard_map/ppermute | solution.py:43
  211.0 45.3 %collective-permute-start.37 = (bf16[512,1024]{1,0:T(8,128)(2,1)S(1)}, bf16[512,1024]{1,0:T(8,128)(2,1)}, u32[]{:S(2)}, u32[]{:S(2)}) collective-permute-start(bf16[512,1024]{1,0:T(8,128)(2,1)S(1)} %collective-permute-done.35.refs_9_.refs_5_), channel_id=1, source_target_pairs={{0,16},{8,24},{16,0},{24,8},{1,17},{9,25},{17,1},{25,9},{2,18},{10... | collective-permute-start | bytes 3145736 | tf_op jit(solution)/shard_map/ppermute | solution.py:32
  220.3 36.0 %collective-permute-start.38 = (bf16[1024,512]{1,0:T(8,128)(2,1)S(1)}, bf16[1024,512]{1,0:T(8,128)(2,1)}, u32[]{:S(2)}, u32[]{:S(2)}) collective-permute-start(bf16[1024,512]{1,0:T(8,128)(2,1)S(1)} %copy-done.7), channel_id=1, source_target_pairs={{0,8},{8,0},{16,24},{24,16},{1,9},{9,1},{17,25},{25,17},{2,10},{10... | collective-permute-start | bytes 3145736 | tf_op jit(solution)/shard_map/ppermute | solution.py:32
  235.6 39.1 %collective-permute-start.40 = (bf16[1024,512]{1,0:T(8,128)(2,1)S(1)}, bf16[1024,512]{1,0:T(8,128)(2,1)}, u32[]{:S(2)}, u32[]{:S(2)}) collective-permute-start(bf16[1024,512]{1,0:T(8,128)(2,1)S(1)} %collective-permute-done.39.refs_14_.refs_10_), channel_id=1, source_target_pairs={{0,8},{8,0},{16,24},{24,16},{1,9},{9,1},{17,25},{25,17},{2,10},{10... | collective-permute-start | bytes 3145736 | tf_op jit(solution)/shard_map/ppermute | solution.py:32
  256.3 47.3 %collective-permute-start.31 = (bf16[256,2048]{1,0:T(8,128)(2,1)}, bf16[256,2048]{1,0:T(8,128)(2,1)S(1)}, u32[]{:S(2)}, u32[]{:S(2)}) collective-permute-start(bf16[256,2048]{1,0:T(8,128)(2,1)} %collective-permute-done.30.refs_2_), channel_id=1, source_target_pairs={{0,1},{1,0},{2,3},{3,2},{4,5},{5,4},{6,7},{7,6},{8,9},{9,8},{10,11... | collective-permute-start | bytes 3145736 | tf_op jit(solution)/shard_map/ppermute | solution.py:27
  256.3 75.0 %collective-permute-start.48 = (bf16[256,2048]{1,0:T(8,128)(2,1)}, bf16[256,2048]{1,0:T(8,128)(2,1)S(1)}, u32[]{:S(2)}, u32[]{:S(2)}) collective-permute-start(bf16[256,2048]{1,0:T(8,128)(2,1)} %collective-permute-done.47.refs_2_), channel_id=1, source_target_pairs={{0,1},{1,0},{2,3},{3,2},{4,5},{5,4},{6,7},{7,6},{8,9},{9,8},{10,11... | collective-permute-start | bytes 3145736 | tf_op jit(solution)/shard_map/ppermute | solution.py:27
  256.8 105.7 %collective-permute-start.54 = (bf16[256,2048]{1,0:T(8,128)(2,1)}, bf16[256,2048]{1,0:T(8,128)(2,1)S(1)}, u32[]{:S(2)}, u32[]{:S(2)}) collective-permute-start(bf16[256,2048]{1,0:T(8,128)(2,1)} %copy-done.28), channel_id=1, source_target_pairs={{0,1},{1,0},{2,3},{3,2},{4,5},{5,4},{6,7},{7,6},{8,9},{9,8},{10,11... | collective-permute-start | bytes 3145736 | tf_op jit(solution)/shard_map/ppermute | solution.py:27
  257.1 47.1 %collective-permute-start.29 = (bf16[256,2048]{1,0:T(8,128)(2,1)}, bf16[256,2048]{1,0:T(8,128)(2,1)S(1)}, u32[]{:S(2)}, u32[]{:S(2)}) collective-permute-start(bf16[256,2048]{1,0:T(8,128)(2,1)} %collective-permute-done.28.refs_0_), channel_id=1, source_target_pairs={{0,1},{1,0},{2,3},{3,2},{4,5},{5,4},{6,7},{7,6},{8,9},{9,8},{10,11... | collective-permute-start | bytes 3145736 | tf_op jit(solution)/shard_map/ppermute | solution.py:27
  303.6 186.6 %collective-permute-start.64 = (bf16[256,2048]{1,0:T(8,128)(2,1)}, bf16[256,2048]{1,0:T(8,128)(2,1)}, u32[]{:S(2)}, u32[]{:S(2)}) collective-permute-start(bf16[256,2048]{1,0:T(8,128)(2,1)} %get-tuple-element.180), channel_id=1, source_target_pairs={{0,1},{1,0},{2,3},{3,2},{4,5},{5,4},{6,7},{7,6},{8,9},{9,8},{10,11... | collective-permute-start | bytes 3145736 | tf_op jit(solution)/shard_map/ppermute | solution.py:27
  358.8 157.1 %collective-permute-start.57 = (bf16[256,2048]{1,0:T(8,128)(2,1)}, bf16[256,2048]{1,0:T(8,128)(2,1)}, u32[]{:S(2)}, u32[]{:S(2)}) collective-permute-start(bf16[256,2048]{1,0:T(8,128)(2,1)} %get-tuple-element.172), channel_id=1, source_target_pairs={{0,1},{1,0},{2,3},{3,2},{4,5},{5,4},{6,7},{7,6},{8,9},{9,8},{10,11... | collective-permute-start | bytes 3145736 | tf_op jit(solution)/shard_map/ppermute | solution.py:27
  360.8 56.2 %collective-permute-start.60 = (bf16[256,2048]{1,0:T(8,128)(2,1)}, bf16[256,2048]{1,0:T(8,128)(2,1)}, u32[]{:S(2)}, u32[]{:S(2)}) collective-permute-start(bf16[256,2048]{1,0:T(8,128)(2,1)} %get-tuple-element.176), channel_id=1, source_target_pairs={{0,1},{1,0},{2,3},{3,2},{4,5},{5,4},{6,7},{7,6},{8,9},{9,8},{10,11... | collective-permute-start | bytes 3145736 | tf_op jit(solution)/shard_map/ppermute | solution.py:27
  362.5 54.7 %collective-permute-start.59 = (bf16[256,2048]{1,0:T(8,128)(2,1)}, bf16[256,2048]{1,0:T(8,128)(2,1)}, u32[]{:S(2)}, u32[]{:S(2)}) collective-permute-start(bf16[256,2048]{1,0:T(8,128)(2,1)} %add_convert_fusion.7), channel_id=1, source_target_pairs={{0,4},{1,5},{4,6},{5,7},{6,2},{7,3},{2,0},{3,1},{8,12},{9,13},{12,... | collective-permute-start | bytes 3145736 | tf_op jit(solution)/shard_map/ppermute | solution.py:43
  363.0 60.5 %collective-permute-start.49 = (bf16[256,2048]{1,0:T(8,128)(2,1)}, bf16[256,2048]{1,0:T(8,128)(2,1)}, u32[]{:S(2)}, u32[]{:S(2)}) collective-permute-start(bf16[256,2048]{1,0:T(8,128)(2,1)} %get-tuple-element.157), channel_id=1, source_target_pairs={{0,1},{1,0},{2,3},{3,2},{4,5},{5,4},{6,7},{7,6},{8,9},{9,8},{10,11... | collective-permute-start | bytes 3145736 | tf_op jit(solution)/shard_map/ppermute | solution.py:27
  423.6 41.9 %collective-permute-start.61 = (bf16[256,2048]{1,0:T(8,128)(2,1)S(1)}, bf16[256,2048]{1,0:T(8,128)(2,1)S(1)}, u32[]{:S(2)}, u32[]{:S(2)}) collective-permute-start(bf16[256,2048]{1,0:T(8,128)(2,1)S(1)} %add_convert_fusion.6), channel_id=1, source_target_pairs={{0,4},{1,5},{4,6},{5,7},{6,2},{7,3},{2,0},{3,1},{8,12},{9,13},{12,... | collective-permute-start | bytes 3145736 | tf_op jit(solution)/shard_map/ppermute | solution.py:43
  448.8 39.1 %collective-permute-start.50 = (bf16[256,2048]{1,0:T(8,128)(2,1)S(1)}, bf16[256,2048]{1,0:T(8,128)(2,1)S(1)}, u32[]{:S(2)}, u32[]{:S(2)}) collective-permute-start(bf16[256,2048]{1,0:T(8,128)(2,1)S(1)} %add_convert_fusion.9), channel_id=1, source_target_pairs={{0,4},{1,5},{4,6},{5,7},{6,2},{7,3},{2,0},{3,1},{8,12},{9,13},{12,... | collective-permute-start | bytes 3145736 | tf_op jit(solution)/shard_map/ppermute | solution.py:43
  466.0 43.9 %collective-permute-start.63 = (bf16[256,2048]{1,0:T(8,128)(2,1)S(1)}, bf16[256,2048]{1,0:T(8,128)(2,1)S(1)}, u32[]{:S(2)}, u32[]{:S(2)}) collective-permute-start(bf16[256,2048]{1,0:T(8,128)(2,1)S(1)} %add_convert_fusion.5), channel_id=1, source_target_pairs={{0,4},{1,5},{4,6},{5,7},{6,2},{7,3},{2,0},{3,1},{8,12},{9,13},{12,... | collective-permute-start | bytes 3145736 | tf_op jit(solution)/shard_map/ppermute | solution.py:43
  470.5 89.2 %collective-permute-start.99 = (bf16[512,1024]{1,0:T(8,128)(2,1)}, bf16[512,1024]{1,0:T(8,128)(2,1)}, u32[]{:S(2)}, u32[]{:S(2)}) collective-permute-start(bf16[512,1024]{1,0:T(8,128)(2,1)} %convolution_convert_fusion.8), channel_id=1, source_target_pairs={{0,8},{8,0},{16,24},{24,16},{1,9},{9,1},{17,25},{25,17},{2,10},{10... | collective-permute-start | bytes 3145736 | tf_op jit(solution)/shard_map/ppermute | solution.py:32
  487.9 140.0 %collective-permute-start.98 = (bf16[512,1024]{1,0:T(8,128)(2,1)}, bf16[512,1024]{1,0:T(8,128)(2,1)}, u32[]{:S(2)}, u32[]{:S(2)}) collective-permute-start(bf16[512,1024]{1,0:T(8,128)(2,1)} %convolution_convert_fusion.10), channel_id=1, source_target_pairs={{0,8},{8,0},{16,24},{24,16},{1,9},{9,1},{17,25},{25,17},{2,10},{10... | collective-permute-start | bytes 3145736 | tf_op jit(solution)/shard_map/ppermute | solution.py:32
  490.2 115.2 %collective-permute-start.102 = (bf16[512,1024]{1,0:T(8,128)(2,1)}, bf16[512,1024]{1,0:T(8,128)(2,1)}, u32[]{:S(2)}, u32[]{:S(2)}) collective-permute-start(bf16[512,1024]{1,0:T(8,128)(2,1)} %convolution_convert_fusion.4), channel_id=1, source_target_pairs={{0,16},{8,24},{16,0},{24,8},{1,17},{9,25},{17,1},{25,9},{2,18},{10... | collective-permute-start | bytes 3145736 | tf_op jit(solution)/shard_map/ppermute | solution.py:32
  515.9 116.1 %collective-permute-start.101 = (bf16[512,1024]{1,0:T(8,128)(2,1)}, bf16[512,1024]{1,0:T(8,128)(2,1)}, u32[]{:S(2)}, u32[]{:S(2)}) collective-permute-start(bf16[512,1024]{1,0:T(8,128)(2,1)} %convolution_convert_fusion.6), channel_id=1, source_target_pairs={{0,16},{8,24},{16,0},{24,8},{1,17},{9,25},{17,1},{25,9},{2,18},{10... | collective-permute-start | bytes 3145736 | tf_op jit(solution)/shard_map/ppermute | solution.py:32
  559.8 49.0 %collective-permute-start.105 = (bf16[1024,512]{1,0:T(8,128)(2,1)}, bf16[1024,512]{1,0:T(8,128)(2,1)S(1)}, u32[]{:S(2)}, u32[]{:S(2)}) collective-permute-start(bf16[1024,512]{1,0:T(8,128)(2,1)} %convolution_convert_fusion), channel_id=1, source_target_pairs={{0,8},{8,0},{16,24},{24,16},{1,9},{9,1},{17,25},{25,17},{2,10},{10... | collective-permute-start | bytes 3145736 | tf_op jit(solution)/shard_map/ppermute | solution.py:32
  569.0 60.8 %collective-permute-start.92 = (bf16[512,1024]{1,0:T(8,128)(2,1)}, bf16[512,1024]{1,0:T(8,128)(2,1)S(1)}, u32[]{:S(2)}, u32[]{:S(2)}) collective-permute-start(bf16[512,1024]{1,0:T(8,128)(2,1)} %get-tuple-element.206), channel_id=1, source_target_pairs={{0,16},{8,24},{16,0},{24,8},{1,17},{9,25},{17,1},{25,9},{2,18},{10... | collective-permute-start | bytes 3145736 | tf_op jit(solution)/shard_map/ppermute | solution.py:32
  627.9 41.1 %collective-permute-start.78 = (bf16[512,1024]{1,0:T(8,128)(2,1)}, bf16[512,1024]{1,0:T(8,128)(2,1)S(1)}, u32[]{:S(2)}, u32[]{:S(2)}) collective-permute-start(bf16[512,1024]{1,0:T(8,128)(2,1)} %get-tuple-element.197), channel_id=1, source_target_pairs={{0,8},{8,0},{16,24},{24,16},{1,9},{9,1},{17,25},{25,17},{2,10},{10... | collective-permute-start | bytes 3145736 | tf_op jit(solution)/shard_map/ppermute | solution.py:32
  632.1 37.7 %collective-permute-start.91 = (bf16[512,1024]{1,0:T(8,128)(2,1)S(1)}, bf16[512,1024]{1,0:T(8,128)(2,1)S(1)}, u32[]{:S(2)}, u32[]{:S(2)}) collective-permute-start(bf16[512,1024]{1,0:T(8,128)(2,1)S(1)} %copy-done.70), channel_id=1, source_target_pairs={{0,16},{8,24},{16,0},{24,8},{1,17},{9,25},{17,1},{25,9},{2,18},{10... | collective-permute-start | bytes 3145736 | tf_op jit(solution)/shard_map/ppermute | solution.py:32
  634.3 57.3 %collective-permute-start.93 = (bf16[512,1024]{1,0:T(8,128)(2,1)S(1)}, bf16[512,1024]{1,0:T(8,128)(2,1)S(1)}, u32[]{:S(2)}, u32[]{:S(2)}) collective-permute-start(bf16[512,1024]{1,0:T(8,128)(2,1)S(1)} %add_convert_fusion.3), channel_id=1, source_target_pairs={{0,8},{8,0},{16,24},{24,16},{1,9},{9,1},{17,25},{25,17},{2,10},{10... | collective-permute-start | bytes 3145736 | tf_op jit(solution)/shard_map/ppermute | solution.py:32
  646.6 67.4 %collective-permute-start.104 = (bf16[1024,512]{1,0:T(8,128)(2,1)S(1)}, bf16[1024,512]{1,0:T(8,128)(2,1)S(1)}, u32[]{:S(2)}, u32[]{:S(2)}) collective-permute-start(bf16[1024,512]{1,0:T(8,128)(2,1)S(1)} %copy-done.68), channel_id=1, source_target_pairs={{0,8},{8,0},{16,24},{24,16},{1,9},{9,1},{17,25},{25,17},{2,10},{10... | collective-permute-start | bytes 3145736 | tf_op jit(solution)/shard_map/ppermute | solution.py:32
  646.9 68.8 %collective-permute-start.106 = (bf16[1024,512]{1,0:T(8,128)(2,1)S(1)}, bf16[1024,512]{1,0:T(8,128)(2,1)S(1)}, u32[]{:S(2)}, u32[]{:S(2)}) collective-permute-start(bf16[1024,512]{1,0:T(8,128)(2,1)S(1)} %add_convert_fusion), channel_id=1, source_target_pairs={{0,16},{8,24},{16,0},{24,8},{1,17},{9,25},{17,1},{25,9},{2,18},{10... | collective-permute-start | bytes 3145736 | tf_op jit(solution)/shard_map/ppermute | solution.py:32
  669.0 72.9 %collective-permute-start.77 = (bf16[512,1024]{1,0:T(8,128)(2,1)}, bf16[512,1024]{1,0:T(8,128)(2,1)S(1)}, u32[]{:S(2)}, u32[]{:S(2)}) collective-permute-start(bf16[512,1024]{1,0:T(8,128)(2,1)} %get-tuple-element.195), channel_id=1, source_target_pairs={{0,8},{8,0},{16,24},{24,16},{1,9},{9,1},{17,25},{25,17},{2,10},{10... | collective-permute-start | bytes 3145736 | tf_op jit(solution)/shard_map/ppermute | solution.py:32
  669.7 54.3 %collective-permute-start.69 = (bf16[512,512]{1,0:T(8,128)(2,1)S(1)}, bf16[512,512]{1,0:T(8,128)(2,1)S(1)}, u32[]{:S(2)}, u32[]{:S(2)}) collective-permute-start(bf16[512,512]{1,0:T(8,128)(2,1)S(1)} %add_convert_fusion.12), channel_id=1, source_target_pairs={{0,4},{1,5},{4,6},{5,7},{6,2},{7,3},{2,0},{3,1},{8,12},{9,13},{12,... | collective-permute-start | bytes 1572872 | tf_op jit(solution)/shard_map/ppermute | solution.py:43
  691.5 51.0 %collective-permute-start.79 = (bf16[512,1024]{1,0:T(8,128)(2,1)S(1)}, bf16[512,1024]{1,0:T(8,128)(2,1)}, u32[]{:S(2)}, u32[]{:S(2)}) collective-permute-start(bf16[512,1024]{1,0:T(8,128)(2,1)S(1)} %add_convert_fusion.4), channel_id=1, source_target_pairs={{0,16},{8,24},{16,0},{24,8},{1,17},{9,25},{17,1},{25,9},{2,18},{10... | collective-permute-start | bytes 3145736 | tf_op jit(solution)/shard_map/ppermute | solution.py:32
  735.4 53.1 %collective-permute-start.70 = (f32[256,2048]{1,0:T(8,128)}, f32[256,2048]{1,0:T(8,128)S(1)}, u32[]{:S(2)}, u32[]{:S(2)}) collective-permute-start(f32[256,2048]{1,0:T(8,128)} %get-tuple-element.192), channel_id=1, source_target_pairs={{0,1},{1,0},{2,3},{3,2},{4,5},{5,4},{6,7},{7,6},{8,9},{9,8},{10,11... | collective-permute-start | bytes 6291464 | tf_op jit(solution)/shard_map/ppermute | solution.py:27
  (153 other events, 2439.3 us)

commit v3 on v2

--- a/solution.py
+++ b/solution.py
@@ -13,6 +13,7 @@
 EPSILON = 1e-05
 ROPE_BASE = 500000.0
 MASKED = -1e30
+WEIGHT = 6
 VMEM_LIMIT = 56 * 1024 * 1024
 F32 = jnp.float32
 BF16 = jnp.bfloat16
@@ -67,13 +68,15 @@
     return [pieces[r] for r in range(seq)]
 
 
-def cube_scatter(chunks, route):
+def cube_scatter(chunks, route, *waits):
     seq = lax.axis_size("seq")
     bits = [1 << i for i in range(seq.bit_length() - 1)]
     held = dict(enumerate(chunks))
     for bit in bits if route == 0 else bits[::-1]:
+        seen = waits if len(held) > 2 else ()
         held = {
-            r: held[r].astype(F32) + swap_seq(held[r ^ bit].astype(BF16), bit).astype(F32)
+            r: held[r].astype(F32)
+            + after(swap_seq(held[r ^ bit].astype(BF16), bit), *seen).astype(F32)
             for r in held
             if not r & bit
         }
@@ -121,7 +124,7 @@
 
 def cost(flops, nbytes, transcendentals=0):
     return pl.CostEstimate(
-        flops=int(flops), bytes_accessed=int(nbytes), transcendentals=int(transcendentals)
+        flops=int(WEIGHT * flops), bytes_accessed=int(nbytes), transcendentals=int(transcendentals)
     )
 
 
@@ -140,18 +143,16 @@
 def pack_kernel(kv_half, core_ref, wq, wk, wv, wo, gains, mine, other):
     def fill(out, which):
         at = 0
-        half = wq.shape[1] // 2
-        out[:, at : at + half] = wq[:, which * half : (which + 1) * half]
-        at += half
+        for source in (wo, wq):
+            half = source.shape[1] // 2
+            out[:, at : at + half] = source[:, which * half : (which + 1) * half]
+            at += half
         for i in range(kv_half // LANES):
             for source in (wk, wv):
                 lo = which * kv_half + i * LANES
                 out[:, at : at + LANES] = source[:, lo : lo + LANES]
                 at += LANES
         out[:, at : at + LANES] = gains[...]
-        at += LANES
-        half = wo.shape[1] // 2
-        out[:, at : at + half] = wo[:, which * half : (which + 1) * half]
 
     for core in range(2):
 
@@ -175,121 +176,126 @@
     )(core, wq, wk, wv, wo, gains)
 
 
-def stack_kernel(cut, core_ref, mine, other, left, right):
+def stack_kernel(edges, core_ref, mine, other, *outs):
     rows = mine.shape[0]
     for core in range(2):
 
         @pl.when(core_ref[0] == core)
         def _():
             for source, at in ((mine, core), (other, 1 - core)):
-                left[at * rows : (at + 1) * rows] = source[:, :cut]
-                right[at * rows : (at + 1) * rows] = source[:, cut:]
-
-
-def stack_pieces(core, mine, other, cut):
-    rows, width = mine.shape
-    return pl.pallas_call(
-        functools.partial(stack_kernel, cut),
+                for i, out in enumerate(outs):
+                    out[at * rows : (at + 1) * rows] = source[:, edges[i] : edges[i + 1]]
+
+
+def stack_pieces(core, mine, other, widths):
+    rows = mine.shape[0]
+    edges = [sum(widths[:i]) for i in range(len(widths) + 1)]
+    return pl.pallas_call(
+        functools.partial(stack_kernel, edges),
         in_specs=[SCALARS] + [pl.BlockSpec(memory_space=pltpu.VMEM)] * 2,
-        out_shape=[
-            jax.ShapeDtypeStruct((2 * rows, cut), BF16),
-            jax.ShapeDtypeStruct((2 * rows, width - cut), BF16),
-        ],
-        compiler_params=PARAMS,
-        cost_estimate=cost(0, 8 * rows * width),
+        out_shape=[jax.ShapeDtypeStruct((2 * rows, width), BF16) for width in widths],
+        compiler_params=PARAMS,
+        cost_estimate=cost(0, 8 * mine.size),
     )(core, mine, other)
 
 
-def qkv_kernel(count, batches, query_blocks, *refs):
+def placing(starts, pieces, w, sems):
+    return [
+        pltpu.make_async_copy(
+            piece, w.at[pl.ds(pl.multiple_of(starts[i], 16), piece.shape[0])], sems.at[i]
+        )
+        for i, piece in enumerate(pieces)
+    ]
+
+
+def kv_kernel(count, batches, *refs):
     core_ref, starts, x_own, x_oth, cos_ref, sin_ref = refs[:6]
     pieces = refs[6 : 6 + count]
-    q_ref, kv_ref, normed, gains_ref, w_out, w, sems, out_sem = refs[6 + count :]
-    step = pl.program_id(0)
-    rows, depth = normed.shape
-    slots = rows // (2 * batches)
-
-    def arriving(i):
-        start = pl.multiple_of(starts[i], 16)
-        return pltpu.make_async_copy(
-            pieces[i], w.at[pl.ds(start, pieces[i].shape[0])], sems.at[i]
-        )
-
-    @pl.when(step == 0)
-    def _():
-        for i in range(count):
-            arriving(i).start()
-        for i in range(count):
-            arriving(i).wait()
-        pltpu.make_async_copy(w, w_out, out_sem.at[0]).start()
-        table = w[:, w.shape[1] - LANES :].astype(F32).T
-        gains_ref[...] = table[:8]
-        for source, which in ((x_own, core_ref[0]), (x_oth, 1 - core_ref[0])):
-            for b in range(batches):
-                x = source[b * slots : (b + 1) * slots].astype(F32)
-                inverse = lax.rsqrt(jnp.mean(x * x, axis=-1, keepdims=True) + EPSILON)
-                at = pl.multiple_of((2 * b + which) * slots, slots)
-                normed[pl.ds(at, slots)] = (x * inverse * table[:1]).astype(BF16)
-
+    kv_ref, normed, gains_ref, w_out, w, sems = refs[6 + count :]
+    first = w.shape[1] - LANES - kv_ref.shape[1]
+    slots = normed.shape[0] // (2 * batches)
+    arriving = placing(starts, pieces, w, sems)
+    for copy in arriving:
+        copy.start()
+    for copy in arriving:
+        copy.wait()
+    leaving = pltpu.make_async_copy(w, w_out, sems.at[count])
+    leaving.start()
+    table = w[:, w.shape[1] - LANES :].astype(F32).T
+    gains_ref[...] = table[:8]
+    for source, which in ((x_own, core_ref[0]), (x_oth, 1 - core_ref[0])):
+        for b in range(batches):
+            x = source[b * slots : (b + 1) * slots].astype(F32)
+            inverse = lax.rsqrt(jnp.mean(x * x, axis=-1, keepdims=True) + EPSILON)
+            at = pl.multiple_of((2 * b + which) * slots, slots)
+            normed[pl.ds(at, slots)] = (x * inverse * table[:1]).astype(BF16)
     block = 2 * LANES
-    at = pl.multiple_of(step * block, block)
-    raw = dot(normed[...], w[:, pl.ds(at, block)])
-    left = rotate_lanes(raw[:, :LANES], cos_ref[...], sin_ref[...])
-
-    @pl.when(step < query_blocks)
-    def _():
-        right = rotate_lanes(raw[:, LANES:], cos_ref[...], sin_ref[...])
-        scale = 1.0 / math.sqrt(HEAD_DIM)
-        q_ref[:, :LANES] = (left * scale).astype(BF16)
-        q_ref[:, LANES:] = (right * scale).astype(BF16)
-
-    @pl.when(step >= query_blocks)
-    def _():
-        kv_ref[:, :LANES] = left.astype(BF16)
-        kv_ref[:, LANES:] = raw[:, LANES:].astype(BF16)
-
-    @pl.when(step == pl.num_programs(0) - 1)
-    def _():
-        pltpu.make_async_copy(w, w_out, out_sem.at[0]).wait()
-
-
-def project_qkv(core, starts, x_own, x_oth, cosine, sine, pieces, batches, query_width, kv_width):
+    for at in range(0, kv_ref.shape[1], block):
+        raw = dot(normed[...], w[:, first + at : first + at + block])
+        turned = rotate_lanes(raw[:, :LANES], cos_ref[...], sin_ref[...])
+        kv_ref[:, at : at + LANES] = turned.astype(BF16)
+        kv_ref[:, at + LANES : at + block] = raw[:, LANES:].astype(BF16)
+    leaving.wait()
+
+
+def project_kv(core, starts, x_own, x_oth, cosine, sine, pieces, batches, kv_width):
     rows, depth = 2 * x_own.shape[0], x_own.shape[1]
-    block = 2 * LANES
-    query_blocks = query_width // block
     width = pieces[0].shape[1]
     count = len(pieces)
-
-    def whole(shape):
-        return pl.BlockSpec(shape, lambda j: (0, 0))
-
-    return pl.pallas_call(
-        functools.partial(qkv_kernel, count, batches, query_blocks),
-        grid=((query_width + 2 * kv_width) // block,),
-        in_specs=[SCALARS, SCALARS, whole(x_own.shape), whole(x_own.shape)]
-        + [whole((rows, LANES))] * 2
-        + [ANYWHERE] * count,
-        out_specs=[
-            pl.BlockSpec((rows, block), lambda j: (0, jnp.minimum(j, query_blocks - 1))),
-            pl.BlockSpec((rows, block), lambda j: (0, jnp.maximum(j - query_blocks, 0))),
-            whole((rows, depth)),
-            whole((8, depth)),
-            ANYWHERE,
-        ],
+    vmem = pl.BlockSpec(memory_space=pltpu.VMEM)
+    return pl.pallas_call(
+        functools.partial(kv_kernel, count, batches),
+        in_specs=[SCALARS, SCALARS] + [vmem] * 4 + [ANYWHERE] * count,
+        out_specs=[vmem, vmem, vmem, ANYWHERE],
         out_shape=[
-            jax.ShapeDtypeStruct((rows, query_width), BF16),
-            jax.ShapeDtypeStruct((rows, 2 * kv_width), BF16),
+            jax.ShapeDtypeStruct((rows, kv_width), BF16),
             jax.ShapeDtypeStruct((rows, depth), BF16),
             jax.ShapeDtypeStruct((8, depth), F32),
             jax.ShapeDtypeStruct((depth, width), BF16),
         ],
         scratch_shapes=[
             pltpu.VMEM((depth, width), BF16),
-            pltpu.SemaphoreType.DMA((count,)),
-            pltpu.SemaphoreType.DMA((1,)),
+            pltpu.SemaphoreType.DMA((count + 1,)),
         ],
         compiler_params=PARAMS,
         cost_estimate=cost(2 * rows * depth * width, 4 * rows * depth + 4 * depth * width),
     )(core, starts, x_own, x_oth, cosine, sine, *pieces)
+
+
+def q_kernel(first, normed, cos_ref, sin_ref, w, q_ref, held, sems):
+    block = 2 * LANES
+    width = q_ref.shape[1]
+    copies = [
+        pltpu.make_async_copy(
+            w.at[:, pl.ds(first + at, block)], held.at[:, pl.ds(at, block)], sems.at[at // block]
+        )
+        for at in range(0, width, block)
+    ]
+    for copy in copies:
+        copy.start()
+    for at in range(0, width, block):
+        copies[at // block].wait()
+        raw = dot(normed[...], held[:, at : at + block])
+        for lo in range(0, block, LANES):
+            turned = rotate_lanes(raw[:, lo : lo + LANES], cos_ref[...], sin_ref[...])
+            q_ref[:, at + lo : at + lo + LANES] = (turned / math.sqrt(HEAD_DIM)).astype(BF16)
+
+
+def project_q(normed, cosine, sine, w, first, width):
+    rows, depth = normed.shape
+    vmem = pl.BlockSpec(memory_space=pltpu.VMEM)
+    return pl.pallas_call(
+        functools.partial(q_kernel, first),
+        in_specs=[vmem] * 3 + [ANYWHERE],
+        out_specs=vmem,
+        out_shape=jax.ShapeDtypeStruct((rows, width), BF16),
+        scratch_shapes=[
+            pltpu.VMEM((depth, width), BF16),
+            pltpu.SemaphoreType.DMA((width // (2 * LANES),)),
+        ],
+        compiler_params=PARAMS,
+        cost_estimate=cost(2 * rows * depth * width, 2 * rows * depth + 4 * depth * width),
+    )(normed, cosine, sine, w)
 
 
 def set_bias(limit_ref, kpos_ref, qpos_ref, bias):
@@ -469,80 +475,49 @@
             out[b * slots : (b + 1) * slots] = acc[pl.ds(at, slots)].astype(out.dtype)
 
 
-def out_kernel(batches, chips, core_ref, starts, o_mine, o_other, *refs):
-    count = len(refs) - 6
-    pieces = refs[:count]
-    own, other, w_out, w, acc, sems = refs[count:]
-    shard = pieces[0].shape[0] // chips
-    half = o_mine.shape[1]
-    arriving = [
+def out_kernel(batches, core_ref, o_mine, o_other, w_all, own, other, w, acc, sems):
+    half, width = o_mine.shape[1], w.shape[1]
+    block = 2 * LANES
+    copies = [
         pltpu.make_async_copy(
-            pieces[r].at[pl.ds(k * shard, shard)],
-            w.at[pl.ds(pl.multiple_of(starts[r * chips + k], 16), shard)],
-            sems.at[r * chips + k],
+            w_all.at[:, pl.ds(lo, block)], w.at[:, pl.ds(lo, block)], sems.at[lo // block]
         )
-        for r in range(count)
-        for k in range(chips)
+        for lo in range(0, width, block)
     ]
-    for copy in arriving:
+    for copy in copies:
         copy.start()
-    for copy in arriving:
-        copy.wait()
-    leaving = pltpu.make_async_copy(w, w_out, sems.at[count * chips])
-    leaving.start()
-    block = 2 * LANES
-
-    @pl.loop(0, w.shape[1] // block)
-    def _(j):
-        cut = pl.ds(pl.multiple_of(j * block, block), block)
-        acc[:, cut] = dot(o_mine[...], w[:half, cut]) + dot(o_other[...], w[half:, cut])
-
+    rows_mine = pl.ds(pl.multiple_of(core_ref[0] * half, half), half)
+    rows_other = pl.ds(pl.multiple_of((1 - core_ref[0]) * half, half), half)
+    for lo in range(0, width, block):
+        cut = slice(lo, lo + block)
+        copies[lo // block].wait()
+        acc[:, cut] = dot(o_mine[...], w[rows_mine, cut]) + dot(o_other[...], w[rows_other, cut])
     split_rows(batches, core_ref, acc, own, other)
-    leaving.wait()
-
-
-def project_out(core, starts, o_mine, o_other, pieces, batches, chips):
+
+
+def project_out(core, o_mine, o_other, w, width, batches):
     rows, half = o_mine.shape
-    width = pieces[0].shape[1]
-    count = len(pieces)
     vmem = pl.BlockSpec(memory_space=pltpu.VMEM)
     part = jax.ShapeDtypeStruct((rows // 2, width), F32)
     return pl.pallas_call(
-        functools.partial(out_kernel, batches, chips),
-        in_specs=[SCALARS, SCALARS, vmem, vmem] + [ANYWHERE] * count,
-        out_specs=[vmem, vmem, ANYWHERE],
-        out_shape=[part, part, jax.ShapeDtypeStruct((2 * half, width), BF16)],
+        functools.partial(out_kernel, batches),
+        in_specs=[SCALARS, vmem, vmem, ANYWHERE],
+        out_specs=[vmem, vmem],
+        out_shape=[part, part],
         scratch_shapes=[
             pltpu.VMEM((2 * half, width), BF16),
             pltpu.VMEM((rows, width), F32),
-            pltpu.SemaphoreType.DMA((count * chips + 1,)),
+            pltpu.SemaphoreType.DMA((width // (2 * LANES),)),
         ],
         compiler_params=PARAMS,
-        cost_estimate=cost(4 * rows * half * width, 8 * half * width + 12 * rows * width),
-    )(core, starts, o_mine, o_other, *pieces)
-
-
-def mlp_kernel(seq, filled, *refs):
-    x_mine, x_other, d_mine, d_other = refs[:4]
-    gates, ups, downs = (refs[4 + i * seq : 4 + (i + 1) * seq] for i in range(3))
-    refs = refs[4 + 3 * seq + filled :]
-    xs, ds = refs[:seq], refs[seq : 2 * seq]
-    hidden_ref, d_gate_ref, d_up_ref = refs[2 * seq : 2 * seq + 3]
-    rows = x_mine.shape[0]
-    block = x_mine.shape[1] // seq
-
-    @pl.when(pl.program_id(0) == 0)
-    def _():
-        for r in range(seq):
-            cut = slice(r * block, (r + 1) * block)
-            xs[r][:rows] = x_mine[:, cut]
-            xs[r][rows:] = x_other[:, cut]
-            ds[r][:rows] = d_mine[:, cut]
-            ds[r][rows:] = d_other[:, cut]
-
-    gate_val = sum(dot(xs[r][...], gates[r][...]) for r in range(seq))
-    up_val = sum(dot(xs[r][...], ups[r][...]) for r in range(seq))
-    d_hidden = sum(dot_nt(ds[r][...], downs[r][...]) for r in range(seq))
+        cost_estimate=cost(4 * rows * half * width, 4 * half * width + 12 * rows * width),
+    )(core, o_mine, o_other, w)
+
+
+def hidden_units(x, d, gate, up, down_t, hidden_ref, d_gate_ref, d_up_ref):
+    gate_val = dot(x[...], gate[...])
+    up_val = dot(x[...], up[...])
+    d_hidden = dot(d[...], down_t[...])
     sigmoid_g = 1.0 / (1.0 + jnp.exp(-gate_val))
     activated = gate_val * sigmoid_g
     slope = sigmoid_g * (1.0 + gate_val * (1.0 - sigmoid_g))
@@ -551,81 +526,132 @@
     d_up_ref[...] = (d_hidden * activated).astype(BF16)
 
 
-def mlp_slot(slot, slots, x_mine, x_other, d_mine, d_other, gates, ups, downs, kept):
-    seq = len(gates)
-    rows, width = x_mine.shape
-    block = width // seq
-    hidden_width = gates[0].shape[1]
+def first_hidden_kernel(per, filled, *refs):
+    arrived = refs[: 2 * per]
+    weights = refs[2 * per : 2 * per + 3]
+    x, d, hidden_ref, d_gate_ref, d_up_ref, sems = refs[2 * per + 3 + filled :]
+    rows = arrived[0].shape[0]
+
+    @pl.when(pl.program_id(0) == 0)
+    def _():
+        copies = [
+            pltpu.make_async_copy(
+                arrived[2 * i + j], out.at[pl.ds(i * rows, rows)], sems.at[2 * i + j]
+            )
+            for i in range(per)
+            for j, out in enumerate((x, d))
+        ]
+        for copy in copies:
+            copy.start()
+        for copy in copies:
+            copy.wait()
+
+    hidden_units(x, d, *weights, hidden_ref, d_gate_ref, d_up_ref)
+
+
+def second_hidden_kernel(filled, x, d, gate, up, down_t, *refs):
+    hidden_units(x, d, gate, up, down_t, *refs[filled:])
+
+
+def hidden_group(at, groups, arrived, weights, kept, rows_of=None):
+    width = weights.shape[0]
+    hidden_width = weights.shape[1] // 3
     tile = 2 * LANES
-
-    def whole(shape):
-        return pl.BlockSpec(shape, lambda j: (0, 0))
-
-    wide = [jax.ShapeDtypeStruct((2 * rows * slots, block), BF16)] * (2 * seq)
-    narrow = [jax.ShapeDtypeStruct((2 * rows * slots, hidden_width), BF16)] * 3
-    filled = 0 if kept is None else 2 * seq + 3
-    first = 4 + 3 * seq
-    return pl.pallas_call(
-        functools.partial(mlp_kernel, seq, filled),
-        grid=(hidden_width // tile,),
-        in_specs=[whole((rows, width))] * 4
-        + [pl.BlockSpec((block, tile), lambda j: (0, j))] * (2 * seq)
-        + [pl.BlockSpec((tile, block), lambda j: (j, 0))] * seq
+    tiles = hidden_width // tile
+    if rows_of is None:
+        height = arrived[0].shape[0] * len(arrived) // 2
+        per = len(arrived) // 2
+        total = height * groups
+        sources, source_specs = arrived, [ANYWHERE] * len(arrived)
+        wide = [jax.ShapeDtypeStruct((total, width), BF16)] * 2
+        scratch = [pltpu.SemaphoreType.DMA((2 * per,))]
+    else:
+        total = rows_of[0].shape[0]
+        height = total // groups
+        sources = list(rows_of)
+        source_specs = [pl.BlockSpec((height, width), lambda j: (at, 0))] * 2
+        wide, scratch = [], []
+    narrow = [jax.ShapeDtypeStruct((total, hidden_width), BF16)] * 3
+    filled = 0 if kept is None else len(wide) + 3
+    kernel = (
+        functools.partial(first_hidden_kernel, per, filled)
+        if rows_of is None
+        else functools.partial(second_hidden_kernel, filled)
+    )
+    first = len(sources) + 3
+    return pl.pallas_call(
+        kernel,
+        grid=(tiles,),
+        in_specs=source_specs
+        + [
+            pl.BlockSpec((width, tile), lambda j, skipped=i * tiles: (0, skipped + j))
+            for i in range(3)
+        ]
         + [ANYWHERE] * filled,
-        out_specs=[pl.BlockSpec((2 * rows, block), lambda j: (slot, 0))] * (2 * seq)
-        + [pl.BlockSpec((2 * rows, tile), lambda j: (slot, j))] * 3,
+        out_specs=[pl.BlockSpec((height, width), lambda j: (at, 0))] * len(wide)
+        + [pl.BlockSpec((height, tile), lambda j: (at, j))] * 3,
         out_shape=wide + narrow,
+        scratch_shapes=scratch,
         input_output_aliases={first + i: i for i in range(filled)},
         compiler_params=PARAMS,
         cost_estimate=cost(
-            12 * rows * width * hidden_width,
-            6 * width * hidden_width + 24 * rows * width,
-            2 * rows * hidden_width,
+            6 * height * width * hidden_width,
+            6 * width * hidden_width + 12 * height * width,
+            height * hidden_width,
         ),
-    )(x_mine, x_other, d_mine, d_other, *gates, *ups, *downs, *([] if kept is None else kept))
-
-
-def mlp_back_kernel(seq, hidden, d_gate, d_up, *refs):
-    weights = refs[: 3 * seq]
-    back_mine, back_other, out_mine, out_other = refs[3 * seq : 3 * seq + 4]
-    held, sems = refs[3 * seq + 4 : -1], refs[-1]
-    rows = back_mine.shape[0]
-    block = back_mine.shape[1] // seq
-    copies = [pltpu.make_async_copy(weights[i], held[i], sems.at[i]) for i in range(3 * seq)]
-    for r in range(seq):
-        for i in range(3):
-            copies[i * seq + r].start()
-    for r in range(seq):
-        cut = slice(r * block, (r + 1) * block)
-        for i in range(3):
-            copies[i * seq + r].wait()
-        back = dot_nt(d_gate[...], held[r][...]) + dot_nt(d_up[...], held[seq + r][...])
-        back_mine[:, cut] = back[:rows].astype(BF16)
-        back_other[:, cut] = back[rows:].astype(BF16)
-        out = dot(hidden[...], held[2 * seq + r][...])
-        out_mine[:, cut] = out[:rows].astype(BF16)
-        out_other[:, cut] = out[rows:].astype(BF16)
-
-
-def mlp_back(slot, slots, hidden, d_gate, d_up, gates, ups, downs):
-    seq = len(gates)
-    rows, width = hidden.shape[0] // (2 * slots), gates[0].shape[0] * seq
-    hidden_width = hidden.shape[1]
-    weights = [*gates, *ups, *downs]
-    return pl.pallas_call(
-        functools.partial(mlp_back_kernel, seq),
+    )(*sources, weights, weights, weights, *([] if kept is None else kept))
+
+
+def mlp_back_kernel(*refs):
+    parts, weights = (refs[:3], refs[3:6]), refs[6:8]
+    back_ref, out_ref, held_own, held_oth, sems = refs[8:]
+    width, count = back_ref.shape[1], refs[0].shape[1]
+    block = 4 * LANES
+    steps = width // block
+    copies = [
+        pltpu.make_async_copy(
+            weight.at[pl.ds(lo, block)],
+            held.at[pl.ds(lo, block)],
+            sems.at[i * steps + lo // block],
+        )
+        for i, (weight, held) in enumerate(zip(weights, (held_own, held_oth)))
+        for lo in range(0, width, block)
+    ]
+    for step in range(steps):
+        for i in range(2):
+            copies[i * steps + step].start()
+    for step in range(steps):
+        cut = slice(step * block, (step + 1) * block)
+        back, out = 0.0, 0.0
+        for i, held in enumerate((held_own, held_oth)):
+            copies[i * steps + step].wait()
+            hidden, d_gate, d_up = parts[i]
+            back += dot_nt(d_gate[...], held[cut, :count])
+            back += dot_nt(d_up[...], held[cut, count : 2 * count])
+            out += dot_nt(hidden[...], held[cut, 2 * count :])
+        back_ref[:, cut] = back.astype(BF16)
+        out_ref[:, cut] = out.astype(BF16)
+
+
+def mlp_back(at, groups, own, other, weights, weights_oth):
+    height, hidden_width = own[0].shape[0] // groups, own[0].shape[1]
+    width = weights.shape[0]
+    return pl.pallas_call(
+        mlp_back_kernel,
         grid=(1,),
-        in_specs=[pl.BlockSpec((2 * rows, hidden_width), lambda j: (slot, 0))] * 3
-        + [ANYWHERE] * (3 * seq),
-        out_specs=[pl.BlockSpec((rows, width), lambda j: (0, 0))] * 4,
-        out_shape=[jax.ShapeDtypeStruct((rows, width), BF16)] * 4,
-        scratch_shapes=[pltpu.VMEM(w.shape, BF16) for w in weights]
-        + [pltpu.SemaphoreType.DMA((3 * seq,))],
+        in_specs=[pl.BlockSpec((height, hidden_width), lambda j: (at, 0))] * 6 + [ANYWHERE] * 2,
+        out_specs=[pl.BlockSpec((height, width), lambda j: (0, 0))] * 2,
+        out_shape=[jax.ShapeDtypeStruct((height, width), BF16)] * 2,
+        scratch_shapes=[
+            pltpu.VMEM(weights.shape, BF16),
+            pltpu.VMEM(weights.shape, BF16),
+            pltpu.SemaphoreType.DMA((2 * (width // (4 * LANES)),)),
+        ],
         compiler_params=PARAMS,
         cost_estimate=cost(
-            12 * rows * width * hidden_width, 6 * width * hidden_width + 14 * rows * width
+            12 * height * width * hidden_width, 12 * width * hidden_width + 14 * height * width
         ),
-    )(hidden, d_gate, d_up, *weights)
+    )(*own, *other, weights, weights_oth)
 
 
 def d_attended_kernel(batches, other_blocks, core_ref, d_own, d_oth, w_ref, mine, other, d_rows):
@@ -657,22 +683,24 @@
     blocks = heads_width // 2 // block
 
     def whole(shape):
-        return pl.BlockSpec(shape, lambda j: (0, 0))
+        return pl.BlockSpec(shape, lambda j, c: (0, 0))
 
     return pl.pallas_call(
         functools.partial(d_attended_kernel, batches, blocks),
-        grid=(2 * blocks,),
-        in_specs=[
-            SCALARS,
-            whole(d_own.shape),
-            whole(d_own.shape),
-            pl.BlockSpec((block, width), lambda j: ((j + blocks) % (2 * blocks), 0)),
-        ],
-        out_specs=[
-            pl.BlockSpec((rows, block), lambda j: (0, jnp.maximum(j - blocks, 0))),
-            pl.BlockSpec((rows, block), lambda j: (0, jnp.minimum(j, blocks - 1))),
-            whole((rows, width)),
-        ],
+        grid_spec=pltpu.PrefetchScalarGridSpec(
+            num_scalar_prefetch=1,
+            grid=(2 * blocks,),
+            in_specs=[
+                whole(d_own.shape),
+                whole(d_own.shape),
+                pl.BlockSpec((block, width), lambda j, c: ((j + (1 - c[0]) * blocks) % (2 * blocks), 0)),
+            ],
+            out_specs=[
+                pl.BlockSpec((rows, block), lambda j, c: (0, jnp.maximum(j - blocks, 0))),
+                pl.BlockSpec((rows, block), lambda j, c: (0, jnp.minimum(j, blocks - 1))),
+                whole((rows, width)),
+            ],
+        ),
         out_shape=[
             jax.ShapeDtypeStruct((rows, heads_width // 2), F32),
             jax.ShapeDtypeStruct((rows, heads_width // 2), BF16),
@@ -721,18 +749,16 @@
     )(starts, *sources, right)
 
 
-def d_normed_kernel(batches, core_ref, dq_ref, dkv_ref, w_ref, own, other, acc):
-    width = dq_ref.shape[1]
-    acc[...] = dot_nt(dq_ref[...], w_ref[:, :width]) + dot_nt(
-        dkv_ref[...], w_ref[:, width : width + dkv_ref.shape[1]]
-    )
+def d_normed_kernel(batches, core_ref, dq_ref, dkv_ref, wq_ref, wkv_ref, own, other, acc):
+    acc[...] = dot_nt(dq_ref[...], wq_ref[...]) + dot_nt(dkv_ref[...], wkv_ref[...])
     split_rows(batches, core_ref, acc, own, other)
 
 
-def d_normed_rows(core, dq, dkv, w, batches):
-    rows = dq.shape[0]
-    depth, width = w.shape
+def d_normed_rows(core, dq, dkv, w, first, batches):
+    rows, depth = dq.shape[0], w.shape[0]
+    width = dq.shape[1] + dkv.shape[1]
     block = 4 * LANES
+    q_at, kv_at = first // dq.shape[1], (first + dq.shape[1]) // dkv.shape[1]
 
     def whole(shape):
         return pl.BlockSpec(shape, lambda j: (0, 0))
@@ -745,14 +771,15 @@
             SCALARS,
             whole(dq.shape),
             whole(dkv.shape),
-            pl.BlockSpec((block, width), lambda j: (j, 0)),
+            pl.BlockSpec((block, dq.shape[1]), lambda j: (j, q_at)),
+            pl.BlockSpec((block, dkv.shape[1]), lambda j: (j, kv_at)),
         ],
         out_specs=[part, part],
         out_shape=[jax.ShapeDtypeStruct((rows // 2, depth), F32)] * 2,
         scratch_shapes=[pltpu.VMEM((rows, block), F32)],
         compiler_params=PARAMS,
         cost_estimate=cost(2 * rows * depth * width, 2 * depth * width + 4 * rows * depth),
-    )(core, dq, dkv, w)
+    )(core, dq, dkv, w, w)
 
 
 def rms_inverse(values):
@@ -788,9 +815,9 @@
     order = folded_order(chips)
     shard = w_query.shape[0]
     query_half, kv_half = w_query.shape[1] // 2, w_key.shape[1] // 2
+    out_half = model_width // 2
     chip_rows = 2 * slot_count
     own_rows = batches * slot_count
-    attn_width = query_half + 2 * kv_half
     limits = lengths[:, 0]
 
     def chip_back(k):
@@ -820,38 +847,6 @@
             jnp.concatenate([own, other], axis),
             jnp.concatenate([other, own], axis),
         )
-
-    def turn_blocks(array):
-        block = array.shape[-1] // seq_size
-        bit = 1
-        while bit < seq_size:
-            turned = jnp.concatenate(
-                [
-                    array[..., (r ^ bit) * block : ((r ^ bit) + 1) * block]
-                    for r in range(seq_size)
-                ],
-                axis=-1,
-            )
-            array = jnp.where((seq_at & bit) != 0, turned, array)
-            bit *= 2
-        return array
-
-    gains = jnp.concatenate(
-        [attn_gain[:, None], mlp_gain[:, None], jnp.zeros((shard, LANES - 2), BF16)], axis=1
-    )
-    packed, to_other = pack(core_ref, w_query, w_key, w_value, w_out, gains)
-    piece_a, piece_o = stack_pieces(
-        core_ref, packed, swap_core(to_other), attn_width + LANES
-    )
-    ring_a = ring_gather(piece_a)
-    cubes_a = [cube_gather(slot, k % 2) for k, slot in enumerate(ring_a)]
-    x_own = tokens.reshape(own_rows, model_width)
-    x_oth = swap_core(x_own)
-    ring_o = jnp.concatenate(ring_gather(after(piece_o, ring_a[-1])), 0)
-    cube_o = cube_gather(after(ring_o, cubes_a[-1][1], cubes_a[-1][2]), 0)
-    gates = cube_gather(after(w_gate, cube_o[1], cube_o[2]), 1)
-    ups = cube_gather(after(w_up, gates[1], gates[2]), 0)
-    downs = cube_gather(after(w_down, ups[1], ups[2]), 1)
 
     q_positions = chip_at * chip_rows + jnp.arange(chip_rows)
     cosine, sine = rope_tables(q_positions)
@@ -861,60 +856,139 @@
     own_pos = ctx_at * slot_count + jnp.arange(slot_count)
     valid = (own_pos[None, :] < limits[:, None]).astype(F32).reshape(own_rows, 1)
     d_output = cotangent.reshape(own_rows, model_width).astype(F32) * valid
-    d_turned = turn_blocks(d_output.astype(BF16))
-
-    flat_a = [cubes_a[k][r] for r in range(seq_size) for k in range(chips)]
-    q, kv, normed_a, gain_rows, attn_w = project_qkv(
-        core_ref, starts, x_own, x_oth, cosine_all, sine_all, flat_a, batches, query_half, kv_half
+    d_rows = d_output.astype(BF16)
+
+    gains = jnp.concatenate(
+        [attn_gain[:, None], mlp_gain[:, None], jnp.zeros((shard, LANES - 2), BF16)], axis=1
+    )
+    x_own = tokens.reshape(own_rows, model_width)
+    x_oth = swap_core(x_own)
+    packed, to_other = pack(core_ref, w_query, w_key, w_value, w_out, gains)
+    (piece_a,) = stack_pieces(core_ref, packed, swap_core(to_other), [packed.shape[1]])
+    d_slots = [d_rows, ring_step(d_rows)]
+    ring_a, cubes_a = [after(piece_a, x_oth)], []
+    for k in range(chips):
+        cubes_a.append(cube_gather(ring_a[k], k % 2))
+        if k + 1 < chips:
+            seen = [cubes_a[k - 1][1], cubes_a[k - 1][2]] if k else d_slots[1:2]
+            ring_a.append(ring_step(after(ring_a[k], *seen)))
+    mlp_w = jnp.concatenate([w_gate, w_up, w_down.T], axis=1)
+    mlp_w = lax.all_gather(after(mlp_w, *sum(cubes_a, [])), "seq", axis=0, tiled=True)
+
+    def flat(cubes):
+        return [cubes[k][r] for r in range(seq_size) for k in range(chips)]
+
+    kv, normed_a, gain_rows, attn_w = project_kv(
+        core_ref, starts, x_own, x_oth, cosine_all, sine_all, flat(cubes_a), batches, 2 * kv_half
     )
     gain_a, gain_m = gain_rows[0:1], gain_rows[1:2]
     kv_slots = ring_gather(kv)
-    d_slots = ring_gather(after(d_turned, ring_o))
-    d_pairs = [(slot, swap_core(slot)) for slot in d_slots]
+    q = project_q(
+        normed_a, cosine_all, sine_all, attn_w, out_half, query_half
+    )
+    for k in range(2, chips):
+        d_slots.append(ring_step(after(d_slots[-1], *([kv_slots[-1]] if k == 2 else []))))
     attended, lse = attend(q, kv_slots, limits, kpos, qpos)
-    attended_oth = swap_core(attended)
-    branch, branch_oth, out_w = project_out(
-        core_ref, out_starts, attended, attended_oth, cube_o, batches, chips
-    )
-
-    residual = x_own.astype(F32) + by_core(branch, swap_core(branch_oth), 1)
+    attended_oth = swap_core(after(attended, d_slots[2 % chips]))
+    branch, branch_oth = project_out(
+        core_ref, attended, attended_oth, attn_w, out_half, batches
+    )
+
+    branch_oth = after(swap_core(branch_oth), d_slots[-1])
+    residual = x_own.astype(F32) + by_core(branch, branch_oth, 1)
     inverse_m = rms_inverse(residual)
-    x_slots = ring_gather(turn_blocks((residual * inverse_m * gain_m).astype(BF16)))
-    kept = None
-    back_parts, out_parts = [None] * chips, [None] * chips
-    for k in range(chips):
-        kept = mlp_slot(
-            k, chips, x_slots[k], swap_core(x_slots[k]), *d_pairs[k], gates, ups, downs, kept
-        )
-        parts = mlp_back(k, chips, *kept[2 * seq_size :], gates, ups, downs)
-        back_parts[k] = (parts[0], swap_core(parts[1]))
-        out_parts[k] = (parts[2], parts[3])
-    d_normed = turn_blocks(
-        ring_scatter([own.astype(F32) + oth.astype(F32) for own, oth in back_parts])
-    )
-    xs, ds = kept[:seq_size], kept[seq_size : 2 * seq_size]
-    hidden, d_gate, d_up = kept[2 * seq_size :]
+    normed_m = (residual * inverse_m * gain_m).astype(BF16)
+    x_slots = [normed_m]
+    for k in range(1, min(chips, 3)):
+        x_slots.append(ring_step(x_slots[-1]))
+    mlp_w_oth = swap_core(after(mlp_w, x_slots[1 % chips]))
+    per = 2 if chips % 2 == 0 else 1
+    groups = chips // per
+    kept, kept_oth, back_parts, out_slots, out_sums = None, None, [], [], []
+    for g in range(groups):
+        arrived = []
+        for k in range(g * per, (g + 1) * per):
+            arrived += [x_slots[k], d_slots[k]]
+        kept = hidden_group(g, groups, arrived, mlp_w, kept)
+        while len(x_slots) < chips:
+            x_slots.append(ring_step(after(x_slots[-1], kept[0])))
+        kept_oth = hidden_group(g, groups, None, mlp_w_oth, kept_oth, kept[:2])
+        own, other = list(kept[2:]), list(kept_oth)
+        if g == 0:
+            own[0] = after(own[0], x_slots[min(2, chips - 1)])
+        elif g == 1:
+            back_first = ring_step(back_parts[1])
+            own[0] = after(own[0], back_first)
+        back, out = mlp_back(g, groups, own, other, mlp_w, mlp_w_oth)
+        for i in range(per):
+            rows = slice(i * own_rows, (i + 1) * own_rows)
+            back_parts.append(back[rows])
+            out_slots.append(out[rows].astype(F32))
+    total, steps = back_parts[1 % chips].astype(F32), []
+    for k in range(2, chips + 1):
+        low = total.astype(BF16)
+        if k == 3:
+            kept = [after(array, low) for array in kept]
+        steps.append(back_first if k == 2 and groups > 1 else ring_step(low))
+        total = steps[-1].astype(F32) + back_parts[k % chips].astype(F32)
+    d_normed = total
+    x_all, d_all = kept[:2]
 
     def rows_product(left, right):
         return jnp.einsum("ri,rj->ij", left, right, preferred_element_type=F32).astype(BF16)
 
-    grad_gate = cube_scatter([rows_product(x, d_gate) for x in xs], 0)
-    grad_up = cube_scatter([rows_product(x, d_up) for x in xs], 1)
-    grad_down = cube_scatter([rows_product(hidden, d) for d in ds], 0)
+    def seq_sum(array, axis):
+        return lax.psum_scatter(array, "seq", scatter_dimension=axis, tiled=True).astype(F32)
+
+    products = [(rows_product(kept[2], d_all), rows_product(kept_oth[0], d_all))]
+    for i in range(2):
+        products.append(
+            [
+                rows_product(x_all, after(array, *steps[1 : 1 + i]))
+                for array in (kept[3 + i], kept_oth[1 + i])
+            ]
+        )
+    sums = [
+        (own.astype(F32) + swap_core(other).astype(F32)).astype(BF16) for own, other in products
+    ]
+    grad_down, grad_gate, grad_up = (
+        seq_sum(array, axis) for array, axis in zip(sums, (1, 0, 0))
+    )
 
     plain_m = residual * inverse_m
     back_m, gain_m_part = rms_back(d_normed, plain_m, inverse_m, gain_m)
     d_resid = d_output + back_m
     d_low = d_resid.astype(BF16)
-    do_mine, do_other, d_half = d_attended(
-        core_ref, mine(d_low, 1), swap_core(others(d_low, 1)), out_w, batches
-    )
+    out_sum = out_slots[1 % chips]
+    for k in range(2, chips):
+        waits = [d_low]
+        if k > 2:
+            waits = [do_mine]
+        out_sums.append(ring_step(after(out_sum.astype(BF16), *waits)))
+        out_sum = out_sums[-1].astype(F32) + out_slots[k]
+        if k == 2:
+            do_mine, do_other, d_half = d_attended(
+                core_ref,
+                mine(d_low, 1),
+                swap_core(others(d_low, 1)),
+                after(attn_w, *sum(map(list, products), [])),
+                batches,
+            )
     d_query, *d_kv_slots = attend_back(
-        q, kv_slots, do_mine, swap_core(do_other), lse, limits, kpos, qpos, cosine, sine
-    )
-
-    def owner_sum(chunks, route):
-        summed = cube_scatter(chunks, route)
+        q,
+        kv_slots,
+        do_mine,
+        after(swap_core(do_other), out_sums[0], *sums),
+        lse,
+        limits,
+        kpos,
+        qpos,
+        cosine,
+        sine,
+    )
+
+    def owner_sum(chunks, route, *waits):
+        summed = cube_scatter(chunks, route, *waits)
         rows = 2 * shard
         return ring_scatter([summed[k * rows : (k + 1) * rows] for k in range(chips)])
 
@@ -927,27 +1001,20 @@
             for lo, hi in zip(edges[:-1], edges[1:])
         ]
 
+    passing = [ring_step(after(d_kv_slots[1], *out_sums[1:2]))]
+    for k in range(2, chips):
+        total = passing[-1].astype(F32) + d_kv_slots[k].astype(F32)
+        passing.append(ring_step(total.astype(BF16)))
     grad_out = owner_sum(
-        grad_chunks(out_starts, [attended, attended_oth], d_half, seq_size, chips), 1
-    )
-    (grad_out,) = own_shard(grad_out, [model_width // 2])
+        grad_chunks(out_starts, [attended, attended_oth], d_half, seq_size, chips), 1, passing[0]
+    )
+    (grad_out,) = own_shard(grad_out, [out_half])
     grad_query = owner_sum(grad_chunks(starts, [normed_a], d_query, seq_size, chips), 0)
     (grad_query,) = own_shard(grad_query, [query_half])
-    last = d_kv_slots[1 % chips]
-    for k in range(2, chips):
-        last = (ring_step(last).astype(F32) + d_kv_slots[k].astype(F32)).astype(BF16)
-    d_kv = unrotate(ring_step(last), d_kv_slots[0], cosine_all, sine_all)
-    grad_kv = owner_sum(grad_chunks(starts, [normed_a], d_kv, seq_size, chips), 1)
-    kv_parts = own_shard(grad_kv, [LANES] * (2 * kv_half // LANES))
-    grad_kv = [
-        jnp.concatenate(
-            [part[:, :LANES] for part in kv_parts[i::2]]
-            + [part[:, LANES:] for part in kv_parts[i::2]],
-            axis=1,
-        )
-        for i in range(2)
-    ]
-    d_normed_a, d_normed_oth = d_normed_rows(core_ref, d_query, d_kv, attn_w, batches)
+    out_last = ring_step(after(out_sum.astype(BF16), passing[1]))
+    d_kv = unrotate(passing[-1], d_kv_slots[0], cosine_all, sine_all)
+    d_normed_a, d_normed_oth = d_normed_rows(core_ref, d_query, d_kv, attn_w, out_half, batches)
+    d_kv = after(d_kv, d_normed_oth)
     d_normed_a = d_normed_a + swap_core(d_normed_oth)
     x_own_f = x_own.astype(F32)
     inverse_a = rms_inverse(x_own_f)
@@ -959,15 +1026,24 @@
     while bit < seq_size:
         gain_sum = gain_sum + swap_seq(gain_sum, bit)
         bit *= 2
-    passing = gain_sum
+    gain_part = gain_sum
     for _ in range(chips - 1):
-        passing = ring_step(passing)
-        gain_sum = gain_sum + passing
+        gain_part = ring_step(gain_part)
+        gain_sum = gain_sum + gain_part
+    grad_kv = owner_sum(grad_chunks(starts, [normed_a], d_kv, seq_size, chips), 1)
+    kv_parts = own_shard(after(grad_kv, gain_sum), [LANES] * (2 * kv_half // LANES))
+    grad_kv = [
+        jnp.concatenate(
+            [part[:, :LANES] for part in kv_parts[i::2]]
+            + [part[:, LANES:] for part in kv_parts[i::2]],
+            axis=1,
+        )
+        for i in range(2)
+    ]
     gain_sum = lax.dynamic_slice_in_dim(gain_sum, (seq_at * ctx_size + ctx_at) * shard, shard, 1)
 
-    out_parts = [(own, swap_core(oth)) for own, oth in out_parts]
-    branch_m = ring_scatter([own.astype(F32) + oth.astype(F32) for own, oth in out_parts])
-    activations = (residual + turn_blocks(branch_m)).astype(BF16)
+    branch_m = out_slots[0] + out_last.astype(F32)
+    activations = (residual + branch_m).astype(BF16)
     return (
         activations.reshape(tokens.shape),
         input_grad.reshape(tokens.shape),

time: 821 us -> 746 us (0.909)
  waiting for transfers between devices: 344 us -> 268 us
  starting transfers between devices: 122 us -> 94.6 us
  other arithmetic: 54.5 us -> 72.6 us
  between operations: 2.38 us -> 15 us
    ppermute x44 -> x23, waiting for transfers between devices: 180 us -> 81.3 us  [swap_seq(): return lax.ppermute(array, 'seq', [(i, i ^ bit) for i in range(seq)])]
    convert_element_type x4 -> x15, other arithmetic: 5.27 us -> 42.4 us  [the longest x3 20.5 us: body(): (own.astype(F32) + swap_core(other).astype(F32)).astype(BF16)]
    ppermute x36 -> x33, waiting for transfers between devices: 160 us -> 181 us  [ring_step(): return lax.ppermute(array, 'ctx', pairs)]
    ppermute x44 -> x23, starting transfers between devices: 46.8 us -> 30.9 us  [swap_seq(): return lax.ppermute(array, 'seq', [(i, i ^ bit) for i in range(seq)])]
    ppermute x36 -> x33, starting transfers between devices: 69.6 us -> 61.7 us  [ring_step(): return lax.ppermute(array, 'ctx', pairs)]
    dot_general x12 -> x6, matrix products: 42.1 us -> 43 us  [rows_product(): jnp.einsum('ri,rj->ij', left, right, preferred_element_type=F32)]
    pallas_call x11 -> x10, Pallas kernels: 128 us -> 129 us  [the longest x4 52.9 us: hidden_group(): pl.pallas_call(kernel, grid=(tiles,), in_specs=source_specs + [pl.BlockSp...]
  transfers between devices with their start and end apart: 107 -> 75, of which waited for: 51 -> 39; matrix products, arithmetic and copies ran while one was open for 13% -> 15% of each run, Pallas kernels for 27% -> 28%
where the time goes in v3:
time: 746 us; the launch traced here: 737 us
  waiting for transfers between devices  268 us (36%)
  Pallas kernels  227 us (30%)
  starting transfers between devices  94.6 us (13%)
  other arithmetic  72.6 us (10%)
  matrix products  43 us (6%)
  local copies, waits for them, and re-layouts  17.3 us (2%)
  between operations  15 us (2%)
    ppermute x33, waiting for transfers between devices, ring_step(): return lax.ppermute(array, 'ctx', pairs)  181 us
    ppermute x23, waiting for transfers between devices, swap_seq(): return lax.ppermute(array, 'seq', [(i, i ^ bit) for i in range(seq)])  81.3 us
    ppermute x33, starting transfers between devices, ring_step(): return lax.ppermute(array, 'ctx', pairs)  61.7 us
    pallas_call x4, Pallas kernels, hidden_group(): pl.pallas_call(kernel, grid=(tiles,), in_specs=source_specs + [pl.BlockSp...  52.9 us
    dot_general x6, matrix products, rows_product(): jnp.einsum('ri,rj->ij', left, right, preferred_element_type=F32)  43 us
    pallas_call x2, Pallas kernels, mlp_back(): pl.pallas_call(mlp_back_kernel, grid=(1,), in_specs=[pl.BlockSpec((height...  41.6 us
    pallas_call x1, Pallas kernels, attend_back(): pl.pallas_call(functools.partial(attend_back_kernel, chips), grid_spec=pl...  34.6 us
    ppermute x23, starting transfers between devices, swap_seq(): return lax.ppermute(array, 'seq', [(i, i ^ bit) for i in range(seq)])  30.9 us
  transfers between devices with their start and end apart: 75, of which 39 were waited for; matrix products, arithmetic and copies ran while one was open for 15% of the time, Pallas kernels for 28%

profile of v3, /device:TPU:0, one launch (start us, length us, event | category | flops | bytes accessed | tf_op | source)
XLA Modules:
  0.0 737.4 jit_solution(6744554838097370797)
XLA Ops:
  21.9 15.5 %collective-permute-done.2.refs_3_ = bf16[256,2048]{1,0:T(8,128)(2,1)} collective-permute-done((bf16[256,2048]{1,0:T(8,128)(2,1)S(1)}, bf16[256,2048]{1,0:T(8,128)(2,1)}, u32[]{:S(2)}, u32[]{:S(2)}) %collective-permute-start.2) | collective-permute-done | bytes 1048608 | tf_op jit(solution)/shard_map/ppermute | solution.py:44
  43.9 11.9 %collective-permute-done.3.refs_7_ = bf16[128,2688]{1,0:T(8,128)(2,1)S(1)} collective-permute-done((bf16[128,2688]{1,0:T(8,128)(2,1)}, bf16[128,2688]{1,0:T(8,128)(2,1)S(1)}, u32[]{:S(2)}, u32[]{:S(2)}) %collective-permute-start.3) | collective-permute-done | bytes 688160 | tf_op jit(solution)/shard_map/ppermute | solution.py:44
  62.1 12.6 %collective-permute-done.6.refs_8_ = bf16[128,2688]{1,0:T(8,128)(2,1)} collective-permute-done((bf16[128,2688]{1,0:T(8,128)(2,1)S(1)}, bf16[128,2688]{1,0:T(8,128)(2,1)}, u32[]{:S(2)}, u32[]{:S(2)}) %collective-permute-start.6) | collective-permute-done | bytes 688160 | tf_op jit(solution)/shard_map/ppermute | solution.py:44
  79.6 11.6 %collective-permute-done.9.refs_9_ = bf16[128,2688]{1,0:T(8,128)(2,1)} collective-permute-done((bf16[128,2688]{1,0:T(8,128)(2,1)}, bf16[128,2688]{1,0:T(8,128)(2,1)}, u32[]{:S(2)}, u32[]{:S(2)}) %collective-permute-start.9) | collective-permute-done | bytes 688160 | tf_op jit(solution)/shard_map/ppermute | solution.py:44
  96.8 13.1 %collective-permute-done.13.refs_17_ = bf16[128,2688]{1,0:T(8,128)(2,1)} collective-permute-done((bf16[128,2688]{1,0:T(8,128)(2,1)}, bf16[128,2688]{1,0:T(8,128)(2,1)}, u32[]{:S(2)}, u32[]{:S(2)}) %collective-permute-start.13) | collective-permute-done | bytes 688160 | tf_op jit(solution)/shard_map/ppermute | solution.py:33
  113.9 10.7 %collective-permute-done.12.refs_16_ = bf16[128,2688]{1,0:T(8,128)(2,1)} collective-permute-done((bf16[128,2688]{1,0:T(8,128)(2,1)}, bf16[128,2688]{1,0:T(8,128)(2,1)}, u32[]{:S(2)}, u32[]{:S(2)}) %collective-permute-start.12) | collective-permute-done | bytes 688160 | tf_op jit(solution)/shard_map/ppermute | solution.py:33
  126.7 8.6 %collective-permute-done.16.refs_20_ = bf16[128,2688]{1,0:T(8,128)(2,1)} collective-permute-done((bf16[128,2688]{1,0:T(8,128)(2,1)}, bf16[128,2688]{1,0:T(8,128)(2,1)}, u32[]{:S(2)}, u32[]{:S(2)}) %collective-permute-start.16) | collective-permute-done | bytes 688160 | tf_op jit(solution)/shard_map/ppermute | solution.py:33
  140.6 13.6 %shard_map.205 = (bf16[512,512]{1,0:T(8,128)(2,1)}, bf16[512,2048]{1,0:T(8,128)(2,1)}, f32[8,2048]{1,0:T(8,128)}, bf16[2048,2688]{1,0:T(8,128)(2,1)}) custom-call(s32[1]{0:T(128)} %bitcast.1.core_ref.refs_0_, s32[16]{0:T(128)} %mul.187.refs_1_.starts, bf16[256,2048]{1,0:T(8,128)(2,1)} %bitcast.68, bf16[256,2048]{1,0:T(8,128)(2,1)} %collective-permute-done.refs_3_, ...), custom_call_target="tpu_custom_call" | custom-call | flops 33822867456 | bytes 26214400 | tf_op jit(solution)/shard_map/pallas_call | solution.py:246
  156.4 9.6 %collective-permute-done.18.refs_1_ = bf16[512,512]{1,0:T(8,128)(2,1)S(1)} collective-permute-done((bf16[512,512]{1,0:T(8,128)(2,1)}, bf16[512,512]{1,0:T(8,128)(2,1)S(1)}, u32[]{:S(2)}, u32[]{:S(2)}) %collective-permute-start.18) | collective-permute-done | bytes 524320 | tf_op jit(solution)/shard_map/ppermute | solution.py:44
  170.9 8.6 %collective-permute-done.19.refs_2_ = bf16[512,512]{1,0:T(8,128)(2,1)S(1)} collective-permute-done((bf16[512,512]{1,0:T(8,128)(2,1)S(1)}, bf16[512,512]{1,0:T(8,128)(2,1)S(1)}, u32[]{:S(2)}, u32[]{:S(2)}) %collective-permute-start.19) | collective-permute-done | bytes 524320 | tf_op jit(solution)/shard_map/ppermute | solution.py:44
  182.9 9.7 %shard_map.206.q_ref = bf16[512,1024]{1,0:T(8,128)(2,1)} custom-call(bf16[512,2048]{1,0:T(8,128)(2,1)} %get-tuple-element.98.normed.refs_0_, f32[512,128]{1,0:T(8,128)} %bitcast.75, f32[512,128]{1,0:T(8,128)} %bitcast.78, bf16[2048,2688]{1,0:T(8,128)(2,1)} %get-tuple-element.141.w.w_all.w_ref.wq_ref.wkv_ref), custom_call_target="tpu_custom_call" | custom-call | flops 12884901888 | bytes 10485760 | tf_op jit(solution)/shard_map/pallas_call | solution.py:287
  197.5 25.9 %shard_map.207 = (bf16[512,1024]{1,0:T(8,128)(2,1)}, f32[32,256]{1,0:T(8,128)}) custom-call(s32[2]{0:T(128)} %bitcast.97, s32[1024,1]{1,0:T(8,128)} %bitcast.80, s32[1,256]{1,0:T(1,128)} %iota_add_fusion.qpos_ref, bf16[512,1024]{1,0:T(8,128)(2,1)} %shard_map.206.q_ref, bf16[512,512]{1,0:T(8,128)(2,1)} %get-tuple-element.100.refs_0_, ...), custom_call_target="tpu_custom_call" | custom-call | flops 51539607552 | bytes 4194304 | tf_op jit(solution)/shard_map/pallas_call | solution.py:352
  227.4 9.1 %shard_map.208 = (f32[256,1024]{1,0:T(8,128)}, f32[256,1024]{1,0:T(8,128)}) custom-call(s32[1]{0:T(128)} %bitcast.1.core_ref.refs_0_, bf16[512,1024]{1,0:T(8,128)(2,1)} %get-tuple-element.103.o_mine.refs_0_, bf16[512,1024]{1,0:T(8,128)(2,1)} %copy-done.40, bf16[2048,2688]{1,0:T(8,128)(2,1)} %get-tuple-element.141.w.w_all.w_ref.wq_ref.wkv_ref), custom_call_target="tpu_custom_call" | custom-call | flops 12884901888 | bytes 10485760 | tf_op jit(solution)/shard_map/pallas_call | solution.py:502
  238.3 11.1 %collective-permute-done.24.refs_3_ = bf16[256,2048]{1,0:T(8,128)(2,1)} collective-permute-done((bf16[256,2048]{1,0:T(8,128)(2,1)}, bf16[256,2048]{1,0:T(8,128)(2,1)}, u32[]{:S(2)}, u32[]{:S(2)}) %collective-permute-start.24) | collective-permute-done | bytes 1048608 | tf_op jit(solution)/shard_map/ppermute | solution.py:44
  256.7 23.2 %collective-permute-done.25.refs_2_ = bf16[256,2048]{1,0:T(8,128)(2,1)S(1)} collective-permute-done((bf16[256,2048]{1,0:T(8,128)(2,1)S(1)}, bf16[256,2048]{1,0:T(8,128)(2,1)S(1)}, u32[]{:S(2)}, u32[]{:S(2)}) %collective-permute-start.25) | collective-permute-done | bytes 1048608 | tf_op jit(solution)/shard_map/ppermute | solution.py:44
  282.4 14.1 %shard_map.209 = (bf16[1024,2048]{1,0:T(8,128)(2,1)}, bf16[1024,2048]{1,0:T(8,128)(2,1)}, bf16[1024,1024]{1,0:T(8,128)(2,1)}, bf16[1024,1024]{1,0:T(8,128)(2,1)}, bf16[1024,1024]{1,0:T(8,128)(2,1)}) custom-call(bf16[256,2048]{1,0:T(8,128)(2,1)} %copy-done.21, bf16[256,2048]{1,0:T(8,128)(2,1)} %copy-done.19, bf16[256,2048]{1,0:T(8,128)(2,1)} %copy-done.43, ...), custom_call_target="tpu_custom_call" | custom-call | flops 38654705664 | bytes 25165824 | tf_op jit(solution)/shard_map/pallas_call | solution.py:582
  296.5 9.0 %collective-permute-done.26.refs_0_ = bf16[256,2048]{1,0:T(8,128)(2,1)S(1)} collective-permute-done((bf16[256,2048]{1,0:T(8,128)(2,1)S(1)}, bf16[256,2048]{1,0:T(8,128)(2,1)S(1)}, u32[]{:S(2)}, u32[]{:S(2)}) %collective-permute-start.26) | collective-permute-done | bytes 1048608 | tf_op jit(solution)/shard_map/ppermute | solution.py:44
  309.2 12.3 %shard_map.210 = (bf16[1024,1024]{1,0:T(8,128)(2,1)}, bf16[1024,1024]{1,0:T(8,128)(2,1)}, bf16[1024,1024]{1,0:T(8,128)(2,1)}) custom-call(bf16[1024,2048]{1,0:T(8,128)(2,1)} %get-tuple-element.113.x.refs_7_, bf16[1024,2048]{1,0:T(8,128)(2,1)} %get-tuple-element.114.d.refs_8_, bf16[2048,3072]{1,0:T(8,128)(2,1)} %collective-permute-done.27.gate.up.down_t.refs_7_, ...), custom_call_target="tpu_custom_call" | custom-call | flops 38654705664 | bytes 25165824 | tf_op jit(solution)/shard_map/pallas_call | solution.py:582
  321.5 20.8 %shard_map.211 = (bf16[512,2048]{1,0:T(8,128)(2,1)}, bf16[512,2048]{1,0:T(8,128)(2,1)}) custom-call(bf16[1024,1024]{1,0:T(8,128)(2,1)} %get-tuple-element.110.refs_0_.refs_9_, bf16[1024,1024]{1,0:T(8,128)(2,1)} %get-tuple-element.111.refs_1_.refs_10_, bf16[1024,1024]{1,0:T(8,128)(2,1)} %get-tuple-element.112.refs_2_.refs_11_, ...), custom_call_target="tpu_custom_call" | custom-call | flops 77309411328 | bytes 39845888 | tf_op jit(solution)/shard_map/pallas_call | solution.py:639
  344.7 14.2 %shard_map.212 = (bf16[1024,2048]{1,0:T(8,128)(2,1)}, bf16[1024,2048]{1,0:T(8,128)(2,1)}, bf16[1024,1024]{1,0:T(8,128)(2,1)}, bf16[1024,1024]{1,0:T(8,128)(2,1)}, bf16[1024,1024]{1,0:T(8,128)(2,1)}) custom-call(bf16[256,2048]{1,0:T(8,128)(2,1)} %copy-done.41, ...), custom_call_target="tpu_custom_call", output_to_operand_aliasing={{0}: (7, {}), {1}: (8, {}), {2}: (9, {}), {3}: (10, {}), {4... | custom-call | flops 38654705664 | bytes 25165824 | tf_op jit(solution)/shard_map/pallas_call | solution.py:582
  359.0 12.3 %shard_map.213 = (bf16[1024,1024]{1,0:T(8,128)(2,1)}, bf16[1024,1024]{1,0:T(8,128)(2,1)}, bf16[1024,1024]{1,0:T(8,128)(2,1)}) custom-call(bf16[1024,2048]{1,0:T(8,128)(2,1)} %get-tuple-element.136.x, bf16[1024,2048]{1,0:T(8,128)(2,1)} %get-tuple-element.135.d, ...), custom_call_target="tpu_custom_call", output_to_operand_aliasing={{0}: (5, {}), {1}: (6, {}), {2}: (7, {})} | custom-call | flops 38654705664 | bytes 25165824 | tf_op jit(solution)/shard_map/pallas_call | solution.py:582
  371.3 20.8 %shard_map.214 = (bf16[512,2048]{1,0:T(8,128)(2,1)}, bf16[512,2048]{1,0:T(8,128)(2,1)}) custom-call(bf16[1024,1024]{1,0:T(8,128)(2,1)} %get-tuple-element.134.refs_0_, bf16[1024,1024]{1,0:T(8,128)(2,1)} %get-tuple-element.137.refs_1_, bf16[1024,1024]{1,0:T(8,128)(2,1)} %get-tuple-element.139.refs_2_, bf16[1024,1024]{1,0:T(8,128)(2,1)} %get-tuple-element.128.refs_3_, ...), custom_call_target="tpu_custom_call" | custom-call | flops 77309411328 | bytes 39845888 | tf_op jit(solution)/shard_map/pallas_call | solution.py:639
  394.0 8.7 %convolution_convert_fusion.2 = bf16[2048,1024]{1,0:T(8,128)(2,1)} fusion(bf16[1024,2048]{1,0:T(8,128)(2,1)} %get-tuple-element.136.x, bf16[1024,1024]{1,0:T(8,128)(2,1)S(1)} %copy-done.59), kind=kOutput, calls=%fused_computation.5 | convolution fusion | flops 4297064448 | bytes 10485760 | tf_op jit(solution)/shard_map/ri,rj->ij/dot_general | solution.py:938
  433.6 8.0 %convolution_convert_fusion.5 = bf16[1024,2048]{1,0:T(8,128)(2,1)S(1)} fusion(bf16[1024,1024]{1,0:T(8,128)(2,1)S(1)} %copy-done.54, bf16[1024,2048]{1,0:T(8,128)(2,1)} %get-tuple-element.135.d), kind=kOutput, calls=%fused_computation.8 | convolution fusion | flops 4297064448 | bytes 10485760 | tf_op jit(solution)/shard_map/ri,rj->ij/dot_general | solution.py:938
  448.4 9.3 %collective-permute-done.31 = bf16[256,2048]{1,0:T(8,128)(2,1)S(1)} collective-permute-done((bf16[256,2048]{1,0:T(8,128)(2,1)S(1)}, bf16[256,2048]{1,0:T(8,128)(2,1)S(1)}, u32[]{:S(2)}, u32[]{:S(2)}) %collective-permute-start.31) | collective-permute-done | bytes 1048608 | tf_op jit(solution)/shard_map/ppermute | solution.py:44
  471.7 9.0 %shard_map.215 = (f32[512,1024]{1,0:T(8,128)}, bf16[512,1024]{1,0:T(8,128)(2,1)}, bf16[512,1024]{1,0:T(8,128)(2,1)}) custom-call(s32[1]{0:T(128)} %bitcast.1.core_ref.refs_0_, bf16[256,1024]{1,0:T(8,128)(2,1)} %get-tuple-element.219.d_own, bf16[256,1024]{1,0:T(8,128)(2,1)} %copy-done.52, bf16[2048,2688]{1,0:T(8,128)(2,1)} %get-tuple-element.141.w.w_all.w_ref.wq_ref.wkv_ref), custom_call_target="tpu_custom_call" | custom-call | flops 12884901888 | bytes 10485760 | tf_op jit(solution)/shard_map/pallas_call | solution.py:688
  507.4 7.6 %add_convert_fusion = bf16[2048,1024]{1,0:T(8,128)(2,1)} fusion(bf16[2048,1024]{1,0:T(8,128)(2,1)} %collective-permute-done.38, bf16[2048,1024]{1,0:T(8,128)(2,1)} %convolution_convert_fusion.1), kind=kLoop, calls=%fused_computation | loop fusion | flops 8388608 | bytes 12582912 | tf_op jit(solution)/shard_map/convert_element_type | solution.py:952
  515.0 34.6 %shard_map.216 = (bf16[512,1024]{1,0:T(8,128)(2,1)}, bf16[512,512]{1,0:T(8,128)(2,1)}, bf16[512,512]{1,0:T(8,128)(2,1)}, bf16[512,512]{1,0:T(8,128)(2,1)}, bf16[512,512]{1,0:T(8,128)(2,1)}) custom-call(s32[2]{0:T(128)} %bitcast.98, s32[1024,1]{1,0:T(8,128)} %bitcast.81, s32[1,256]{1,0:T(1,128)} %iota_add_fusion.qpos_ref, ...), custom_call_target="tpu_custom_call" | custom-call | flops 128849018880 | bytes 9437184 | tf_op jit(solution)/shard_map/pallas_call | solution.py:431
  579.6 15.1 %collective-permute-done.51 = bf16[512,1024]{1,0:T(8,128)(2,1)S(1)} collective-permute-done((bf16[512,1024]{1,0:T(8,128)(2,1)}, bf16[512,1024]{1,0:T(8,128)(2,1)S(1)}, u32[]{:S(2)}, u32[]{:S(2)}) %collective-permute-start.51) | collective-permute-done | bytes 1048608 | tf_op jit(solution)/shard_map/ppermute | solution.py:33
  596.1 21.2 %collective-permute-done.66 = bf16[512,1024]{1,0:T(8,128)(2,1)} collective-permute-done((bf16[512,1024]{1,0:T(8,128)(2,1)}, bf16[512,1024]{1,0:T(8,128)(2,1)}, u32[]{:S(2)}, u32[]{:S(2)}) %collective-permute-start.66) | collective-permute-done | bytes 1048608 | tf_op jit(solution)/shard_map/ppermute | solution.py:33
  625.5 8.0 %shard_map.218 = (f32[256,2048]{1,0:T(8,128)}, f32[256,2048]{1,0:T(8,128)}) custom-call(s32[1]{0:T(128)} %bitcast.1.core_ref.refs_0_, bf16[512,1024]{1,0:T(8,128)(2,1)} %get-tuple-element.151.dq_ref.refs_1_, bf16[512,512]{1,0:T(8,128)(2,1)} %shard_map.217.dkv_ref.refs_1_, bf16[2048,2688]{1,0:T(8,128)(2,1)} %get-tuple-element.141.w.w_all.w_ref.wq_ref.wkv_ref, ...), custom_call_target="tpu_custom_call" | custom-call | flops 19327352832 | bytes 10485760 | tf_op jit(solution)/shard_map/pallas_call | solution.py:767
  657.1 13.3 %collective-permute-done.41 = bf16[256,2048]{1,0:T(8,128)(2,1)S(1)} collective-permute-done((bf16[256,2048]{1,0:T(8,128)(2,1)}, bf16[256,2048]{1,0:T(8,128)(2,1)S(1)}, u32[]{:S(2)}, u32[]{:S(2)}) %collective-permute-start.41) | collective-permute-done | bytes 1048608 | tf_op jit(solution)/shard_map/ppermute | solution.py:44
  (362 shorter events, 289.2 us)
Async XLA Ops:
  7.2 272.7 %all-gather.2.cloned.1.call-start = ((), (), s32[]{:S(2)}) async-start(), calls=%async_computation.3 | async-start | bytes 15728640 | tf_op jit(solution)/shard_map/all_gather | solution.py:876
  10.6 26.7 %collective-permute-start.2 = (bf16[256,2048]{1,0:T(8,128)(2,1)S(1)}, bf16[256,2048]{1,0:T(8,128)(2,1)}, u32[]{:S(2)}, u32[]{:S(2)}) collective-permute-start(bf16[256,2048]{1,0:T(8,128)(2,1)S(1)} %fusion.12.refs_1_), channel_id=1, source_target_pairs={{0,4},{1,5},{4,6},{5,7},{6,2},{7,3},{2,0},{3,1},{8,12},{9,13},{12,... | collective-permute-start | bytes 3145736 | tf_op jit(solution)/shard_map/ppermute | solution.py:44
  92.7 31.9 %collective-permute-start.12 = (bf16[128,2688]{1,0:T(8,128)(2,1)}, bf16[128,2688]{1,0:T(8,128)(2,1)}, u32[]{:S(2)}, u32[]{:S(2)}) collective-permute-start(bf16[128,2688]{1,0:T(8,128)(2,1)} %collective-permute-done.6.refs_8_), channel_id=1, source_target_pairs={{0,16},{8,24},{16,0},{24,8},{1,17},{9,25},{17,1},{25,9},{2,18},{10... | collective-permute-start | bytes 2064392 | tf_op jit(solution)/shard_map/ppermute | solution.py:33
  93.2 31.4 %collective-permute-start.15 = (bf16[128,2688]{1,0:T(8,128)(2,1)}, bf16[128,2688]{1,0:T(8,128)(2,1)}, u32[]{:S(2)}, u32[]{:S(2)}) collective-permute-start(bf16[128,2688]{1,0:T(8,128)(2,1)} %collective-permute-done.8.refs_15_), channel_id=1, source_target_pairs={{0,8},{8,0},{16,24},{24,16},{1,9},{9,1},{17,25},{25,17},{2,10},{10... | collective-permute-start | bytes 2064392 | tf_op jit(solution)/shard_map/ppermute | solution.py:33
  93.8 32.9 %collective-permute-start.11 = (bf16[128,2688]{1,0:T(8,128)(2,1)}, bf16[128,2688]{1,0:T(8,128)(2,1)}, u32[]{:S(2)}, u32[]{:S(2)}) collective-permute-start(bf16[128,2688]{1,0:T(8,128)(2,1)} %collective-permute-done.9.refs_9_), channel_id=1, source_target_pairs={{0,8},{8,0},{16,24},{24,16},{1,9},{9,1},{17,25},{25,17},{2,10},{10... | collective-permute-start | bytes 2064392 | tf_op jit(solution)/shard_map/ppermute | solution.py:33
  95.3 40.0 %collective-permute-start.16 = (bf16[128,2688]{1,0:T(8,128)(2,1)}, bf16[128,2688]{1,0:T(8,128)(2,1)}, u32[]{:S(2)}, u32[]{:S(2)}) collective-permute-start(bf16[128,2688]{1,0:T(8,128)(2,1)} %collective-permute-done.10.refs_12_), channel_id=1, source_target_pairs={{0,16},{8,24},{16,0},{24,8},{1,17},{9,25},{17,1},{25,9},{2,18},{10... | collective-permute-start | bytes 2064392 | tf_op jit(solution)/shard_map/ppermute | solution.py:33
  109.9 26.8 %collective-permute-start.17 = (bf16[128,2688]{1,0:T(8,128)(2,1)}, bf16[128,2688]{1,0:T(8,128)(2,1)}, u32[]{:S(2)}, u32[]{:S(2)}) collective-permute-start(bf16[128,2688]{1,0:T(8,128)(2,1)} %collective-permute-done.13.refs_17_), channel_id=1, source_target_pairs={{0,8},{8,0},{16,24},{24,16},{1,9},{9,1},{17,25},{25,17},{2,10},{10... | collective-permute-start | bytes 2064392 | tf_op jit(solution)/shard_map/ppermute | solution.py:33
  136.8 585.4 %reduce-scatter.4.cloned.1.call-start = ((), (), s32[]{:S(2)}) async-start(), calls=%async_computation.4 | async-start | bytes 5242880 | tf_op jit(solution)/shard_map/reduce_scatter | solution.py:941
  193.9 29.5 %collective-permute-start.21 = (bf16[256,2048]{1,0:T(8,128)(2,1)}, bf16[256,2048]{1,0:T(8,128)(2,1)}, u32[]{:S(2)}, u32[]{:S(2)}) collective-permute-start(bf16[256,2048]{1,0:T(8,128)(2,1)} %collective-permute-done.2.refs_3_), channel_id=1, source_target_pairs={{0,4},{1,5},{4,6},{5,7},{6,2},{7,3},{2,0},{3,1},{8,12},{9,13},{12,... | collective-permute-start | bytes 3145736 | tf_op jit(solution)/shard_map/ppermute | solution.py:44
  223.5 25.9 %collective-permute-start.24 = (bf16[256,2048]{1,0:T(8,128)(2,1)}, bf16[256,2048]{1,0:T(8,128)(2,1)}, u32[]{:S(2)}, u32[]{:S(2)}) collective-permute-start(bf16[256,2048]{1,0:T(8,128)(2,1)} %collective-permute-done.21.refs_1_), channel_id=1, source_target_pairs={{0,4},{1,5},{4,6},{5,7},{6,2},{7,3},{2,0},{3,1},{8,12},{9,13},{12,... | collective-permute-start | bytes 3145736 | tf_op jit(solution)/shard_map/ppermute | solution.py:44
  279.9 29.3 %collective-permute-start.27 = (bf16[2048,3072]{1,0:T(8,128)(2,1)}, bf16[2048,3072]{1,0:T(8,128)(2,1)}, u32[]{:S(2)}, u32[]{:S(2)}) collective-permute-start(bf16[2048,3072]{1,0:T(8,128)(2,1)} %all-gather.2.cloned.1.call-done.refs_4_.refs_5_.refs_6_), channel_id=1, source_target_pairs={{0,1},{1,0},{2,3},{3,2},{4,5},{5,4},{6,7},{7,6},{8,9},{9,8},{10,11... | collective-permute-start | bytes 37748744 | tf_op jit(solution)/shard_map/ppermute | solution.py:28
  305.5 38.2 %collective-permute-start.29 = (bf16[256,2048]{1,0:T(8,128)(2,1)S(1)}, bf16[256,2048]{1,0:T(8,128)(2,1)S(1)}, u32[]{:S(2)}, u32[]{:S(2)}) collective-permute-start(bf16[256,2048]{1,0:T(8,128)(2,1)S(1)} %collective-permute-done.26.refs_0_), channel_id=1, source_target_pairs={{0,4},{1,5},{4,6},{5,7},{6,2},{7,3},{2,0},{3,1},{8,12},{9,13},{12,... | collective-permute-start | bytes 3145736 | tf_op jit(solution)/shard_map/ppermute | solution.py:44
  343.6 27.6 %collective-permute-start.28 = (bf16[256,2048]{1,0:T(8,128)(2,1)S(1)}, bf16[256,2048]{1,0:T(8,128)(2,1)S(1)}, u32[]{:S(2)}, u32[]{:S(2)}) collective-permute-start(bf16[256,2048]{1,0:T(8,128)(2,1)S(1)} %slice.126), channel_id=1, source_target_pairs={{0,4},{1,5},{4,6},{5,7},{6,2},{7,3},{2,0},{3,1},{8,12},{9,13},{12,... | collective-permute-start | bytes 3145736 | tf_op jit(solution)/shard_map/ppermute | solution.py:44
  404.4 25.9 %collective-permute-start.30 = (bf16[256,2048]{1,0:T(8,128)(2,1)S(1)}, bf16[256,2048]{1,0:T(8,128)(2,1)}, u32[]{:S(2)}, u32[]{:S(2)}) collective-permute-start(bf16[256,2048]{1,0:T(8,128)(2,1)S(1)} %add_convert_fusion.9), channel_id=1, source_target_pairs={{0,4},{1,5},{4,6},{5,7},{6,2},{7,3},{2,0},{3,1},{8,12},{9,13},{12,... | collective-permute-start | bytes 3145736 | tf_op jit(solution)/shard_map/ppermute | solution.py:44
  425.4 299.5 %reduce-scatter.8.cloned.1.call-start = ((), (), s32[]{:S(2)}) async-start(), calls=%async_computation.6 | async-start | bytes 5242880 | tf_op jit(solution)/shard_map/reduce_scatter | solution.py:941
  431.9 25.7 %collective-permute-start.31 = (bf16[256,2048]{1,0:T(8,128)(2,1)S(1)}, bf16[256,2048]{1,0:T(8,128)(2,1)S(1)}, u32[]{:S(2)}, u32[]{:S(2)}) collective-permute-start(bf16[256,2048]{1,0:T(8,128)(2,1)S(1)} %add_convert_fusion.8), channel_id=1, source_target_pairs={{0,4},{1,5},{4,6},{5,7},{6,2},{7,3},{2,0},{3,1},{8,12},{9,13},{12,... | collective-permute-start | bytes 3145736 | tf_op jit(solution)/shard_map/ppermute | solution.py:44
  441.6 57.5 %collective-permute-start.36 = (bf16[1024,2048]{1,0:T(8,128)(2,1)}, bf16[1024,2048]{1,0:T(8,128)(2,1)}, u32[]{:S(2)}, u32[]{:S(2)}) collective-permute-start(bf16[1024,2048]{1,0:T(8,128)(2,1)} %convolution_convert_fusion.4), channel_id=1, source_target_pairs={{0,1},{1,0},{2,3},{3,2},{4,5},{5,4},{6,7},{7,6},{8,9},{9,8},{10,11... | collective-permute-start | bytes 12582920 | tf_op jit(solution)/shard_map/ppermute | solution.py:28
  447.9 59.5 %collective-permute-start.38 = (bf16[2048,1024]{1,0:T(8,128)(2,1)}, bf16[2048,1024]{1,0:T(8,128)(2,1)}, u32[]{:S(2)}, u32[]{:S(2)}) collective-permute-start(bf16[2048,1024]{1,0:T(8,128)(2,1)} %convolution_convert_fusion), channel_id=1, source_target_pairs={{0,1},{1,0},{2,3},{3,2},{4,5},{5,4},{6,7},{7,6},{8,9},{9,8},{10,11... | collective-permute-start | bytes 12582920 | tf_op jit(solution)/shard_map/ppermute | solution.py:28
  469.3 25.8 %collective-permute-start.32 = (bf16[256,2048]{1,0:T(8,128)(2,1)}, bf16[256,2048]{1,0:T(8,128)(2,1)S(1)}, u32[]{:S(2)}, u32[]{:S(2)}) collective-permute-start(bf16[256,2048]{1,0:T(8,128)(2,1)} %slice.125), channel_id=1, source_target_pairs={{0,4},{1,5},{4,6},{5,7},{6,2},{7,3},{2,0},{3,1},{8,12},{9,13},{12,... | collective-permute-start | bytes 3145736 | tf_op jit(solution)/shard_map/ppermute | solution.py:44
  486.7 83.7 %collective-permute-start.64 = (bf16[512,1024]{1,0:T(8,128)(2,1)}, bf16[512,1024]{1,0:T(8,128)(2,1)}, u32[]{:S(2)}, u32[]{:S(2)}) collective-permute-start(bf16[512,1024]{1,0:T(8,128)(2,1)} %get-tuple-element.168), channel_id=1, source_target_pairs={{0,16},{8,24},{16,0},{24,8},{1,17},{9,25},{17,1},{25,9},{2,18},{10... | collective-permute-start | bytes 3145736 | tf_op jit(solution)/shard_map/ppermute | solution.py:33
  489.2 25.9 %collective-permute-start.35 = (bf16[512,1024]{1,0:T(8,128)(2,1)}, bf16[512,1024]{1,0:T(8,128)(2,1)}, u32[]{:S(2)}, u32[]{:S(2)}) collective-permute-start(bf16[512,1024]{1,0:T(8,128)(2,1)} %get-tuple-element.144), channel_id=1, source_target_pairs={{0,1},{1,0},{2,3},{3,2},{4,5},{5,4},{6,7},{7,6},{8,9},{9,8},{10,11... | collective-permute-start | bytes 3145736 | tf_op jit(solution)/shard_map/ppermute | solution.py:28
  495.1 63.9 %collective-permute-start.65 = (bf16[512,1024]{1,0:T(8,128)(2,1)}, bf16[512,1024]{1,0:T(8,128)(2,1)}, u32[]{:S(2)}, u32[]{:S(2)}) collective-permute-start(bf16[512,1024]{1,0:T(8,128)(2,1)} %get-tuple-element.171), channel_id=1, source_target_pairs={{0,16},{8,24},{16,0},{24,8},{1,17},{9,25},{17,1},{25,9},{2,18},{10... | collective-permute-start | bytes 3145736 | tf_op jit(solution)/shard_map/ppermute | solution.py:33
  499.1 50.6 %collective-permute-start.34 = (bf16[256,2048]{1,0:T(8,128)(2,1)}, bf16[256,2048]{1,0:T(8,128)(2,1)S(1)}, u32[]{:S(2)}, u32[]{:S(2)}) collective-permute-start(bf16[256,2048]{1,0:T(8,128)(2,1)} %add_convert_fusion.7), channel_id=1, source_target_pairs={{0,4},{1,5},{4,6},{5,7},{6,2},{7,3},{2,0},{3,1},{8,12},{9,13},{12,... | collective-permute-start | bytes 3145736 | tf_op jit(solution)/shard_map/ppermute | solution.py:44
  507.3 220.4 %reduce-scatter.6.cloned.1.call-start = ((), (), s32[]{:S(2)}) async-start(), calls=%async_computation.5 | async-start | bytes 5242880 | tf_op jit(solution)/shard_map/reduce_scatter | solution.py:941
  557.2 37.5 %collective-permute-start.51 = (bf16[512,1024]{1,0:T(8,128)(2,1)}, bf16[512,1024]{1,0:T(8,128)(2,1)S(1)}, u32[]{:S(2)}, u32[]{:S(2)}) collective-permute-start(bf16[512,1024]{1,0:T(8,128)(2,1)} %get-tuple-element.159), channel_id=1, source_target_pairs={{0,8},{8,0},{16,24},{24,16},{1,9},{9,1},{17,25},{25,17},{2,10},{10... | collective-permute-start | bytes 3145736 | tf_op jit(solution)/shard_map/ppermute | solution.py:33
  568.3 49.0 %collective-permute-start.66 = (bf16[512,1024]{1,0:T(8,128)(2,1)}, bf16[512,1024]{1,0:T(8,128)(2,1)}, u32[]{:S(2)}, u32[]{:S(2)}) collective-permute-start(bf16[512,1024]{1,0:T(8,128)(2,1)} %add_convert_fusion.3), channel_id=1, source_target_pairs={{0,8},{8,0},{16,24},{24,16},{1,9},{9,1},{17,25},{25,17},{2,10},{10... | collective-permute-start | bytes 3145736 | tf_op jit(solution)/shard_map/ppermute | solution.py:33
  570.3 71.4 %collective-permute-start.50 = (bf16[512,1024]{1,0:T(8,128)(2,1)}, bf16[512,1024]{1,0:T(8,128)(2,1)}, u32[]{:S(2)}, u32[]{:S(2)}) collective-permute-start(bf16[512,1024]{1,0:T(8,128)(2,1)} %get-tuple-element.157), channel_id=1, source_target_pairs={{0,8},{8,0},{16,24},{24,16},{1,9},{9,1},{17,25},{25,17},{2,10},{10... | collective-permute-start | bytes 3145736 | tf_op jit(solution)/shard_map/ppermute | solution.py:33
  577.8 44.5 %collective-permute-start.42 = (bf16[512,512]{1,0:T(8,128)(2,1)S(1)}, bf16[512,512]{1,0:T(8,128)(2,1)S(1)}, u32[]{:S(2)}, u32[]{:S(2)}) collective-permute-start(bf16[512,512]{1,0:T(8,128)(2,1)S(1)} %add_convert_fusion.11), channel_id=1, source_target_pairs={{0,4},{1,5},{4,6},{5,7},{6,2},{7,3},{2,0},{3,1},{8,12},{9,13},{12,... | collective-permute-start | bytes 1572872 | tf_op jit(solution)/shard_map/ppermute | solution.py:44
  596.1 56.6 %collective-permute-start.52 = (bf16[512,1024]{1,0:T(8,128)(2,1)}, bf16[512,1024]{1,0:T(8,128)(2,1)}, u32[]{:S(2)}, u32[]{:S(2)}) collective-permute-start(bf16[512,1024]{1,0:T(8,128)(2,1)} %add_convert_fusion.4), channel_id=1, source_target_pairs={{0,16},{8,24},{16,0},{24,8},{1,17},{9,25},{17,1},{25,9},{2,18},{10... | collective-permute-start | bytes 3145736 | tf_op jit(solution)/shard_map/ppermute | solution.py:33
  640.7 29.8 %collective-permute-start.41 = (bf16[256,2048]{1,0:T(8,128)(2,1)}, bf16[256,2048]{1,0:T(8,128)(2,1)S(1)}, u32[]{:S(2)}, u32[]{:S(2)}) collective-permute-start(bf16[256,2048]{1,0:T(8,128)(2,1)} %add_convert_fusion.6), channel_id=1, source_target_pairs={{0,4},{1,5},{4,6},{5,7},{6,2},{7,3},{2,0},{3,1},{8,12},{9,13},{12,... | collective-permute-start | bytes 3145736 | tf_op jit(solution)/shard_map/ppermute | solution.py:44
  641.7 55.9 %collective-permute-start.43 = (f32[256,2048]{1,0:T(8,128)}, f32[256,2048]{1,0:T(8,128)S(1)}, u32[]{:S(2)}, u32[]{:S(2)}) collective-permute-start(f32[256,2048]{1,0:T(8,128)} %get-tuple-element.155), channel_id=1, source_target_pairs={{0,1},{1,0},{2,3},{3,2},{4,5},{5,4},{6,7},{7,6},{8,9},{9,8},{10,11... | collective-permute-start | bytes 6291464 | tf_op jit(solution)/shard_map/ppermute | solution.py:28
  652.7 26.7 %collective-permute-start.59 = (bf16[512,512]{1,0:T(8,128)(2,1)S(1)}, bf16[512,512]{1,0:T(8,128)(2,1)S(1)}, u32[]{:S(2)}, u32[]{:S(2)}) collective-permute-start(bf16[512,512]{1,0:T(8,128)(2,1)S(1)} %add_convert_fusion.10), channel_id=1, source_target_pairs={{0,8},{8,0},{16,24},{24,16},{1,9},{9,1},{17,25},{25,17},{2,10},{10... | collective-permute-start | bytes 1572872 | tf_op jit(solution)/shard_map/ppermute | solution.py:33
  (104 other events, 1561.3 us)
Sparse Core Ops, SparseCore 0:
  136.9 121.3 all-gather.1
  425.5 55.0 reduce-scatter.3
  507.5 84.3 reduce-scatter.7
  641.8 61.9 reduce-scatter.5

commit v4 on v3

--- a/solution.py
+++ b/solution.py
@@ -775,7 +775,10 @@
             pl.BlockSpec((block, dkv.shape[1]), lambda j: (j, kv_at)),
         ],
         out_specs=[part, part],
-        out_shape=[jax.ShapeDtypeStruct((rows // 2, depth), F32)] * 2,
+        out_shape=[
+            jax.ShapeDtypeStruct((rows // 2, depth), F32),
+            jax.ShapeDtypeStruct((rows // 2, depth), BF16),
+        ],
         scratch_shapes=[pltpu.VMEM((rows, block), F32)],
         compiler_params=PARAMS,
         cost_estimate=cost(2 * rows * depth * width, 2 * depth * width + 4 * rows * depth),
@@ -1015,7 +1018,7 @@
     d_kv = unrotate(passing[-1], d_kv_slots[0], cosine_all, sine_all)
     d_normed_a, d_normed_oth = d_normed_rows(core_ref, d_query, d_kv, attn_w, out_half, batches)
     d_kv = after(d_kv, d_normed_oth)
-    d_normed_a = d_normed_a + swap_core(d_normed_oth)
+    d_normed_a = d_normed_a + swap_core(d_normed_oth).astype(F32)
     x_own_f = x_own.astype(F32)
     inverse_a = rms_inverse(x_own_f)
     back_a, gain_a_part = rms_back(d_normed_a, x_own_f * inverse_a, inverse_a, gain_a)

time: 746 us -> 742 us (level)
  waiting for transfers between devices: 268 us -> 260 us
  transfers between devices with their start and end apart: 75 -> 75, of which waited for: 39 -> 38; matrix products, arithmetic and copies ran while one was open for 15% -> 15% of each run, Pallas kernels for 28% -> 28%
where the time goes in v4:
time: 742 us; the launch traced here: 733 us
  waiting for transfers between devices  260 us (35%)
  Pallas kernels  227 us (31%)
  starting transfers between devices  96.5 us (13%)
  other arithmetic  72.5 us (10%)
  matrix products  43 us (6%)
  local copies, waits for them, and re-layouts  18.4 us (2%)
  between operations  14.9 us (2%)
    ppermute x33, waiting for transfers between devices, ring_step(): return lax.ppermute(array, 'ctx', pairs)  177 us
    ppermute x23, waiting for transfers between devices, swap_seq(): return lax.ppermute(array, 'seq', [(i, i ^ bit) for i in range(seq)])  79.1 us
    ppermute x33, starting transfers between devices, ring_step(): return lax.ppermute(array, 'ctx', pairs)  63.1 us
    pallas_call x4, Pallas kernels, hidden_group(): pl.pallas_call(kernel, grid=(tiles,), in_specs=source_specs + [pl.BlockSp...  52.9 us
    dot_general x6, matrix products, rows_product(): jnp.einsum('ri,rj->ij', left, right, preferred_element_type=F32)  43 us
    pallas_call x2, Pallas kernels, mlp_back(): pl.pallas_call(mlp_back_kernel, grid=(1,), in_specs=[pl.BlockSpec((height...  41.6 us
    pallas_call x1, Pallas kernels, attend_back(): pl.pallas_call(functools.partial(attend_back_kernel, chips), grid_spec=pl...  34.6 us
    ppermute x23, starting transfers between devices, swap_seq(): return lax.ppermute(array, 'seq', [(i, i ^ bit) for i in range(seq)])  30.9 us
  transfers between devices with their start and end apart: 75, of which 38 were waited for; matrix products, arithmetic and copies ran while one was open for 15% of the time, Pallas kernels for 28%

profile of v4, /device:TPU:0, one launch (start us, length us, event | category | flops | bytes accessed | tf_op | source)
XLA Modules:
  0.0 732.6 jit_solution(638213078066893672)
XLA Ops:
  21.9 15.5 %collective-permute-done.2.refs_3_ = bf16[256,2048]{1,0:T(8,128)(2,1)} collective-permute-done((bf16[256,2048]{1,0:T(8,128)(2,1)S(1)}, bf16[256,2048]{1,0:T(8,128)(2,1)}, u32[]{:S(2)}, u32[]{:S(2)}) %collective-permute-start.2) | collective-permute-done | bytes 1048608 | tf_op jit(solution)/shard_map/ppermute | solution.py:44
  43.9 11.9 %collective-permute-done.3.refs_7_ = bf16[128,2688]{1,0:T(8,128)(2,1)S(1)} collective-permute-done((bf16[128,2688]{1,0:T(8,128)(2,1)}, bf16[128,2688]{1,0:T(8,128)(2,1)S(1)}, u32[]{:S(2)}, u32[]{:S(2)}) %collective-permute-start.3) | collective-permute-done | bytes 688160 | tf_op jit(solution)/shard_map/ppermute | solution.py:44
  62.1 12.6 %collective-permute-done.6.refs_8_ = bf16[128,2688]{1,0:T(8,128)(2,1)} collective-permute-done((bf16[128,2688]{1,0:T(8,128)(2,1)S(1)}, bf16[128,2688]{1,0:T(8,128)(2,1)}, u32[]{:S(2)}, u32[]{:S(2)}) %collective-permute-start.6) | collective-permute-done | bytes 688160 | tf_op jit(solution)/shard_map/ppermute | solution.py:44
  79.6 11.6 %collective-permute-done.9.refs_9_ = bf16[128,2688]{1,0:T(8,128)(2,1)} collective-permute-done((bf16[128,2688]{1,0:T(8,128)(2,1)}, bf16[128,2688]{1,0:T(8,128)(2,1)}, u32[]{:S(2)}, u32[]{:S(2)}) %collective-permute-start.9) | collective-permute-done | bytes 688160 | tf_op jit(solution)/shard_map/ppermute | solution.py:44
  96.8 13.1 %collective-permute-done.13.refs_17_ = bf16[128,2688]{1,0:T(8,128)(2,1)} collective-permute-done((bf16[128,2688]{1,0:T(8,128)(2,1)}, bf16[128,2688]{1,0:T(8,128)(2,1)}, u32[]{:S(2)}, u32[]{:S(2)}) %collective-permute-start.13) | collective-permute-done | bytes 688160 | tf_op jit(solution)/shard_map/ppermute | solution.py:33
  113.9 10.7 %collective-permute-done.12.refs_16_ = bf16[128,2688]{1,0:T(8,128)(2,1)} collective-permute-done((bf16[128,2688]{1,0:T(8,128)(2,1)}, bf16[128,2688]{1,0:T(8,128)(2,1)}, u32[]{:S(2)}, u32[]{:S(2)}) %collective-permute-start.12) | collective-permute-done | bytes 688160 | tf_op jit(solution)/shard_map/ppermute | solution.py:33
  126.7 8.6 %collective-permute-done.16.refs_20_ = bf16[128,2688]{1,0:T(8,128)(2,1)} collective-permute-done((bf16[128,2688]{1,0:T(8,128)(2,1)}, bf16[128,2688]{1,0:T(8,128)(2,1)}, u32[]{:S(2)}, u32[]{:S(2)}) %collective-permute-start.16) | collective-permute-done | bytes 688160 | tf_op jit(solution)/shard_map/ppermute | solution.py:33
  140.6 13.6 %shard_map.205 = (bf16[512,512]{1,0:T(8,128)(2,1)}, bf16[512,2048]{1,0:T(8,128)(2,1)}, f32[8,2048]{1,0:T(8,128)}, bf16[2048,2688]{1,0:T(8,128)(2,1)}) custom-call(s32[1]{0:T(128)} %bitcast.1.core_ref.refs_0_, s32[16]{0:T(128)} %mul.187.refs_1_.starts, bf16[256,2048]{1,0:T(8,128)(2,1)} %bitcast.68, bf16[256,2048]{1,0:T(8,128)(2,1)} %collective-permute-done.refs_3_, ...), custom_call_target="tpu_custom_call" | custom-call | flops 33822867456 | bytes 26214400 | tf_op jit(solution)/shard_map/pallas_call | solution.py:246
  156.4 9.6 %collective-permute-done.18.refs_1_ = bf16[512,512]{1,0:T(8,128)(2,1)S(1)} collective-permute-done((bf16[512,512]{1,0:T(8,128)(2,1)}, bf16[512,512]{1,0:T(8,128)(2,1)S(1)}, u32[]{:S(2)}, u32[]{:S(2)}) %collective-permute-start.18) | collective-permute-done | bytes 524320 | tf_op jit(solution)/shard_map/ppermute | solution.py:44
  170.9 8.6 %collective-permute-done.19.refs_2_ = bf16[512,512]{1,0:T(8,128)(2,1)S(1)} collective-permute-done((bf16[512,512]{1,0:T(8,128)(2,1)S(1)}, bf16[512,512]{1,0:T(8,128)(2,1)S(1)}, u32[]{:S(2)}, u32[]{:S(2)}) %collective-permute-start.19) | collective-permute-done | bytes 524320 | tf_op jit(solution)/shard_map/ppermute | solution.py:44
  182.9 9.7 %shard_map.206.q_ref = bf16[512,1024]{1,0:T(8,128)(2,1)} custom-call(bf16[512,2048]{1,0:T(8,128)(2,1)} %get-tuple-element.98.normed.refs_0_, f32[512,128]{1,0:T(8,128)} %bitcast.75, f32[512,128]{1,0:T(8,128)} %bitcast.78, bf16[2048,2688]{1,0:T(8,128)(2,1)} %get-tuple-element.141.w.w_all.w_ref.wq_ref.wkv_ref), custom_call_target="tpu_custom_call" | custom-call | flops 12884901888 | bytes 10485760 | tf_op jit(solution)/shard_map/pallas_call | solution.py:287
  197.5 25.9 %shard_map.207 = (bf16[512,1024]{1,0:T(8,128)(2,1)}, f32[32,256]{1,0:T(8,128)}) custom-call(s32[2]{0:T(128)} %bitcast.97, s32[1024,1]{1,0:T(8,128)} %bitcast.80, s32[1,256]{1,0:T(1,128)} %iota_add_fusion.qpos_ref, bf16[512,1024]{1,0:T(8,128)(2,1)} %shard_map.206.q_ref, bf16[512,512]{1,0:T(8,128)(2,1)} %get-tuple-element.100.refs_0_, ...), custom_call_target="tpu_custom_call" | custom-call | flops 51539607552 | bytes 4194304 | tf_op jit(solution)/shard_map/pallas_call | solution.py:352
  227.4 9.1 %shard_map.208 = (f32[256,1024]{1,0:T(8,128)}, f32[256,1024]{1,0:T(8,128)}) custom-call(s32[1]{0:T(128)} %bitcast.1.core_ref.refs_0_, bf16[512,1024]{1,0:T(8,128)(2,1)} %get-tuple-element.103.o_mine.refs_0_, bf16[512,1024]{1,0:T(8,128)(2,1)} %copy-done.40, bf16[2048,2688]{1,0:T(8,128)(2,1)} %get-tuple-element.141.w.w_all.w_ref.wq_ref.wkv_ref), custom_call_target="tpu_custom_call" | custom-call | flops 12884901888 | bytes 10485760 | tf_op jit(solution)/shard_map/pallas_call | solution.py:502
  238.3 11.1 %collective-permute-done.24.refs_3_ = bf16[256,2048]{1,0:T(8,128)(2,1)} collective-permute-done((bf16[256,2048]{1,0:T(8,128)(2,1)}, bf16[256,2048]{1,0:T(8,128)(2,1)}, u32[]{:S(2)}, u32[]{:S(2)}) %collective-permute-start.24) | collective-permute-done | bytes 1048608 | tf_op jit(solution)/shard_map/ppermute | solution.py:44
  256.7 23.2 %collective-permute-done.25.refs_2_ = bf16[256,2048]{1,0:T(8,128)(2,1)S(1)} collective-permute-done((bf16[256,2048]{1,0:T(8,128)(2,1)S(1)}, bf16[256,2048]{1,0:T(8,128)(2,1)S(1)}, u32[]{:S(2)}, u32[]{:S(2)}) %collective-permute-start.25) | collective-permute-done | bytes 1048608 | tf_op jit(solution)/shard_map/ppermute | solution.py:44
  282.4 14.1 %shard_map.209 = (bf16[1024,2048]{1,0:T(8,128)(2,1)}, bf16[1024,2048]{1,0:T(8,128)(2,1)}, bf16[1024,1024]{1,0:T(8,128)(2,1)}, bf16[1024,1024]{1,0:T(8,128)(2,1)}, bf16[1024,1024]{1,0:T(8,128)(2,1)}) custom-call(bf16[256,2048]{1,0:T(8,128)(2,1)} %copy-done.21, bf16[256,2048]{1,0:T(8,128)(2,1)} %copy-done.19, bf16[256,2048]{1,0:T(8,128)(2,1)} %copy-done.43, ...), custom_call_target="tpu_custom_call" | custom-call | flops 38654705664 | bytes 25165824 | tf_op jit(solution)/shard_map/pallas_call | solution.py:582
  296.5 9.0 %collective-permute-done.26.refs_0_ = bf16[256,2048]{1,0:T(8,128)(2,1)S(1)} collective-permute-done((bf16[256,2048]{1,0:T(8,128)(2,1)S(1)}, bf16[256,2048]{1,0:T(8,128)(2,1)S(1)}, u32[]{:S(2)}, u32[]{:S(2)}) %collective-permute-start.26) | collective-permute-done | bytes 1048608 | tf_op jit(solution)/shard_map/ppermute | solution.py:44
  309.2 12.3 %shard_map.210 = (bf16[1024,1024]{1,0:T(8,128)(2,1)}, bf16[1024,1024]{1,0:T(8,128)(2,1)}, bf16[1024,1024]{1,0:T(8,128)(2,1)}) custom-call(bf16[1024,2048]{1,0:T(8,128)(2,1)} %get-tuple-element.113.x.refs_7_, bf16[1024,2048]{1,0:T(8,128)(2,1)} %get-tuple-element.114.d.refs_8_, bf16[2048,3072]{1,0:T(8,128)(2,1)} %collective-permute-done.27.gate.up.down_t.refs_7_, ...), custom_call_target="tpu_custom_call" | custom-call | flops 38654705664 | bytes 25165824 | tf_op jit(solution)/shard_map/pallas_call | solution.py:582
  321.5 20.8 %shard_map.211 = (bf16[512,2048]{1,0:T(8,128)(2,1)}, bf16[512,2048]{1,0:T(8,128)(2,1)}) custom-call(bf16[1024,1024]{1,0:T(8,128)(2,1)} %get-tuple-element.110.refs_0_.refs_9_, bf16[1024,1024]{1,0:T(8,128)(2,1)} %get-tuple-element.111.refs_1_.refs_10_, bf16[1024,1024]{1,0:T(8,128)(2,1)} %get-tuple-element.112.refs_2_.refs_11_, ...), custom_call_target="tpu_custom_call" | custom-call | flops 77309411328 | bytes 39845888 | tf_op jit(solution)/shard_map/pallas_call | solution.py:639
  344.7 14.2 %shard_map.212 = (bf16[1024,2048]{1,0:T(8,128)(2,1)}, bf16[1024,2048]{1,0:T(8,128)(2,1)}, bf16[1024,1024]{1,0:T(8,128)(2,1)}, bf16[1024,1024]{1,0:T(8,128)(2,1)}, bf16[1024,1024]{1,0:T(8,128)(2,1)}) custom-call(bf16[256,2048]{1,0:T(8,128)(2,1)} %copy-done.41, ...), custom_call_target="tpu_custom_call", output_to_operand_aliasing={{0}: (7, {}), {1}: (8, {}), {2}: (9, {}), {3}: (10, {}), {4... | custom-call | flops 38654705664 | bytes 25165824 | tf_op jit(solution)/shard_map/pallas_call | solution.py:582
  359.0 12.3 %shard_map.213 = (bf16[1024,1024]{1,0:T(8,128)(2,1)}, bf16[1024,1024]{1,0:T(8,128)(2,1)}, bf16[1024,1024]{1,0:T(8,128)(2,1)}) custom-call(bf16[1024,2048]{1,0:T(8,128)(2,1)} %get-tuple-element.136.x, bf16[1024,2048]{1,0:T(8,128)(2,1)} %get-tuple-element.135.d, ...), custom_call_target="tpu_custom_call", output_to_operand_aliasing={{0}: (5, {}), {1}: (6, {}), {2}: (7, {})} | custom-call | flops 38654705664 | bytes 25165824 | tf_op jit(solution)/shard_map/pallas_call | solution.py:582
  371.3 20.8 %shard_map.214 = (bf16[512,2048]{1,0:T(8,128)(2,1)}, bf16[512,2048]{1,0:T(8,128)(2,1)}) custom-call(bf16[1024,1024]{1,0:T(8,128)(2,1)} %get-tuple-element.134.refs_0_, bf16[1024,1024]{1,0:T(8,128)(2,1)} %get-tuple-element.137.refs_1_, bf16[1024,1024]{1,0:T(8,128)(2,1)} %get-tuple-element.139.refs_2_, bf16[1024,1024]{1,0:T(8,128)(2,1)} %get-tuple-element.128.refs_3_, ...), custom_call_target="tpu_custom_call" | custom-call | flops 77309411328 | bytes 39845888 | tf_op jit(solution)/shard_map/pallas_call | solution.py:639
  394.0 8.7 %convolution_convert_fusion.2 = bf16[2048,1024]{1,0:T(8,128)(2,1)} fusion(bf16[1024,2048]{1,0:T(8,128)(2,1)} %get-tuple-element.136.x, bf16[1024,1024]{1,0:T(8,128)(2,1)S(1)} %copy-done.59), kind=kOutput, calls=%fused_computation.5 | convolution fusion | flops 4297064448 | bytes 10485760 | tf_op jit(solution)/shard_map/ri,rj->ij/dot_general | solution.py:941
  433.6 8.0 %convolution_convert_fusion.5 = bf16[1024,2048]{1,0:T(8,128)(2,1)S(1)} fusion(bf16[1024,1024]{1,0:T(8,128)(2,1)S(1)} %copy-done.54, bf16[1024,2048]{1,0:T(8,128)(2,1)} %get-tuple-element.135.d), kind=kOutput, calls=%fused_computation.8 | convolution fusion | flops 4297064448 | bytes 10485760 | tf_op jit(solution)/shard_map/ri,rj->ij/dot_general | solution.py:941
  448.4 9.3 %collective-permute-done.31 = bf16[256,2048]{1,0:T(8,128)(2,1)S(1)} collective-permute-done((bf16[256,2048]{1,0:T(8,128)(2,1)S(1)}, bf16[256,2048]{1,0:T(8,128)(2,1)S(1)}, u32[]{:S(2)}, u32[]{:S(2)}) %collective-permute-start.31) | collective-permute-done | bytes 1048608 | tf_op jit(solution)/shard_map/ppermute | solution.py:44
  471.7 9.0 %shard_map.215 = (f32[512,1024]{1,0:T(8,128)}, bf16[512,1024]{1,0:T(8,128)(2,1)}, bf16[512,1024]{1,0:T(8,128)(2,1)}) custom-call(s32[1]{0:T(128)} %bitcast.1.core_ref.refs_0_, bf16[256,1024]{1,0:T(8,128)(2,1)} %get-tuple-element.219.d_own, bf16[256,1024]{1,0:T(8,128)(2,1)} %copy-done.52, bf16[2048,2688]{1,0:T(8,128)(2,1)} %get-tuple-element.141.w.w_all.w_ref.wq_ref.wkv_ref), custom_call_target="tpu_custom_call" | custom-call | flops 12884901888 | bytes 10485760 | tf_op jit(solution)/shard_map/pallas_call | solution.py:688
  507.4 7.6 %add_convert_fusion = bf16[2048,1024]{1,0:T(8,128)(2,1)} fusion(bf16[2048,1024]{1,0:T(8,128)(2,1)} %collective-permute-done.38, bf16[2048,1024]{1,0:T(8,128)(2,1)} %convolution_convert_fusion.1), kind=kLoop, calls=%fused_computation | loop fusion | flops 8388608 | bytes 12582912 | tf_op jit(solution)/shard_map/convert_element_type | solution.py:955
  515.0 34.6 %shard_map.216 = (bf16[512,1024]{1,0:T(8,128)(2,1)}, bf16[512,512]{1,0:T(8,128)(2,1)}, bf16[512,512]{1,0:T(8,128)(2,1)}, bf16[512,512]{1,0:T(8,128)(2,1)}, bf16[512,512]{1,0:T(8,128)(2,1)}) custom-call(s32[2]{0:T(128)} %bitcast.98, s32[1024,1]{1,0:T(8,128)} %bitcast.81, s32[1,256]{1,0:T(1,128)} %iota_add_fusion.qpos_ref, ...), custom_call_target="tpu_custom_call" | custom-call | flops 128849018880 | bytes 9437184 | tf_op jit(solution)/shard_map/pallas_call | solution.py:431
  579.6 15.1 %collective-permute-done.51 = bf16[512,1024]{1,0:T(8,128)(2,1)S(1)} collective-permute-done((bf16[512,1024]{1,0:T(8,128)(2,1)}, bf16[512,1024]{1,0:T(8,128)(2,1)S(1)}, u32[]{:S(2)}, u32[]{:S(2)}) %collective-permute-start.51) | collective-permute-done | bytes 1048608 | tf_op jit(solution)/shard_map/ppermute | solution.py:33
  596.1 21.2 %collective-permute-done.66 = bf16[512,1024]{1,0:T(8,128)(2,1)} collective-permute-done((bf16[512,1024]{1,0:T(8,128)(2,1)}, bf16[512,1024]{1,0:T(8,128)(2,1)}, u32[]{:S(2)}, u32[]{:S(2)}) %collective-permute-start.66) | collective-permute-done | bytes 1048608 | tf_op jit(solution)/shard_map/ppermute | solution.py:33
  625.5 7.7 %shard_map.218 = (f32[256,2048]{1,0:T(8,128)}, bf16[256,2048]{1,0:T(8,128)(2,1)}) custom-call(s32[1]{0:T(128)} %bitcast.1.core_ref.refs_0_, bf16[512,1024]{1,0:T(8,128)(2,1)} %get-tuple-element.151.dq_ref.refs_1_, bf16[512,512]{1,0:T(8,128)(2,1)} %shard_map.217.dkv_ref.refs_1_, bf16[2048,2688]{1,0:T(8,128)(2,1)} %get-tuple-element.141.w.w_all.w_ref.wq_ref.wkv_ref, ...), custom_call_target="tpu_custom_call" | custom-call | flops 19327352832 | bytes 10485760 | tf_op jit(solution)/shard_map/pallas_call | solution.py:767
  656.9 13.3 %collective-permute-done.41 = bf16[256,2048]{1,0:T(8,128)(2,1)S(1)} collective-permute-done((bf16[256,2048]{1,0:T(8,128)(2,1)}, bf16[256,2048]{1,0:T(8,128)(2,1)S(1)}, u32[]{:S(2)}, u32[]{:S(2)}) %collective-permute-start.41) | collective-permute-done | bytes 1048608 | tf_op jit(solution)/shard_map/ppermute | solution.py:44
  (362 shorter events, 284.7 us)
Async XLA Ops:
  7.2 272.7 %all-gather.2.cloned.1.call-start = ((), (), s32[]{:S(2)}) async-start(), calls=%async_computation.3 | async-start | bytes 15728640 | tf_op jit(solution)/shard_map/all_gather | solution.py:879
  10.6 26.7 %collective-permute-start.2 = (bf16[256,2048]{1,0:T(8,128)(2,1)S(1)}, bf16[256,2048]{1,0:T(8,128)(2,1)}, u32[]{:S(2)}, u32[]{:S(2)}) collective-permute-start(bf16[256,2048]{1,0:T(8,128)(2,1)S(1)} %fusion.12.refs_1_), channel_id=1, source_target_pairs={{0,4},{1,5},{4,6},{5,7},{6,2},{7,3},{2,0},{3,1},{8,12},{9,13},{12,... | collective-permute-start | bytes 3145736 | tf_op jit(solution)/shard_map/ppermute | solution.py:44
  92.7 31.9 %collective-permute-start.12 = (bf16[128,2688]{1,0:T(8,128)(2,1)}, bf16[128,2688]{1,0:T(8,128)(2,1)}, u32[]{:S(2)}, u32[]{:S(2)}) collective-permute-start(bf16[128,2688]{1,0:T(8,128)(2,1)} %collective-permute-done.6.refs_8_), channel_id=1, source_target_pairs={{0,16},{8,24},{16,0},{24,8},{1,17},{9,25},{17,1},{25,9},{2,18},{10... | collective-permute-start | bytes 2064392 | tf_op jit(solution)/shard_map/ppermute | solution.py:33
  93.2 31.4 %collective-permute-start.15 = (bf16[128,2688]{1,0:T(8,128)(2,1)}, bf16[128,2688]{1,0:T(8,128)(2,1)}, u32[]{:S(2)}, u32[]{:S(2)}) collective-permute-start(bf16[128,2688]{1,0:T(8,128)(2,1)} %collective-permute-done.8.refs_15_), channel_id=1, source_target_pairs={{0,8},{8,0},{16,24},{24,16},{1,9},{9,1},{17,25},{25,17},{2,10},{10... | collective-permute-start | bytes 2064392 | tf_op jit(solution)/shard_map/ppermute | solution.py:33
  93.8 32.9 %collective-permute-start.11 = (bf16[128,2688]{1,0:T(8,128)(2,1)}, bf16[128,2688]{1,0:T(8,128)(2,1)}, u32[]{:S(2)}, u32[]{:S(2)}) collective-permute-start(bf16[128,2688]{1,0:T(8,128)(2,1)} %collective-permute-done.9.refs_9_), channel_id=1, source_target_pairs={{0,8},{8,0},{16,24},{24,16},{1,9},{9,1},{17,25},{25,17},{2,10},{10... | collective-permute-start | bytes 2064392 | tf_op jit(solution)/shard_map/ppermute | solution.py:33
  95.3 40.0 %collective-permute-start.16 = (bf16[128,2688]{1,0:T(8,128)(2,1)}, bf16[128,2688]{1,0:T(8,128)(2,1)}, u32[]{:S(2)}, u32[]{:S(2)}) collective-permute-start(bf16[128,2688]{1,0:T(8,128)(2,1)} %collective-permute-done.10.refs_12_), channel_id=1, source_target_pairs={{0,16},{8,24},{16,0},{24,8},{1,17},{9,25},{17,1},{25,9},{2,18},{10... | collective-permute-start | bytes 2064392 | tf_op jit(solution)/shard_map/ppermute | solution.py:33
  109.9 26.8 %collective-permute-start.17 = (bf16[128,2688]{1,0:T(8,128)(2,1)}, bf16[128,2688]{1,0:T(8,128)(2,1)}, u32[]{:S(2)}, u32[]{:S(2)}) collective-permute-start(bf16[128,2688]{1,0:T(8,128)(2,1)} %collective-permute-done.13.refs_17_), channel_id=1, source_target_pairs={{0,8},{8,0},{16,24},{24,16},{1,9},{9,1},{17,25},{25,17},{2,10},{10... | collective-permute-start | bytes 2064392 | tf_op jit(solution)/shard_map/ppermute | solution.py:33
  136.8 580.6 %reduce-scatter.4.cloned.1.call-start = ((), (), s32[]{:S(2)}) async-start(), calls=%async_computation.4 | async-start | bytes 5242880 | tf_op jit(solution)/shard_map/reduce_scatter | solution.py:944
  193.9 29.5 %collective-permute-start.21 = (bf16[256,2048]{1,0:T(8,128)(2,1)}, bf16[256,2048]{1,0:T(8,128)(2,1)}, u32[]{:S(2)}, u32[]{:S(2)}) collective-permute-start(bf16[256,2048]{1,0:T(8,128)(2,1)} %collective-permute-done.2.refs_3_), channel_id=1, source_target_pairs={{0,4},{1,5},{4,6},{5,7},{6,2},{7,3},{2,0},{3,1},{8,12},{9,13},{12,... | collective-permute-start | bytes 3145736 | tf_op jit(solution)/shard_map/ppermute | solution.py:44
  223.5 25.9 %collective-permute-start.24 = (bf16[256,2048]{1,0:T(8,128)(2,1)}, bf16[256,2048]{1,0:T(8,128)(2,1)}, u32[]{:S(2)}, u32[]{:S(2)}) collective-permute-start(bf16[256,2048]{1,0:T(8,128)(2,1)} %collective-permute-done.21.refs_1_), channel_id=1, source_target_pairs={{0,4},{1,5},{4,6},{5,7},{6,2},{7,3},{2,0},{3,1},{8,12},{9,13},{12,... | collective-permute-start | bytes 3145736 | tf_op jit(solution)/shard_map/ppermute | solution.py:44
  279.9 29.3 %collective-permute-start.27 = (bf16[2048,3072]{1,0:T(8,128)(2,1)}, bf16[2048,3072]{1,0:T(8,128)(2,1)}, u32[]{:S(2)}, u32[]{:S(2)}) collective-permute-start(bf16[2048,3072]{1,0:T(8,128)(2,1)} %all-gather.2.cloned.1.call-done.refs_4_.refs_5_.refs_6_), channel_id=1, source_target_pairs={{0,1},{1,0},{2,3},{3,2},{4,5},{5,4},{6,7},{7,6},{8,9},{9,8},{10,11... | collective-permute-start | bytes 37748744 | tf_op jit(solution)/shard_map/ppermute | solution.py:28
  305.5 38.2 %collective-permute-start.29 = (bf16[256,2048]{1,0:T(8,128)(2,1)S(1)}, bf16[256,2048]{1,0:T(8,128)(2,1)S(1)}, u32[]{:S(2)}, u32[]{:S(2)}) collective-permute-start(bf16[256,2048]{1,0:T(8,128)(2,1)S(1)} %collective-permute-done.26.refs_0_), channel_id=1, source_target_pairs={{0,4},{1,5},{4,6},{5,7},{6,2},{7,3},{2,0},{3,1},{8,12},{9,13},{12,... | collective-permute-start | bytes 3145736 | tf_op jit(solution)/shard_map/ppermute | solution.py:44
  343.6 27.6 %collective-permute-start.28 = (bf16[256,2048]{1,0:T(8,128)(2,1)S(1)}, bf16[256,2048]{1,0:T(8,128)(2,1)S(1)}, u32[]{:S(2)}, u32[]{:S(2)}) collective-permute-start(bf16[256,2048]{1,0:T(8,128)(2,1)S(1)} %slice.126), channel_id=1, source_target_pairs={{0,4},{1,5},{4,6},{5,7},{6,2},{7,3},{2,0},{3,1},{8,12},{9,13},{12,... | collective-permute-start | bytes 3145736 | tf_op jit(solution)/shard_map/ppermute | solution.py:44
  404.4 25.9 %collective-permute-start.30 = (bf16[256,2048]{1,0:T(8,128)(2,1)S(1)}, bf16[256,2048]{1,0:T(8,128)(2,1)}, u32[]{:S(2)}, u32[]{:S(2)}) collective-permute-start(bf16[256,2048]{1,0:T(8,128)(2,1)S(1)} %add_convert_fusion.9), channel_id=1, source_target_pairs={{0,4},{1,5},{4,6},{5,7},{6,2},{7,3},{2,0},{3,1},{8,12},{9,13},{12,... | collective-permute-start | bytes 3145736 | tf_op jit(solution)/shard_map/ppermute | solution.py:44
  425.4 294.8 %reduce-scatter.8.cloned.1.call-start = ((), (), s32[]{:S(2)}) async-start(), calls=%async_computation.6 | async-start | bytes 5242880 | tf_op jit(solution)/shard_map/reduce_scatter | solution.py:944
  441.6 57.5 %collective-permute-start.36 = (bf16[1024,2048]{1,0:T(8,128)(2,1)}, bf16[1024,2048]{1,0:T(8,128)(2,1)}, u32[]{:S(2)}, u32[]{:S(2)}) collective-permute-start(bf16[1024,2048]{1,0:T(8,128)(2,1)} %convolution_convert_fusion.4), channel_id=1, source_target_pairs={{0,1},{1,0},{2,3},{3,2},{4,5},{5,4},{6,7},{7,6},{8,9},{9,8},{10,11... | collective-permute-start | bytes 12582920 | tf_op jit(solution)/shard_map/ppermute | solution.py:28
  447.9 59.5 %collective-permute-start.38 = (bf16[2048,1024]{1,0:T(8,128)(2,1)}, bf16[2048,1024]{1,0:T(8,128)(2,1)}, u32[]{:S(2)}, u32[]{:S(2)}) collective-permute-start(bf16[2048,1024]{1,0:T(8,128)(2,1)} %convolution_convert_fusion), channel_id=1, source_target_pairs={{0,1},{1,0},{2,3},{3,2},{4,5},{5,4},{6,7},{7,6},{8,9},{9,8},{10,11... | collective-permute-start | bytes 12582920 | tf_op jit(solution)/shard_map/ppermute | solution.py:28
  469.3 25.8 %collective-permute-start.32 = (bf16[256,2048]{1,0:T(8,128)(2,1)}, bf16[256,2048]{1,0:T(8,128)(2,1)S(1)}, u32[]{:S(2)}, u32[]{:S(2)}) collective-permute-start(bf16[256,2048]{1,0:T(8,128)(2,1)} %slice.125), channel_id=1, source_target_pairs={{0,4},{1,5},{4,6},{5,7},{6,2},{7,3},{2,0},{3,1},{8,12},{9,13},{12,... | collective-permute-start | bytes 3145736 | tf_op jit(solution)/shard_map/ppermute | solution.py:44
  486.7 83.7 %collective-permute-start.64 = (bf16[512,1024]{1,0:T(8,128)(2,1)}, bf16[512,1024]{1,0:T(8,128)(2,1)}, u32[]{:S(2)}, u32[]{:S(2)}) collective-permute-start(bf16[512,1024]{1,0:T(8,128)(2,1)} %get-tuple-element.168), channel_id=1, source_target_pairs={{0,16},{8,24},{16,0},{24,8},{1,17},{9,25},{17,1},{25,9},{2,18},{10... | collective-permute-start | bytes 3145736 | tf_op jit(solution)/shard_map/ppermute | solution.py:33
  489.1 25.9 %collective-permute-start.35 = (bf16[512,1024]{1,0:T(8,128)(2,1)}, bf16[512,1024]{1,0:T(8,128)(2,1)}, u32[]{:S(2)}, u32[]{:S(2)}) collective-permute-start(bf16[512,1024]{1,0:T(8,128)(2,1)} %get-tuple-element.144), channel_id=1, source_target_pairs={{0,1},{1,0},{2,3},{3,2},{4,5},{5,4},{6,7},{7,6},{8,9},{9,8},{10,11... | collective-permute-start | bytes 3145736 | tf_op jit(solution)/shard_map/ppermute | solution.py:28
  495.1 63.9 %collective-permute-start.65 = (bf16[512,1024]{1,0:T(8,128)(2,1)}, bf16[512,1024]{1,0:T(8,128)(2,1)}, u32[]{:S(2)}, u32[]{:S(2)}) collective-permute-start(bf16[512,1024]{1,0:T(8,128)(2,1)} %get-tuple-element.171), channel_id=1, source_target_pairs={{0,16},{8,24},{16,0},{24,8},{1,17},{9,25},{17,1},{25,9},{2,18},{10... | collective-permute-start | bytes 3145736 | tf_op jit(solution)/shard_map/ppermute | solution.py:33
  499.1 50.6 %collective-permute-start.34 = (bf16[256,2048]{1,0:T(8,128)(2,1)}, bf16[256,2048]{1,0:T(8,128)(2,1)S(1)}, u32[]{:S(2)}, u32[]{:S(2)}) collective-permute-start(bf16[256,2048]{1,0:T(8,128)(2,1)} %add_convert_fusion.7), channel_id=1, source_target_pairs={{0,4},{1,5},{4,6},{5,7},{6,2},{7,3},{2,0},{3,1},{8,12},{9,13},{12,... | collective-permute-start | bytes 3145736 | tf_op jit(solution)/shard_map/ppermute | solution.py:44
  507.3 215.7 %reduce-scatter.6.cloned.1.call-start = ((), (), s32[]{:S(2)}) async-start(), calls=%async_computation.5 | async-start | bytes 5242880 | tf_op jit(solution)/shard_map/reduce_scatter | solution.py:944
  557.2 37.5 %collective-permute-start.51 = (bf16[512,1024]{1,0:T(8,128)(2,1)}, bf16[512,1024]{1,0:T(8,128)(2,1)S(1)}, u32[]{:S(2)}, u32[]{:S(2)}) collective-permute-start(bf16[512,1024]{1,0:T(8,128)(2,1)} %get-tuple-element.159), channel_id=1, source_target_pairs={{0,8},{8,0},{16,24},{24,16},{1,9},{9,1},{17,25},{25,17},{2,10},{10... | collective-permute-start | bytes 3145736 | tf_op jit(solution)/shard_map/ppermute | solution.py:33
  568.3 49.0 %collective-permute-start.66 = (bf16[512,1024]{1,0:T(8,128)(2,1)}, bf16[512,1024]{1,0:T(8,128)(2,1)}, u32[]{:S(2)}, u32[]{:S(2)}) collective-permute-start(bf16[512,1024]{1,0:T(8,128)(2,1)} %add_convert_fusion.3), channel_id=1, source_target_pairs={{0,8},{8,0},{16,24},{24,16},{1,9},{9,1},{17,25},{25,17},{2,10},{10... | collective-permute-start | bytes 3145736 | tf_op jit(solution)/shard_map/ppermute | solution.py:33
  570.3 71.1 %collective-permute-start.50 = (bf16[512,1024]{1,0:T(8,128)(2,1)}, bf16[512,1024]{1,0:T(8,128)(2,1)}, u32[]{:S(2)}, u32[]{:S(2)}) collective-permute-start(bf16[512,1024]{1,0:T(8,128)(2,1)} %get-tuple-element.157), channel_id=1, source_target_pairs={{0,8},{8,0},{16,24},{24,16},{1,9},{9,1},{17,25},{25,17},{2,10},{10... | collective-permute-start | bytes 3145736 | tf_op jit(solution)/shard_map/ppermute | solution.py:33
  577.8 44.5 %collective-permute-start.42 = (bf16[512,512]{1,0:T(8,128)(2,1)S(1)}, bf16[512,512]{1,0:T(8,128)(2,1)S(1)}, u32[]{:S(2)}, u32[]{:S(2)}) collective-permute-start(bf16[512,512]{1,0:T(8,128)(2,1)S(1)} %add_convert_fusion.11), channel_id=1, source_target_pairs={{0,4},{1,5},{4,6},{5,7},{6,2},{7,3},{2,0},{3,1},{8,12},{9,13},{12,... | collective-permute-start | bytes 1572872 | tf_op jit(solution)/shard_map/ppermute | solution.py:44
  596.1 56.4 %collective-permute-start.52 = (bf16[512,1024]{1,0:T(8,128)(2,1)}, bf16[512,1024]{1,0:T(8,128)(2,1)}, u32[]{:S(2)}, u32[]{:S(2)}) collective-permute-start(bf16[512,1024]{1,0:T(8,128)(2,1)} %add_convert_fusion.4), channel_id=1, source_target_pairs={{0,16},{8,24},{16,0},{24,8},{1,17},{9,25},{17,1},{25,9},{2,18},{10... | collective-permute-start | bytes 3145736 | tf_op jit(solution)/shard_map/ppermute | solution.py:33
  640.4 29.8 %collective-permute-start.41 = (bf16[256,2048]{1,0:T(8,128)(2,1)}, bf16[256,2048]{1,0:T(8,128)(2,1)S(1)}, u32[]{:S(2)}, u32[]{:S(2)}) collective-permute-start(bf16[256,2048]{1,0:T(8,128)(2,1)} %add_convert_fusion.6), channel_id=1, source_target_pairs={{0,4},{1,5},{4,6},{5,7},{6,2},{7,3},{2,0},{3,1},{8,12},{9,13},{12,... | collective-permute-start | bytes 3145736 | tf_op jit(solution)/shard_map/ppermute | solution.py:44
  641.4 32.0 %collective-permute-start.43 = (bf16[256,2048]{1,0:T(8,128)(2,1)}, bf16[256,2048]{1,0:T(8,128)(2,1)S(1)}, u32[]{:S(2)}, u32[]{:S(2)}) collective-permute-start(bf16[256,2048]{1,0:T(8,128)(2,1)} %get-tuple-element.155), channel_id=1, source_target_pairs={{0,1},{1,0},{2,3},{3,2},{4,5},{5,4},{6,7},{7,6},{8,9},{9,8},{10,11... | collective-permute-start | bytes 3145736 | tf_op jit(solution)/shard_map/ppermute | solution.py:28
  652.5 26.7 %collective-permute-start.59 = (bf16[512,512]{1,0:T(8,128)(2,1)S(1)}, bf16[512,512]{1,0:T(8,128)(2,1)S(1)}, u32[]{:S(2)}, u32[]{:S(2)}) collective-permute-start(bf16[512,512]{1,0:T(8,128)(2,1)S(1)} %add_convert_fusion.10), channel_id=1, source_target_pairs={{0,8},{8,0},{16,24},{24,16},{1,9},{9,1},{17,25},{25,17},{2,10},{10... | collective-permute-start | bytes 1572872 | tf_op jit(solution)/shard_map/ppermute | solution.py:33
  673.3 27.0 %collective-permute-start.70 = (f32[64,1024]{1,0:T(8,128)S(1)}, f32[64,1024]{1,0:T(8,128)S(1)}, u32[]{:S(2)}, u32[]{:S(2)}) collective-permute-start(f32[64,1024]{1,0:T(8,128)S(1)} %get-tuple-element.221), channel_id=1, source_target_pairs={{0,1},{1,0},{2,3},{3,2},{4,5},{5,4},{6,7},{7,6},{8,9},{9,8},{10,11... | collective-permute-start | bytes 786440 | tf_op jit(solution)/shard_map/ppermute | solution.py:28
  (104 other events, 1542.3 us)
Sparse Core Ops, SparseCore 0:
  136.9 121.3 all-gather.1
  425.5 55.0 reduce-scatter.3
  507.5 84.3 reduce-scatter.7
  641.5 62.3 reduce-scatter.5

commit v5 on v4

--- a/solution.py
+++ b/solution.py
@@ -889,21 +889,19 @@
     q = project_q(
         normed_a, cosine_all, sine_all, attn_w, out_half, query_half
     )
-    for k in range(2, chips):
-        d_slots.append(ring_step(after(d_slots[-1], *([kv_slots[-1]] if k == 2 else []))))
+    d_slots.append(ring_step(after(d_slots[-1], kv_slots[-1])))
     attended, lse = attend(q, kv_slots, limits, kpos, qpos)
     attended_oth = swap_core(after(attended, d_slots[2 % chips]))
     branch, branch_oth = project_out(
         core_ref, attended, attended_oth, attn_w, out_half, batches
     )
 
-    branch_oth = after(swap_core(branch_oth), d_slots[-1])
+    branch_oth = swap_core(branch_oth)
     residual = x_own.astype(F32) + by_core(branch, branch_oth, 1)
     inverse_m = rms_inverse(residual)
     normed_m = (residual * inverse_m * gain_m).astype(BF16)
-    x_slots = [normed_m]
-    for k in range(1, min(chips, 3)):
-        x_slots.append(ring_step(x_slots[-1]))
+    x_slots = [normed_m, ring_step(normed_m)]
+    x_slots.append(ring_step(x_slots[1]))
     mlp_w_oth = swap_core(after(mlp_w, x_slots[1 % chips]))
     per = 2 if chips % 2 == 0 else 1
     groups = chips // per
@@ -913,9 +911,13 @@
         for k in range(g * per, (g + 1) * per):
             arrived += [x_slots[k], d_slots[k]]
         kept = hidden_group(g, groups, arrived, mlp_w, kept)
+        if g == 0 and len(x_slots) < chips:
+            d_slots.append(ring_step(after(d_slots[-1], kept[0])))
+        kept_oth = hidden_group(g, groups, None, mlp_w_oth, kept_oth, kept[:2])
         while len(x_slots) < chips:
-            x_slots.append(ring_step(after(x_slots[-1], kept[0])))
-        kept_oth = hidden_group(g, groups, None, mlp_w_oth, kept_oth, kept[:2])
+            x_slots.append(ring_step(after(x_slots[-1], d_slots[-1], kept_oth[0])))
+            if len(d_slots) < chips:
+                d_slots.append(ring_step(d_slots[-1]))
         own, other = list(kept[2:]), list(kept_oth)
         if g == 0:
             own[0] = after(own[0], x_slots[min(2, chips - 1)])

time: 742 us -> 750 us (1.011)
  transfers between devices with their start and end apart: 75 -> 75, of which waited for: 38 -> 40; matrix products, arithmetic and copies ran while one was open for 15% -> 15% of each run, Pallas kernels for 28% -> 26%
where the time goes in v5:
time: 750 us; the launch traced here: 741 us
  waiting for transfers between devices  264 us (35%)
  Pallas kernels  227 us (30%)
  starting transfers between devices  101 us (13%)
  other arithmetic  72.3 us (10%)
  matrix products  42.4 us (6%)
  local copies, waits for them, and re-layouts  19.4 us (3%)
  between operations  14.9 us (2%)
    ppermute x33, waiting for transfers between devices, ring_step(): return lax.ppermute(array, 'ctx', pairs)  180 us
    ppermute x23, waiting for transfers between devices, swap_seq(): return lax.ppermute(array, 'seq', [(i, i ^ bit) for i in range(seq)])  77.5 us
    ppermute x33, starting transfers between devices, ring_step(): return lax.ppermute(array, 'ctx', pairs)  67.2 us
    pallas_call x4, Pallas kernels, hidden_group(): pl.pallas_call(kernel, grid=(tiles,), in_specs=source_specs + [pl.BlockSp...  53.1 us
    dot_general x6, matrix products, rows_product(): jnp.einsum('ri,rj->ij', left, right, preferred_element_type=F32)  42.4 us
    pallas_call x2, Pallas kernels, mlp_back(): pl.pallas_call(mlp_back_kernel, grid=(1,), in_specs=[pl.BlockSpec((height...  41.6 us
    pallas_call x1, Pallas kernels, attend_back(): pl.pallas_call(functools.partial(attend_back_kernel, chips), grid_spec=pl...  34.6 us
    ppermute x23, starting transfers between devices, swap_seq(): return lax.ppermute(array, 'seq', [(i, i ^ bit) for i in range(seq)])  31.4 us
  transfers between devices with their start and end apart: 75, of which 40 were waited for; matrix products, arithmetic and copies ran while one was open for 15% of the time, Pallas kernels for 26%

profile of v5, /device:TPU:0, one launch (start us, length us, event | category | flops | bytes accessed | tf_op | source)
XLA Modules:
  0.0 741.3 jit_solution(18329643526315057384)
XLA Ops:
  21.8 15.5 %collective-permute-done.2.refs_3_ = bf16[256,2048]{1,0:T(8,128)(2,1)} collective-permute-done((bf16[256,2048]{1,0:T(8,128)(2,1)S(1)}, bf16[256,2048]{1,0:T(8,128)(2,1)}, u32[]{:S(2)}, u32[]{:S(2)}) %collective-permute-start.2) | collective-permute-done | bytes 1048608 | tf_op jit(solution)/shard_map/ppermute | solution.py:44
  43.8 11.9 %collective-permute-done.3.refs_7_ = bf16[128,2688]{1,0:T(8,128)(2,1)S(1)} collective-permute-done((bf16[128,2688]{1,0:T(8,128)(2,1)}, bf16[128,2688]{1,0:T(8,128)(2,1)S(1)}, u32[]{:S(2)}, u32[]{:S(2)}) %collective-permute-start.3) | collective-permute-done | bytes 688160 | tf_op jit(solution)/shard_map/ppermute | solution.py:44
  62.0 12.6 %collective-permute-done.6.refs_8_ = bf16[128,2688]{1,0:T(8,128)(2,1)} collective-permute-done((bf16[128,2688]{1,0:T(8,128)(2,1)S(1)}, bf16[128,2688]{1,0:T(8,128)(2,1)}, u32[]{:S(2)}, u32[]{:S(2)}) %collective-permute-start.6) | collective-permute-done | bytes 688160 | tf_op jit(solution)/shard_map/ppermute | solution.py:44
  79.5 11.6 %collective-permute-done.9.refs_9_ = bf16[128,2688]{1,0:T(8,128)(2,1)} collective-permute-done((bf16[128,2688]{1,0:T(8,128)(2,1)}, bf16[128,2688]{1,0:T(8,128)(2,1)}, u32[]{:S(2)}, u32[]{:S(2)}) %collective-permute-start.9) | collective-permute-done | bytes 688160 | tf_op jit(solution)/shard_map/ppermute | solution.py:44
  96.8 13.1 %collective-permute-done.13.refs_17_ = bf16[128,2688]{1,0:T(8,128)(2,1)} collective-permute-done((bf16[128,2688]{1,0:T(8,128)(2,1)}, bf16[128,2688]{1,0:T(8,128)(2,1)}, u32[]{:S(2)}, u32[]{:S(2)}) %collective-permute-start.13) | collective-permute-done | bytes 688160 | tf_op jit(solution)/shard_map/ppermute | solution.py:33
  113.9 10.7 %collective-permute-done.12.refs_16_ = bf16[128,2688]{1,0:T(8,128)(2,1)} collective-permute-done((bf16[128,2688]{1,0:T(8,128)(2,1)}, bf16[128,2688]{1,0:T(8,128)(2,1)}, u32[]{:S(2)}, u32[]{:S(2)}) %collective-permute-start.12) | collective-permute-done | bytes 688160 | tf_op jit(solution)/shard_map/ppermute | solution.py:33
  126.6 8.6 %collective-permute-done.16.refs_20_ = bf16[128,2688]{1,0:T(8,128)(2,1)} collective-permute-done((bf16[128,2688]{1,0:T(8,128)(2,1)}, bf16[128,2688]{1,0:T(8,128)(2,1)}, u32[]{:S(2)}, u32[]{:S(2)}) %collective-permute-start.16) | collective-permute-done | bytes 688160 | tf_op jit(solution)/shard_map/ppermute | solution.py:33
  140.6 13.5 %shard_map.205 = (bf16[512,512]{1,0:T(8,128)(2,1)}, bf16[512,2048]{1,0:T(8,128)(2,1)}, f32[8,2048]{1,0:T(8,128)}, bf16[2048,2688]{1,0:T(8,128)(2,1)}) custom-call(s32[1]{0:T(128)} %bitcast.1.core_ref.refs_0_, s32[16]{0:T(128)} %mul.187.refs_1_.starts, bf16[256,2048]{1,0:T(8,128)(2,1)} %bitcast.68, bf16[256,2048]{1,0:T(8,128)(2,1)} %collective-permute-done.refs_3_, ...), custom_call_target="tpu_custom_call" | custom-call | flops 33822867456 | bytes 26214400 | tf_op jit(solution)/shard_map/pallas_call | solution.py:246
  156.3 9.6 %collective-permute-done.18.refs_1_ = bf16[512,512]{1,0:T(8,128)(2,1)S(1)} collective-permute-done((bf16[512,512]{1,0:T(8,128)(2,1)}, bf16[512,512]{1,0:T(8,128)(2,1)S(1)}, u32[]{:S(2)}, u32[]{:S(2)}) %collective-permute-start.18) | collective-permute-done | bytes 524320 | tf_op jit(solution)/shard_map/ppermute | solution.py:44
  170.9 8.6 %collective-permute-done.19.refs_2_ = bf16[512,512]{1,0:T(8,128)(2,1)S(1)} collective-permute-done((bf16[512,512]{1,0:T(8,128)(2,1)S(1)}, bf16[512,512]{1,0:T(8,128)(2,1)S(1)}, u32[]{:S(2)}, u32[]{:S(2)}) %collective-permute-start.19) | collective-permute-done | bytes 524320 | tf_op jit(solution)/shard_map/ppermute | solution.py:44
  182.9 9.7 %shard_map.206.q_ref = bf16[512,1024]{1,0:T(8,128)(2,1)} custom-call(bf16[512,2048]{1,0:T(8,128)(2,1)} %get-tuple-element.98.normed.refs_0_, f32[512,128]{1,0:T(8,128)} %bitcast.75, f32[512,128]{1,0:T(8,128)} %bitcast.78, bf16[2048,2688]{1,0:T(8,128)(2,1)} %get-tuple-element.141.w.w_all.w_ref.wq_ref.wkv_ref), custom_call_target="tpu_custom_call" | custom-call | flops 12884901888 | bytes 10485760 | tf_op jit(solution)/shard_map/pallas_call | solution.py:287
  197.4 25.9 %shard_map.207 = (bf16[512,1024]{1,0:T(8,128)(2,1)}, f32[32,256]{1,0:T(8,128)}) custom-call(s32[2]{0:T(128)} %bitcast.97, s32[1024,1]{1,0:T(8,128)} %bitcast.80, s32[1,256]{1,0:T(1,128)} %iota_add_fusion.qpos_ref, bf16[512,1024]{1,0:T(8,128)(2,1)} %shard_map.206.q_ref, bf16[512,512]{1,0:T(8,128)(2,1)} %get-tuple-element.100.refs_0_, ...), custom_call_target="tpu_custom_call" | custom-call | flops 51539607552 | bytes 4194304 | tf_op jit(solution)/shard_map/pallas_call | solution.py:352
  228.3 9.1 %shard_map.208 = (f32[256,1024]{1,0:T(8,128)}, f32[256,1024]{1,0:T(8,128)}) custom-call(s32[1]{0:T(128)} %bitcast.1.core_ref.refs_0_, bf16[512,1024]{1,0:T(8,128)(2,1)} %get-tuple-element.103.o_mine.refs_0_, bf16[512,1024]{1,0:T(8,128)(2,1)} %copy-done.40, bf16[2048,2688]{1,0:T(8,128)(2,1)} %get-tuple-element.141.w.w_all.w_ref.wq_ref.wkv_ref), custom_call_target="tpu_custom_call" | custom-call | flops 12884901888 | bytes 10485760 | tf_op jit(solution)/shard_map/pallas_call | solution.py:502
  246.8 24.6 %collective-permute-done.24.refs_2_ = bf16[256,2048]{1,0:T(8,128)(2,1)S(1)} collective-permute-done((bf16[256,2048]{1,0:T(8,128)(2,1)S(1)}, bf16[256,2048]{1,0:T(8,128)(2,1)S(1)}, u32[]{:S(2)}, u32[]{:S(2)}) %collective-permute-start.24) | collective-permute-done | bytes 1048608 | tf_op jit(solution)/shard_map/ppermute | solution.py:44
  273.0 14.1 %shard_map.209 = (bf16[1024,2048]{1,0:T(8,128)(2,1)}, bf16[1024,2048]{1,0:T(8,128)(2,1)}, bf16[1024,1024]{1,0:T(8,128)(2,1)}, bf16[1024,1024]{1,0:T(8,128)(2,1)}, bf16[1024,1024]{1,0:T(8,128)(2,1)}) custom-call(bf16[256,2048]{1,0:T(8,128)(2,1)} %copy-done.21, bf16[256,2048]{1,0:T(8,128)(2,1)} %copy-done.19, bf16[256,2048]{1,0:T(8,128)(2,1)} %copy-done.45, ...), custom_call_target="tpu_custom_call" | custom-call | flops 38654705664 | bytes 25165824 | tf_op jit(solution)/shard_map/pallas_call | solution.py:582
  288.4 8.9 %collective-permute-done.25.refs_0_ = bf16[256,2048]{1,0:T(8,128)(2,1)S(1)} collective-permute-done((bf16[256,2048]{1,0:T(8,128)(2,1)S(1)}, bf16[256,2048]{1,0:T(8,128)(2,1)S(1)}, u32[]{:S(2)}, u32[]{:S(2)}) %collective-permute-start.25) | collective-permute-done | bytes 1048608 | tf_op jit(solution)/shard_map/ppermute | solution.py:44
  297.4 12.6 %shard_map.210 = (bf16[1024,1024]{1,0:T(8,128)(2,1)}, bf16[1024,1024]{1,0:T(8,128)(2,1)}, bf16[1024,1024]{1,0:T(8,128)(2,1)}) custom-call(bf16[1024,2048]{1,0:T(8,128)(2,1)} %get-tuple-element.112.x.refs_7_, bf16[1024,2048]{1,0:T(8,128)(2,1)} %get-tuple-element.113.d.refs_8_, bf16[2048,3072]{1,0:T(8,128)(2,1)} %collective-permute-done.26.gate.up.down_t.refs_7_, ...), custom_call_target="tpu_custom_call" | custom-call | flops 38654705664 | bytes 25165824 | tf_op jit(solution)/shard_map/pallas_call | solution.py:582
  310.0 9.4 %collective-permute-done.28.refs_3_ = bf16[256,2048]{1,0:T(8,128)(2,1)S(1)} collective-permute-done((bf16[256,2048]{1,0:T(8,128)(2,1)S(1)}, bf16[256,2048]{1,0:T(8,128)(2,1)S(1)}, u32[]{:S(2)}, u32[]{:S(2)}) %collective-permute-start.28) | collective-permute-done | bytes 1048608 | tf_op jit(solution)/shard_map/ppermute | solution.py:44
  321.9 20.8 %shard_map.211 = (bf16[512,2048]{1,0:T(8,128)(2,1)}, bf16[512,2048]{1,0:T(8,128)(2,1)}) custom-call(bf16[1024,1024]{1,0:T(8,128)(2,1)} %get-tuple-element.109.refs_0_.refs_9_, bf16[1024,1024]{1,0:T(8,128)(2,1)} %get-tuple-element.110.refs_1_.refs_10_, bf16[1024,1024]{1,0:T(8,128)(2,1)} %get-tuple-element.111.refs_2_.refs_11_, ...), custom_call_target="tpu_custom_call" | custom-call | flops 77309411328 | bytes 39845888 | tf_op jit(solution)/shard_map/pallas_call | solution.py:639
  345.6 14.1 %shard_map.212 = (bf16[1024,2048]{1,0:T(8,128)(2,1)}, bf16[1024,2048]{1,0:T(8,128)(2,1)}, bf16[1024,1024]{1,0:T(8,128)(2,1)}, bf16[1024,1024]{1,0:T(8,128)(2,1)}, bf16[1024,1024]{1,0:T(8,128)(2,1)}) custom-call(bf16[256,2048]{1,0:T(8,128)(2,1)} %copy-done.43, ...), custom_call_target="tpu_custom_call", output_to_operand_aliasing={{0}: (7, {}), {1}: (8, {}), {2}: (9, {}), {3}: (10, {}), {4... | custom-call | flops 38654705664 | bytes 25165824 | tf_op jit(solution)/shard_map/pallas_call | solution.py:582
  359.7 9.0 %collective-permute-done.27 = bf16[256,2048]{1,0:T(8,128)(2,1)S(1)} collective-permute-done((bf16[256,2048]{1,0:T(8,128)(2,1)S(1)}, bf16[256,2048]{1,0:T(8,128)(2,1)S(1)}, u32[]{:S(2)}, u32[]{:S(2)}) %collective-permute-start.27) | collective-permute-done | bytes 1048608 | tf_op jit(solution)/shard_map/ppermute | solution.py:44
  368.7 12.3 %shard_map.213 = (bf16[1024,1024]{1,0:T(8,128)(2,1)}, bf16[1024,1024]{1,0:T(8,128)(2,1)}, bf16[1024,1024]{1,0:T(8,128)(2,1)}) custom-call(bf16[1024,2048]{1,0:T(8,128)(2,1)} %get-tuple-element.136.x, bf16[1024,2048]{1,0:T(8,128)(2,1)} %get-tuple-element.135.d, ...), custom_call_target="tpu_custom_call", output_to_operand_aliasing={{0}: (5, {}), {1}: (6, {}), {2}: (7, {})} | custom-call | flops 38654705664 | bytes 25165824 | tf_op jit(solution)/shard_map/pallas_call | solution.py:582
  381.0 20.8 %shard_map.214 = (bf16[512,2048]{1,0:T(8,128)(2,1)}, bf16[512,2048]{1,0:T(8,128)(2,1)}) custom-call(bf16[1024,1024]{1,0:T(8,128)(2,1)} %get-tuple-element.134.refs_0_, bf16[1024,1024]{1,0:T(8,128)(2,1)} %get-tuple-element.137.refs_1_, bf16[1024,1024]{1,0:T(8,128)(2,1)} %get-tuple-element.139.refs_2_, bf16[1024,1024]{1,0:T(8,128)(2,1)} %get-tuple-element.128.refs_3_, ...), custom_call_target="tpu_custom_call" | custom-call | flops 77309411328 | bytes 39845888 | tf_op jit(solution)/shard_map/pallas_call | solution.py:639
  403.7 8.7 %convolution_convert_fusion.2 = bf16[2048,1024]{1,0:T(8,128)(2,1)} fusion(bf16[1024,2048]{1,0:T(8,128)(2,1)} %get-tuple-element.136.x, bf16[1024,1024]{1,0:T(8,128)(2,1)S(1)} %copy-done.62), kind=kOutput, calls=%fused_computation.5 | convolution fusion | flops 4297064448 | bytes 10485760 | tf_op jit(solution)/shard_map/ri,rj->ij/dot_general | solution.py:943
  458.2 8.0 %collective-permute-done.31 = bf16[256,2048]{1,0:T(8,128)(2,1)S(1)} collective-permute-done((bf16[256,2048]{1,0:T(8,128)(2,1)S(1)}, bf16[256,2048]{1,0:T(8,128)(2,1)S(1)}, u32[]{:S(2)}, u32[]{:S(2)}) %collective-permute-start.31) | collective-permute-done | bytes 1048608 | tf_op jit(solution)/shard_map/ppermute | solution.py:44
  482.0 9.0 %shard_map.215 = (f32[512,1024]{1,0:T(8,128)}, bf16[512,1024]{1,0:T(8,128)(2,1)}, bf16[512,1024]{1,0:T(8,128)(2,1)}) custom-call(s32[1]{0:T(128)} %bitcast.1.core_ref.refs_0_, bf16[256,1024]{1,0:T(8,128)(2,1)} %get-tuple-element.219.d_own, bf16[256,1024]{1,0:T(8,128)(2,1)} %copy-done.55, bf16[2048,2688]{1,0:T(8,128)(2,1)} %get-tuple-element.141.w.w_all.w_ref.wq_ref.wkv_ref), custom_call_target="tpu_custom_call" | custom-call | flops 12884901888 | bytes 10485760 | tf_op jit(solution)/shard_map/pallas_call | solution.py:688
  517.7 7.6 %add_convert_fusion = bf16[2048,1024]{1,0:T(8,128)(2,1)} fusion(bf16[2048,1024]{1,0:T(8,128)(2,1)} %collective-permute-done.38, bf16[2048,1024]{1,0:T(8,128)(2,1)} %convolution_convert_fusion.1), kind=kLoop, calls=%fused_computation | loop fusion | flops 8388608 | bytes 12582912 | tf_op jit(solution)/shard_map/convert_element_type | solution.py:957
  525.4 34.6 %shard_map.216 = (bf16[512,1024]{1,0:T(8,128)(2,1)}, bf16[512,512]{1,0:T(8,128)(2,1)}, bf16[512,512]{1,0:T(8,128)(2,1)}, bf16[512,512]{1,0:T(8,128)(2,1)}, bf16[512,512]{1,0:T(8,128)(2,1)}) custom-call(s32[2]{0:T(128)} %bitcast.98, s32[1024,1]{1,0:T(8,128)} %bitcast.81, s32[1,256]{1,0:T(1,128)} %iota_add_fusion.qpos_ref, ...), custom_call_target="tpu_custom_call" | custom-call | flops 128849018880 | bytes 9437184 | tf_op jit(solution)/shard_map/pallas_call | solution.py:431
  589.8 13.9 %collective-permute-done.51 = bf16[512,1024]{1,0:T(8,128)(2,1)S(1)} collective-permute-done((bf16[512,1024]{1,0:T(8,128)(2,1)}, bf16[512,1024]{1,0:T(8,128)(2,1)S(1)}, u32[]{:S(2)}, u32[]{:S(2)}) %collective-permute-start.51) | collective-permute-done | bytes 1048608 | tf_op jit(solution)/shard_map/ppermute | solution.py:33
  605.8 20.5 %collective-permute-done.66 = bf16[512,1024]{1,0:T(8,128)(2,1)} collective-permute-done((bf16[512,1024]{1,0:T(8,128)(2,1)}, bf16[512,1024]{1,0:T(8,128)(2,1)}, u32[]{:S(2)}, u32[]{:S(2)}) %collective-permute-start.66) | collective-permute-done | bytes 1048608 | tf_op jit(solution)/shard_map/ppermute | solution.py:33
  633.7 7.7 %shard_map.218 = (f32[256,2048]{1,0:T(8,128)}, bf16[256,2048]{1,0:T(8,128)(2,1)}) custom-call(s32[1]{0:T(128)} %bitcast.1.core_ref.refs_0_, bf16[512,1024]{1,0:T(8,128)(2,1)} %get-tuple-element.151.dq_ref.refs_1_, bf16[512,512]{1,0:T(8,128)(2,1)} %shard_map.217.dkv_ref.refs_1_, bf16[2048,2688]{1,0:T(8,128)(2,1)} %get-tuple-element.141.w.w_all.w_ref.wq_ref.wkv_ref, ...), custom_call_target="tpu_custom_call" | custom-call | flops 19327352832 | bytes 10485760 | tf_op jit(solution)/shard_map/pallas_call | solution.py:767
  665.0 13.4 %collective-permute-done.41 = bf16[256,2048]{1,0:T(8,128)(2,1)S(1)} collective-permute-done((bf16[256,2048]{1,0:T(8,128)(2,1)}, bf16[256,2048]{1,0:T(8,128)(2,1)S(1)}, u32[]{:S(2)}, u32[]{:S(2)}) %collective-permute-start.41) | collective-permute-done | bytes 1048608 | tf_op jit(solution)/shard_map/ppermute | solution.py:44
  (368 shorter events, 295.9 us)
Async XLA Ops:
  7.2 264.2 %all-gather.2.cloned.1.call-start = ((), (), s32[]{:S(2)}) async-start(), calls=%async_computation.3 | async-start | bytes 15728640 | tf_op jit(solution)/shard_map/all_gather | solution.py:879
  10.6 26.7 %collective-permute-start.2 = (bf16[256,2048]{1,0:T(8,128)(2,1)S(1)}, bf16[256,2048]{1,0:T(8,128)(2,1)}, u32[]{:S(2)}, u32[]{:S(2)}) collective-permute-start(bf16[256,2048]{1,0:T(8,128)(2,1)S(1)} %fusion.12.refs_1_), channel_id=1, source_target_pairs={{0,4},{1,5},{4,6},{5,7},{6,2},{7,3},{2,0},{3,1},{8,12},{9,13},{12,... | collective-permute-start | bytes 3145736 | tf_op jit(solution)/shard_map/ppermute | solution.py:44
  92.7 31.9 %collective-permute-start.12 = (bf16[128,2688]{1,0:T(8,128)(2,1)}, bf16[128,2688]{1,0:T(8,128)(2,1)}, u32[]{:S(2)}, u32[]{:S(2)}) collective-permute-start(bf16[128,2688]{1,0:T(8,128)(2,1)} %collective-permute-done.6.refs_8_), channel_id=1, source_target_pairs={{0,16},{8,24},{16,0},{24,8},{1,17},{9,25},{17,1},{25,9},{2,18},{10... | collective-permute-start | bytes 2064392 | tf_op jit(solution)/shard_map/ppermute | solution.py:33
  93.2 31.4 %collective-permute-start.15 = (bf16[128,2688]{1,0:T(8,128)(2,1)}, bf16[128,2688]{1,0:T(8,128)(2,1)}, u32[]{:S(2)}, u32[]{:S(2)}) collective-permute-start(bf16[128,2688]{1,0:T(8,128)(2,1)} %collective-permute-done.8.refs_15_), channel_id=1, source_target_pairs={{0,8},{8,0},{16,24},{24,16},{1,9},{9,1},{17,25},{25,17},{2,10},{10... | collective-permute-start | bytes 2064392 | tf_op jit(solution)/shard_map/ppermute | solution.py:33
  93.8 32.9 %collective-permute-start.11 = (bf16[128,2688]{1,0:T(8,128)(2,1)}, bf16[128,2688]{1,0:T(8,128)(2,1)}, u32[]{:S(2)}, u32[]{:S(2)}) collective-permute-start(bf16[128,2688]{1,0:T(8,128)(2,1)} %collective-permute-done.9.refs_9_), channel_id=1, source_target_pairs={{0,8},{8,0},{16,24},{24,16},{1,9},{9,1},{17,25},{25,17},{2,10},{10... | collective-permute-start | bytes 2064392 | tf_op jit(solution)/shard_map/ppermute | solution.py:33
  95.2 40.0 %collective-permute-start.16 = (bf16[128,2688]{1,0:T(8,128)(2,1)}, bf16[128,2688]{1,0:T(8,128)(2,1)}, u32[]{:S(2)}, u32[]{:S(2)}) collective-permute-start(bf16[128,2688]{1,0:T(8,128)(2,1)} %collective-permute-done.10.refs_12_), channel_id=1, source_target_pairs={{0,16},{8,24},{16,0},{24,8},{1,17},{9,25},{17,1},{25,9},{2,18},{10... | collective-permute-start | bytes 2064392 | tf_op jit(solution)/shard_map/ppermute | solution.py:33
  109.9 26.8 %collective-permute-start.17 = (bf16[128,2688]{1,0:T(8,128)(2,1)}, bf16[128,2688]{1,0:T(8,128)(2,1)}, u32[]{:S(2)}, u32[]{:S(2)}) collective-permute-start(bf16[128,2688]{1,0:T(8,128)(2,1)} %collective-permute-done.13.refs_17_), channel_id=1, source_target_pairs={{0,8},{8,0},{16,24},{24,16},{1,9},{9,1},{17,25},{25,17},{2,10},{10... | collective-permute-start | bytes 2064392 | tf_op jit(solution)/shard_map/ppermute | solution.py:33
  136.7 589.4 %reduce-scatter.4.cloned.1.call-start = ((), (), s32[]{:S(2)}) async-start(), calls=%async_computation.4 | async-start | bytes 5242880 | tf_op jit(solution)/shard_map/reduce_scatter | solution.py:946
  193.9 29.5 %collective-permute-start.21 = (bf16[256,2048]{1,0:T(8,128)(2,1)}, bf16[256,2048]{1,0:T(8,128)(2,1)S(1)}, u32[]{:S(2)}, u32[]{:S(2)}) collective-permute-start(bf16[256,2048]{1,0:T(8,128)(2,1)} %collective-permute-done.2.refs_3_), channel_id=1, source_target_pairs={{0,4},{1,5},{4,6},{5,7},{6,2},{7,3},{2,0},{3,1},{8,12},{9,13},{12,... | collective-permute-start | bytes 3145736 | tf_op jit(solution)/shard_map/ppermute | solution.py:44
  246.2 25.2 %collective-permute-start.24 = (bf16[256,2048]{1,0:T(8,128)(2,1)S(1)}, bf16[256,2048]{1,0:T(8,128)(2,1)S(1)}, u32[]{:S(2)}, u32[]{:S(2)}) collective-permute-start(bf16[256,2048]{1,0:T(8,128)(2,1)S(1)} %get-tuple-element.214.refs_0_), channel_id=1, source_target_pairs={{0,4},{1,5},{4,6},{5,7},{6,2},{7,3},{2,0},{3,1},{8,12},{9,13},{12,... | collective-permute-start | bytes 3145736 | tf_op jit(solution)/shard_map/ppermute | solution.py:44
  271.4 26.0 %collective-permute-start.26 = (bf16[2048,3072]{1,0:T(8,128)(2,1)}, bf16[2048,3072]{1,0:T(8,128)(2,1)}, u32[]{:S(2)}, u32[]{:S(2)}) collective-permute-start(bf16[2048,3072]{1,0:T(8,128)(2,1)} %all-gather.2.cloned.1.call-done.refs_4_.refs_5_.refs_6_), channel_id=1, source_target_pairs={{0,1},{1,0},{2,3},{3,2},{4,5},{5,4},{6,7},{7,6},{8,9},{9,8},{10,11... | collective-permute-start | bytes 37748744 | tf_op jit(solution)/shard_map/ppermute | solution.py:28
  271.4 26.0 %collective-permute-start.25 = (bf16[256,2048]{1,0:T(8,128)(2,1)S(1)}, bf16[256,2048]{1,0:T(8,128)(2,1)S(1)}, u32[]{:S(2)}, u32[]{:S(2)}) collective-permute-start(bf16[256,2048]{1,0:T(8,128)(2,1)S(1)} %collective-permute-done.24.refs_2_), channel_id=1, source_target_pairs={{0,4},{1,5},{4,6},{5,7},{6,2},{7,3},{2,0},{3,1},{8,12},{9,13},{12,... | collective-permute-start | bytes 3145736 | tf_op jit(solution)/shard_map/ppermute | solution.py:44
  287.1 32.4 %collective-permute-start.28 = (bf16[256,2048]{1,0:T(8,128)(2,1)S(1)}, bf16[256,2048]{1,0:T(8,128)(2,1)S(1)}, u32[]{:S(2)}, u32[]{:S(2)}) collective-permute-start(bf16[256,2048]{1,0:T(8,128)(2,1)S(1)} %copy-done.42), channel_id=1, source_target_pairs={{0,4},{1,5},{4,6},{5,7},{6,2},{7,3},{2,0},{3,1},{8,12},{9,13},{12,... | collective-permute-start | bytes 3145736 | tf_op jit(solution)/shard_map/ppermute | solution.py:44
  414.1 25.7 %collective-permute-start.30 = (bf16[256,2048]{1,0:T(8,128)(2,1)S(1)}, bf16[256,2048]{1,0:T(8,128)(2,1)}, u32[]{:S(2)}, u32[]{:S(2)}) collective-permute-start(bf16[256,2048]{1,0:T(8,128)(2,1)S(1)} %add_convert_fusion.9), channel_id=1, source_target_pairs={{0,4},{1,5},{4,6},{5,7},{6,2},{7,3},{2,0},{3,1},{8,12},{9,13},{12,... | collective-permute-start | bytes 3145736 | tf_op jit(solution)/shard_map/ppermute | solution.py:44
  435.7 293.3 %reduce-scatter.8.cloned.1.call-start = ((), (), s32[]{:S(2)}) async-start(), calls=%async_computation.6 | async-start | bytes 5242880 | tf_op jit(solution)/shard_map/reduce_scatter | solution.py:946
  451.4 56.3 %collective-permute-start.36 = (bf16[1024,2048]{1,0:T(8,128)(2,1)}, bf16[1024,2048]{1,0:T(8,128)(2,1)}, u32[]{:S(2)}, u32[]{:S(2)}) collective-permute-start(bf16[1024,2048]{1,0:T(8,128)(2,1)} %convolution_convert_fusion.4), channel_id=1, source_target_pairs={{0,1},{1,0},{2,3},{3,2},{4,5},{5,4},{6,7},{7,6},{8,9},{9,8},{10,11... | collective-permute-start | bytes 12582920 | tf_op jit(solution)/shard_map/ppermute | solution.py:28
  457.7 60.0 %collective-permute-start.38 = (bf16[2048,1024]{1,0:T(8,128)(2,1)}, bf16[2048,1024]{1,0:T(8,128)(2,1)}, u32[]{:S(2)}, u32[]{:S(2)}) collective-permute-start(bf16[2048,1024]{1,0:T(8,128)(2,1)} %convolution_convert_fusion), channel_id=1, source_target_pairs={{0,1},{1,0},{2,3},{3,2},{4,5},{5,4},{6,7},{7,6},{8,9},{9,8},{10,11... | collective-permute-start | bytes 12582920 | tf_op jit(solution)/shard_map/ppermute | solution.py:28
  477.9 25.9 %collective-permute-start.32 = (bf16[256,2048]{1,0:T(8,128)(2,1)}, bf16[256,2048]{1,0:T(8,128)(2,1)S(1)}, u32[]{:S(2)}, u32[]{:S(2)}) collective-permute-start(bf16[256,2048]{1,0:T(8,128)(2,1)} %slice.125), channel_id=1, source_target_pairs={{0,4},{1,5},{4,6},{5,7},{6,2},{7,3},{2,0},{3,1},{8,12},{9,13},{12,... | collective-permute-start | bytes 3145736 | tf_op jit(solution)/shard_map/ppermute | solution.py:44
  497.0 83.1 %collective-permute-start.64 = (bf16[512,1024]{1,0:T(8,128)(2,1)}, bf16[512,1024]{1,0:T(8,128)(2,1)}, u32[]{:S(2)}, u32[]{:S(2)}) collective-permute-start(bf16[512,1024]{1,0:T(8,128)(2,1)} %get-tuple-element.168), channel_id=1, source_target_pairs={{0,16},{8,24},{16,0},{24,8},{1,17},{9,25},{17,1},{25,9},{2,18},{10... | collective-permute-start | bytes 3145736 | tf_op jit(solution)/shard_map/ppermute | solution.py:33
  499.5 25.9 %collective-permute-start.35 = (bf16[512,1024]{1,0:T(8,128)(2,1)}, bf16[512,1024]{1,0:T(8,128)(2,1)}, u32[]{:S(2)}, u32[]{:S(2)}) collective-permute-start(bf16[512,1024]{1,0:T(8,128)(2,1)} %get-tuple-element.144), channel_id=1, source_target_pairs={{0,1},{1,0},{2,3},{3,2},{4,5},{5,4},{6,7},{7,6},{8,9},{9,8},{10,11... | collective-permute-start | bytes 3145736 | tf_op jit(solution)/shard_map/ppermute | solution.py:28
  503.8 64.5 %collective-permute-start.65 = (bf16[512,1024]{1,0:T(8,128)(2,1)}, bf16[512,1024]{1,0:T(8,128)(2,1)}, u32[]{:S(2)}, u32[]{:S(2)}) collective-permute-start(bf16[512,1024]{1,0:T(8,128)(2,1)} %get-tuple-element.171), channel_id=1, source_target_pairs={{0,16},{8,24},{16,0},{24,8},{1,17},{9,25},{17,1},{25,9},{2,18},{10... | collective-permute-start | bytes 3145736 | tf_op jit(solution)/shard_map/ppermute | solution.py:33
  507.7 52.3 %collective-permute-start.34 = (bf16[256,2048]{1,0:T(8,128)(2,1)}, bf16[256,2048]{1,0:T(8,128)(2,1)S(1)}, u32[]{:S(2)}, u32[]{:S(2)}) collective-permute-start(bf16[256,2048]{1,0:T(8,128)(2,1)} %add_convert_fusion.7), channel_id=1, source_target_pairs={{0,4},{1,5},{4,6},{5,7},{6,2},{7,3},{2,0},{3,1},{8,12},{9,13},{12,... | collective-permute-start | bytes 3145736 | tf_op jit(solution)/shard_map/ppermute | solution.py:44
  517.7 214.1 %reduce-scatter.6.cloned.1.call-start = ((), (), s32[]{:S(2)}) async-start(), calls=%async_computation.5 | async-start | bytes 5242880 | tf_op jit(solution)/shard_map/reduce_scatter | solution.py:946
  566.2 37.6 %collective-permute-start.51 = (bf16[512,1024]{1,0:T(8,128)(2,1)}, bf16[512,1024]{1,0:T(8,128)(2,1)S(1)}, u32[]{:S(2)}, u32[]{:S(2)}) collective-permute-start(bf16[512,1024]{1,0:T(8,128)(2,1)} %get-tuple-element.159), channel_id=1, source_target_pairs={{0,8},{8,0},{16,24},{24,16},{1,9},{9,1},{17,25},{25,17},{2,10},{10... | collective-permute-start | bytes 3145736 | tf_op jit(solution)/shard_map/ppermute | solution.py:33
  577.9 48.4 %collective-permute-start.66 = (bf16[512,1024]{1,0:T(8,128)(2,1)}, bf16[512,1024]{1,0:T(8,128)(2,1)}, u32[]{:S(2)}, u32[]{:S(2)}) collective-permute-start(bf16[512,1024]{1,0:T(8,128)(2,1)} %add_convert_fusion.3), channel_id=1, source_target_pairs={{0,8},{8,0},{16,24},{24,16},{1,9},{9,1},{17,25},{25,17},{2,10},{10... | collective-permute-start | bytes 3145736 | tf_op jit(solution)/shard_map/ppermute | solution.py:33
  580.0 71.1 %collective-permute-start.50 = (bf16[512,1024]{1,0:T(8,128)(2,1)}, bf16[512,1024]{1,0:T(8,128)(2,1)}, u32[]{:S(2)}, u32[]{:S(2)}) collective-permute-start(bf16[512,1024]{1,0:T(8,128)(2,1)} %get-tuple-element.157), channel_id=1, source_target_pairs={{0,8},{8,0},{16,24},{24,16},{1,9},{9,1},{17,25},{25,17},{2,10},{10... | collective-permute-start | bytes 3145736 | tf_op jit(solution)/shard_map/ppermute | solution.py:33
  586.4 44.0 %collective-permute-start.42 = (bf16[512,512]{1,0:T(8,128)(2,1)S(1)}, bf16[512,512]{1,0:T(8,128)(2,1)S(1)}, u32[]{:S(2)}, u32[]{:S(2)}) collective-permute-start(bf16[512,512]{1,0:T(8,128)(2,1)S(1)} %add_convert_fusion.11), channel_id=1, source_target_pairs={{0,4},{1,5},{4,6},{5,7},{6,2},{7,3},{2,0},{3,1},{8,12},{9,13},{12,... | collective-permute-start | bytes 1572872 | tf_op jit(solution)/shard_map/ppermute | solution.py:44
  605.1 55.5 %collective-permute-start.52 = (bf16[512,1024]{1,0:T(8,128)(2,1)}, bf16[512,1024]{1,0:T(8,128)(2,1)}, u32[]{:S(2)}, u32[]{:S(2)}) collective-permute-start(bf16[512,1024]{1,0:T(8,128)(2,1)} %add_convert_fusion.4), channel_id=1, source_target_pairs={{0,16},{8,24},{16,0},{24,8},{1,17},{9,25},{17,1},{25,9},{2,18},{10... | collective-permute-start | bytes 3145736 | tf_op jit(solution)/shard_map/ppermute | solution.py:33
  648.6 29.8 %collective-permute-start.41 = (bf16[256,2048]{1,0:T(8,128)(2,1)}, bf16[256,2048]{1,0:T(8,128)(2,1)S(1)}, u32[]{:S(2)}, u32[]{:S(2)}) collective-permute-start(bf16[256,2048]{1,0:T(8,128)(2,1)} %add_convert_fusion.6), channel_id=1, source_target_pairs={{0,4},{1,5},{4,6},{5,7},{6,2},{7,3},{2,0},{3,1},{8,12},{9,13},{12,... | collective-permute-start | bytes 3145736 | tf_op jit(solution)/shard_map/ppermute | solution.py:44
  651.2 30.5 %collective-permute-start.43 = (bf16[256,2048]{1,0:T(8,128)(2,1)}, bf16[256,2048]{1,0:T(8,128)(2,1)S(1)}, u32[]{:S(2)}, u32[]{:S(2)}) collective-permute-start(bf16[256,2048]{1,0:T(8,128)(2,1)} %get-tuple-element.155), channel_id=1, source_target_pairs={{0,1},{1,0},{2,3},{3,2},{4,5},{5,4},{6,7},{7,6},{8,9},{9,8},{10,11... | collective-permute-start | bytes 3145736 | tf_op jit(solution)/shard_map/ppermute | solution.py:28
  660.6 26.8 %collective-permute-start.59 = (bf16[512,512]{1,0:T(8,128)(2,1)S(1)}, bf16[512,512]{1,0:T(8,128)(2,1)S(1)}, u32[]{:S(2)}, u32[]{:S(2)}) collective-permute-start(bf16[512,512]{1,0:T(8,128)(2,1)S(1)} %add_convert_fusion.10), channel_id=1, source_target_pairs={{0,8},{8,0},{16,24},{24,16},{1,9},{9,1},{17,25},{25,17},{2,10},{10... | collective-permute-start | bytes 1572872 | tf_op jit(solution)/shard_map/ppermute | solution.py:33
  681.6 26.7 %collective-permute-start.70 = (f32[64,1024]{1,0:T(8,128)S(1)}, f32[64,1024]{1,0:T(8,128)S(1)}, u32[]{:S(2)}, u32[]{:S(2)}) collective-permute-start(f32[64,1024]{1,0:T(8,128)S(1)} %get-tuple-element.221), channel_id=1, source_target_pairs={{0,1},{1,0},{2,3},{3,2},{4,5},{5,4},{6,7},{7,6},{8,9},{9,8},{10,11... | collective-permute-start | bytes 786440 | tf_op jit(solution)/shard_map/ppermute | solution.py:28
  (107 other events, 1568.1 us)
Sparse Core Ops, SparseCore 0:
  136.9 121.3 all-gather.1
  435.8 52.9 reduce-scatter.3
  517.8 82.0 reduce-scatter.7
  651.3 60.8 reduce-scatter.5

commit v6 on v4

--- a/solution.py
+++ b/solution.py
@@ -59,12 +59,13 @@
     return total
 
 
-def cube_gather(array, route):
+def cube_gather(array, route, *waits):
     seq = lax.axis_size("seq")
     bits = [1 << i for i in range(seq.bit_length() - 1)]
     pieces = {0: array}
     for bit in bits if route == 0 else bits[::-1]:
-        pieces.update({r ^ bit: swap_seq(piece, bit) for r, piece in pieces.items()})
+        seen = waits if len(pieces) > 1 else ()
+        pieces.update({r ^ bit: swap_seq(after(p, *seen), bit) for r, p in pieces.items()})
     return [pieces[r] for r in range(seq)]
 
 
@@ -868,12 +869,15 @@
     x_oth = swap_core(x_own)
     packed, to_other = pack(core_ref, w_query, w_key, w_value, w_out, gains)
     (piece_a,) = stack_pieces(core_ref, packed, swap_core(to_other), [packed.shape[1]])
-    d_slots = [d_rows, ring_step(d_rows)]
     ring_a, cubes_a = [after(piece_a, x_oth)], []
     for k in range(chips):
-        cubes_a.append(cube_gather(ring_a[k], k % 2))
+        waits = []
+        if k + 1 == chips:
+            d_slots = [d_rows, ring_step(after(d_rows, ring_a[-1]))]
+            waits = [d_slots[1]]
+        cubes_a.append(cube_gather(ring_a[k], k % 2, *waits))
         if k + 1 < chips:
-            seen = [cubes_a[k - 1][1], cubes_a[k - 1][2]] if k else d_slots[1:2]
+            seen = [cubes_a[k - 1][1], cubes_a[k - 1][2]] if k else []
             ring_a.append(ring_step(after(ring_a[k], *seen)))
     mlp_w = jnp.concatenate([w_gate, w_up, w_down.T], axis=1)
     mlp_w = lax.all_gather(after(mlp_w, *sum(cubes_a, [])), "seq", axis=0, tiled=True)

time: 742 us -> 736 us (level)
    ppermute x33, waiting for transfers between devices: 177 us -> 166 us  [ring_step(): return lax.ppermute(array, 'ctx', pairs)]
    ppermute x23, waiting for transfers between devices: 79.1 us -> 87.8 us  [swap_seq(): return lax.ppermute(array, 'seq', [(i, i ^ bit) for i in range(seq)])]
where the time goes in v6:
time: 736 us; the launch traced here: 727 us
  waiting for transfers between devices  259 us (35%)
  Pallas kernels  227 us (31%)
  starting transfers between devices  94.1 us (13%)
  other arithmetic  70.3 us (10%)
  matrix products  42 us (6%)
  local copies, waits for them, and re-layouts  20.1 us (3%)
  between operations  14.9 us (2%)
    ppermute x33, waiting for transfers between devices, ring_step(): return lax.ppermute(array, 'ctx', pairs)  166 us
    ppermute x23, waiting for transfers between devices, swap_seq(): return lax.ppermute(array, 'seq', [(i, i ^ bit) for i in range(seq)])  87.8 us
    ppermute x33, starting transfers between devices, ring_step(): return lax.ppermute(array, 'ctx', pairs)  64.1 us
    pallas_call x4, Pallas kernels, hidden_group(): pl.pallas_call(kernel, grid=(tiles,), in_specs=source_specs + [pl.BlockSp...  52.9 us
    dot_general x6, matrix products, rows_product(): jnp.einsum('ri,rj->ij', left, right, preferred_element_type=F32)  42 us
    pallas_call x2, Pallas kernels, mlp_back(): pl.pallas_call(mlp_back_kernel, grid=(1,), in_specs=[pl.BlockSpec((height...  41.6 us
    pallas_call x1, Pallas kernels, attend_back(): pl.pallas_call(functools.partial(attend_back_kernel, chips), grid_spec=pl...  34.6 us
    ppermute x23, starting transfers between devices, swap_seq(): return lax.ppermute(array, 'seq', [(i, i ^ bit) for i in range(seq)])  27.5 us
  transfers between devices with their start and end apart: 75, of which 38 were waited for; matrix products, arithmetic and copies ran while one was open for 15% of the time, Pallas kernels for 28%

profile of v6, /device:TPU:0, one launch (start us, length us, event | category | flops | bytes accessed | tf_op | source)
XLA Modules:
  0.0 727.3 jit_solution(3267727517339925819)
XLA Ops:
  23.4 12.5 %collective-permute-done.2.refs_7_ = bf16[128,2688]{1,0:T(8,128)(2,1)S(1)} collective-permute-done((bf16[128,2688]{1,0:T(8,128)(2,1)}, bf16[128,2688]{1,0:T(8,128)(2,1)S(1)}, u32[]{:S(2)}, u32[]{:S(2)}) %collective-permute-start.2) | collective-permute-done | bytes 688160 | tf_op jit(solution)/shard_map/ppermute | solution.py:44
  42.8 12.7 %collective-permute-done.5.refs_8_ = bf16[128,2688]{1,0:T(8,128)(2,1)} collective-permute-done((bf16[128,2688]{1,0:T(8,128)(2,1)S(1)}, bf16[128,2688]{1,0:T(8,128)(2,1)}, u32[]{:S(2)}, u32[]{:S(2)}) %collective-permute-start.5) | collective-permute-done | bytes 688160 | tf_op jit(solution)/shard_map/ppermute | solution.py:44
  58.8 14.3 %collective-permute-done.8.refs_9_ = bf16[128,2688]{1,0:T(8,128)(2,1)} collective-permute-done((bf16[128,2688]{1,0:T(8,128)(2,1)}, bf16[128,2688]{1,0:T(8,128)(2,1)}, u32[]{:S(2)}, u32[]{:S(2)}) %collective-permute-start.8) | collective-permute-done | bytes 688160 | tf_op jit(solution)/shard_map/ppermute | solution.py:44
  79.2 11.5 %collective-permute-done.9.refs_12_ = bf16[128,2688]{1,0:T(8,128)(2,1)} collective-permute-done((bf16[128,2688]{1,0:T(8,128)(2,1)}, bf16[128,2688]{1,0:T(8,128)(2,1)}, u32[]{:S(2)}, u32[]{:S(2)}) %collective-permute-start.9) | collective-permute-done | bytes 688160 | tf_op jit(solution)/shard_map/ppermute | solution.py:33
  97.3 11.6 %collective-permute-done.14.refs_18_ = bf16[128,2688]{1,0:T(8,128)(2,1)S(1)} collective-permute-done((bf16[128,2688]{1,0:T(8,128)(2,1)S(1)}, bf16[128,2688]{1,0:T(8,128)(2,1)S(1)}, u32[]{:S(2)}, u32[]{:S(2)}) %collective-permute-start.14) | collective-permute-done | bytes 688160 | tf_op jit(solution)/shard_map/ppermute | solution.py:33
  114.7 9.2 %collective-permute-done.12.refs_16_ = bf16[128,2688]{1,0:T(8,128)(2,1)} collective-permute-done((bf16[128,2688]{1,0:T(8,128)(2,1)}, bf16[128,2688]{1,0:T(8,128)(2,1)}, u32[]{:S(2)}, u32[]{:S(2)}) %collective-permute-start.12) | collective-permute-done | bytes 688160 | tf_op jit(solution)/shard_map/ppermute | solution.py:33
  123.8 10.4 %collective-permute-done.16.refs_20_ = bf16[128,2688]{1,0:T(8,128)(2,1)} collective-permute-done((bf16[128,2688]{1,0:T(8,128)(2,1)}, bf16[128,2688]{1,0:T(8,128)(2,1)}, u32[]{:S(2)}, u32[]{:S(2)}) %collective-permute-start.16) | collective-permute-done | bytes 688160 | tf_op jit(solution)/shard_map/ppermute | solution.py:33
  138.1 14.0 %shard_map.205 = (bf16[512,512]{1,0:T(8,128)(2,1)}, bf16[512,2048]{1,0:T(8,128)(2,1)}, f32[8,2048]{1,0:T(8,128)}, bf16[2048,2688]{1,0:T(8,128)(2,1)}) custom-call(s32[1]{0:T(128)} %bitcast.1.core_ref.refs_0_, s32[16]{0:T(128)} %mul.187.refs_1_.starts, bf16[256,2048]{1,0:T(8,128)(2,1)} %bitcast.68, bf16[256,2048]{1,0:T(8,128)(2,1)} %collective-permute-done.refs_3_, ...), custom_call_target="tpu_custom_call" | custom-call | flops 33822867456 | bytes 26214400 | tf_op jit(solution)/shard_map/pallas_call | solution.py:247
  152.4 11.9 %collective-permute-done.18.refs_1_ = bf16[512,512]{1,0:T(8,128)(2,1)S(1)} collective-permute-done((bf16[512,512]{1,0:T(8,128)(2,1)}, bf16[512,512]{1,0:T(8,128)(2,1)S(1)}, u32[]{:S(2)}, u32[]{:S(2)}) %collective-permute-start.18) | collective-permute-done | bytes 524320 | tf_op jit(solution)/shard_map/ppermute | solution.py:44
  166.6 10.3 %collective-permute-done.19.refs_2_ = bf16[512,512]{1,0:T(8,128)(2,1)S(1)} collective-permute-done((bf16[512,512]{1,0:T(8,128)(2,1)S(1)}, bf16[512,512]{1,0:T(8,128)(2,1)S(1)}, u32[]{:S(2)}, u32[]{:S(2)}) %collective-permute-start.19) | collective-permute-done | bytes 524320 | tf_op jit(solution)/shard_map/ppermute | solution.py:44
  178.3 9.7 %shard_map.206.q_ref = bf16[512,1024]{1,0:T(8,128)(2,1)} custom-call(bf16[512,2048]{1,0:T(8,128)(2,1)} %get-tuple-element.102.normed.refs_0_, f32[512,128]{1,0:T(8,128)} %bitcast.75, f32[512,128]{1,0:T(8,128)} %bitcast.78, bf16[2048,2688]{1,0:T(8,128)(2,1)} %get-tuple-element.145.w.w_all.w_ref.wq_ref.wkv_ref), custom_call_target="tpu_custom_call" | custom-call | flops 12884901888 | bytes 10485760 | tf_op jit(solution)/shard_map/pallas_call | solution.py:288
  192.7 25.9 %shard_map.207 = (bf16[512,1024]{1,0:T(8,128)(2,1)}, f32[32,256]{1,0:T(8,128)}) custom-call(s32[2]{0:T(128)} %bitcast.96, s32[1024,1]{1,0:T(8,128)} %bitcast.80, s32[1,256]{1,0:T(1,128)} %iota_add_fusion.qpos_ref, bf16[512,1024]{1,0:T(8,128)(2,1)} %shard_map.206.q_ref, bf16[512,512]{1,0:T(8,128)(2,1)} %get-tuple-element.104.refs_0_, ...), custom_call_target="tpu_custom_call" | custom-call | flops 51539607552 | bytes 4194304 | tf_op jit(solution)/shard_map/pallas_call | solution.py:353
  222.6 9.1 %shard_map.208 = (f32[256,1024]{1,0:T(8,128)}, f32[256,1024]{1,0:T(8,128)}) custom-call(s32[1]{0:T(128)} %bitcast.1.core_ref.refs_0_, bf16[512,1024]{1,0:T(8,128)(2,1)} %get-tuple-element.107.o_mine.refs_0_, bf16[512,1024]{1,0:T(8,128)(2,1)} %copy-done.42, bf16[2048,2688]{1,0:T(8,128)(2,1)} %get-tuple-element.145.w.w_all.w_ref.wq_ref.wkv_ref), custom_call_target="tpu_custom_call" | custom-call | flops 12884901888 | bytes 10485760 | tf_op jit(solution)/shard_map/pallas_call | solution.py:503
  233.5 11.1 %collective-permute-done.24.refs_3_ = bf16[256,2048]{1,0:T(8,128)(2,1)} collective-permute-done((bf16[256,2048]{1,0:T(8,128)(2,1)}, bf16[256,2048]{1,0:T(8,128)(2,1)}, u32[]{:S(2)}, u32[]{:S(2)}) %collective-permute-start.24) | collective-permute-done | bytes 1048608 | tf_op jit(solution)/shard_map/ppermute | solution.py:44
  252.1 23.1 %collective-permute-done.25.refs_2_ = bf16[256,2048]{1,0:T(8,128)(2,1)S(1)} collective-permute-done((bf16[256,2048]{1,0:T(8,128)(2,1)S(1)}, bf16[256,2048]{1,0:T(8,128)(2,1)S(1)}, u32[]{:S(2)}, u32[]{:S(2)}) %collective-permute-start.25) | collective-permute-done | bytes 1048608 | tf_op jit(solution)/shard_map/ppermute | solution.py:44
  277.8 14.1 %shard_map.209 = (bf16[1024,2048]{1,0:T(8,128)(2,1)}, bf16[1024,2048]{1,0:T(8,128)(2,1)}, bf16[1024,1024]{1,0:T(8,128)(2,1)}, bf16[1024,1024]{1,0:T(8,128)(2,1)}, bf16[1024,1024]{1,0:T(8,128)(2,1)}) custom-call(bf16[256,2048]{1,0:T(8,128)(2,1)} %copy-done.22, bf16[256,2048]{1,0:T(8,128)(2,1)} %copy-done.20, bf16[256,2048]{1,0:T(8,128)(2,1)} %copy-done.45, ...), custom_call_target="tpu_custom_call" | custom-call | flops 38654705664 | bytes 25165824 | tf_op jit(solution)/shard_map/pallas_call | solution.py:583
  291.9 9.8 %collective-permute-done.26.refs_0_ = bf16[256,2048]{1,0:T(8,128)(2,1)S(1)} collective-permute-done((bf16[256,2048]{1,0:T(8,128)(2,1)S(1)}, bf16[256,2048]{1,0:T(8,128)(2,1)S(1)}, u32[]{:S(2)}, u32[]{:S(2)}) %collective-permute-start.26) | collective-permute-done | bytes 1048608 | tf_op jit(solution)/shard_map/ppermute | solution.py:44
  304.6 12.3 %shard_map.210 = (bf16[1024,1024]{1,0:T(8,128)(2,1)}, bf16[1024,1024]{1,0:T(8,128)(2,1)}, bf16[1024,1024]{1,0:T(8,128)(2,1)}) custom-call(bf16[1024,2048]{1,0:T(8,128)(2,1)} %get-tuple-element.117.x.refs_7_, bf16[1024,2048]{1,0:T(8,128)(2,1)} %get-tuple-element.118.d.refs_8_, bf16[2048,3072]{1,0:T(8,128)(2,1)} %collective-permute-done.27.gate.up.down_t.refs_7_, ...), custom_call_target="tpu_custom_call" | custom-call | flops 38654705664 | bytes 25165824 | tf_op jit(solution)/shard_map/pallas_call | solution.py:583
  316.9 20.8 %shard_map.211 = (bf16[512,2048]{1,0:T(8,128)(2,1)}, bf16[512,2048]{1,0:T(8,128)(2,1)}) custom-call(bf16[1024,1024]{1,0:T(8,128)(2,1)} %get-tuple-element.114.refs_0_.refs_9_, bf16[1024,1024]{1,0:T(8,128)(2,1)} %get-tuple-element.115.refs_1_.refs_10_, bf16[1024,1024]{1,0:T(8,128)(2,1)} %get-tuple-element.116.refs_2_.refs_11_, ...), custom_call_target="tpu_custom_call" | custom-call | flops 77309411328 | bytes 39845888 | tf_op jit(solution)/shard_map/pallas_call | solution.py:640
  340.1 14.2 %shard_map.212 = (bf16[1024,2048]{1,0:T(8,128)(2,1)}, bf16[1024,2048]{1,0:T(8,128)(2,1)}, bf16[1024,1024]{1,0:T(8,128)(2,1)}, bf16[1024,1024]{1,0:T(8,128)(2,1)}, bf16[1024,1024]{1,0:T(8,128)(2,1)}) custom-call(bf16[256,2048]{1,0:T(8,128)(2,1)} %copy-done.43, ...), custom_call_target="tpu_custom_call", output_to_operand_aliasing={{0}: (7, {}), {1}: (8, {}), {2}: (9, {}), {3}: (10, {}), {4... | custom-call | flops 38654705664 | bytes 25165824 | tf_op jit(solution)/shard_map/pallas_call | solution.py:583
  354.4 12.3 %shard_map.213 = (bf16[1024,1024]{1,0:T(8,128)(2,1)}, bf16[1024,1024]{1,0:T(8,128)(2,1)}, bf16[1024,1024]{1,0:T(8,128)(2,1)}) custom-call(bf16[1024,2048]{1,0:T(8,128)(2,1)} %get-tuple-element.140.x, bf16[1024,2048]{1,0:T(8,128)(2,1)} %get-tuple-element.139.d, ...), custom_call_target="tpu_custom_call", output_to_operand_aliasing={{0}: (5, {}), {1}: (6, {}), {2}: (7, {})} | custom-call | flops 38654705664 | bytes 25165824 | tf_op jit(solution)/shard_map/pallas_call | solution.py:583
  366.7 20.8 %shard_map.214 = (bf16[512,2048]{1,0:T(8,128)(2,1)}, bf16[512,2048]{1,0:T(8,128)(2,1)}) custom-call(bf16[1024,1024]{1,0:T(8,128)(2,1)} %get-tuple-element.138.refs_0_, bf16[1024,1024]{1,0:T(8,128)(2,1)} %get-tuple-element.141.refs_1_, bf16[1024,1024]{1,0:T(8,128)(2,1)} %get-tuple-element.143.refs_2_, bf16[1024,1024]{1,0:T(8,128)(2,1)} %get-tuple-element.132.refs_3_, ...), custom_call_target="tpu_custom_call" | custom-call | flops 77309411328 | bytes 39845888 | tf_op jit(solution)/shard_map/pallas_call | solution.py:640
  389.4 8.7 %convolution_convert_fusion.2 = bf16[2048,1024]{1,0:T(8,128)(2,1)} fusion(bf16[1024,2048]{1,0:T(8,128)(2,1)} %get-tuple-element.140.x, bf16[1024,1024]{1,0:T(8,128)(2,1)S(1)} %copy-done.61), kind=kOutput, calls=%fused_computation.5 | convolution fusion | flops 4297064448 | bytes 10485760 | tf_op jit(solution)/shard_map/ri,rj->ij/dot_general | solution.py:945
  431.0 7.4 %convolution_convert_fusion.5 = bf16[1024,2048]{1,0:T(8,128)(2,1)S(1)} fusion(bf16[1024,1024]{1,0:T(8,128)(2,1)S(1)} %copy-done.56, bf16[1024,2048]{1,0:T(8,128)(2,1)} %get-tuple-element.139.d), kind=kOutput, calls=%fused_computation.8 | convolution fusion | flops 4297064448 | bytes 10485760 | tf_op jit(solution)/shard_map/ri,rj->ij/dot_general | solution.py:945
  445.3 8.0 %collective-permute-done.31 = bf16[256,2048]{1,0:T(8,128)(2,1)S(1)} collective-permute-done((bf16[256,2048]{1,0:T(8,128)(2,1)S(1)}, bf16[256,2048]{1,0:T(8,128)(2,1)S(1)}, u32[]{:S(2)}, u32[]{:S(2)}) %collective-permute-start.31) | collective-permute-done | bytes 1048608 | tf_op jit(solution)/shard_map/ppermute | solution.py:44
  469.1 8.9 %shard_map.215 = (f32[512,1024]{1,0:T(8,128)}, bf16[512,1024]{1,0:T(8,128)(2,1)}, bf16[512,1024]{1,0:T(8,128)(2,1)}) custom-call(s32[1]{0:T(128)} %bitcast.1.core_ref.refs_0_, bf16[256,1024]{1,0:T(8,128)(2,1)} %get-tuple-element.223.d_own, bf16[256,1024]{1,0:T(8,128)(2,1)} %copy-done.54, bf16[2048,2688]{1,0:T(8,128)(2,1)} %get-tuple-element.145.w.w_all.w_ref.wq_ref.wkv_ref), custom_call_target="tpu_custom_call" | custom-call | flops 12884901888 | bytes 10485760 | tf_op jit(solution)/shard_map/pallas_call | solution.py:689
  504.2 7.6 %add_convert_fusion = bf16[2048,1024]{1,0:T(8,128)(2,1)} fusion(bf16[2048,1024]{1,0:T(8,128)(2,1)} %collective-permute-done.38, bf16[2048,1024]{1,0:T(8,128)(2,1)} %convolution_convert_fusion.1), kind=kLoop, calls=%fused_computation | loop fusion | flops 8388608 | bytes 12582912 | tf_op jit(solution)/shard_map/convert_element_type | solution.py:959
  511.9 34.6 %shard_map.216 = (bf16[512,1024]{1,0:T(8,128)(2,1)}, bf16[512,512]{1,0:T(8,128)(2,1)}, bf16[512,512]{1,0:T(8,128)(2,1)}, bf16[512,512]{1,0:T(8,128)(2,1)}, bf16[512,512]{1,0:T(8,128)(2,1)}) custom-call(s32[2]{0:T(128)} %bitcast.97, s32[1024,1]{1,0:T(8,128)} %bitcast.81, s32[1,256]{1,0:T(1,128)} %iota_add_fusion.qpos_ref, ...), custom_call_target="tpu_custom_call" | custom-call | flops 128849018880 | bytes 9437184 | tf_op jit(solution)/shard_map/pallas_call | solution.py:432
  576.3 13.8 %collective-permute-done.51 = bf16[512,1024]{1,0:T(8,128)(2,1)S(1)} collective-permute-done((bf16[512,1024]{1,0:T(8,128)(2,1)}, bf16[512,1024]{1,0:T(8,128)(2,1)S(1)}, u32[]{:S(2)}, u32[]{:S(2)}) %collective-permute-start.51) | collective-permute-done | bytes 1048608 | tf_op jit(solution)/shard_map/ppermute | solution.py:33
  592.0 20.8 %collective-permute-done.66 = bf16[512,1024]{1,0:T(8,128)(2,1)} collective-permute-done((bf16[512,1024]{1,0:T(8,128)(2,1)}, bf16[512,1024]{1,0:T(8,128)(2,1)}, u32[]{:S(2)}, u32[]{:S(2)}) %collective-permute-start.66) | collective-permute-done | bytes 1048608 | tf_op jit(solution)/shard_map/ppermute | solution.py:33
  620.2 7.7 %shard_map.218 = (f32[256,2048]{1,0:T(8,128)}, bf16[256,2048]{1,0:T(8,128)(2,1)}) custom-call(s32[1]{0:T(128)} %bitcast.1.core_ref.refs_0_, bf16[512,1024]{1,0:T(8,128)(2,1)} %get-tuple-element.155.dq_ref.refs_1_, bf16[512,512]{1,0:T(8,128)(2,1)} %shard_map.217.dkv_ref.refs_1_, bf16[2048,2688]{1,0:T(8,128)(2,1)} %get-tuple-element.145.w.w_all.w_ref.wq_ref.wkv_ref, ...), custom_call_target="tpu_custom_call" | custom-call | flops 19327352832 | bytes 10485760 | tf_op jit(solution)/shard_map/pallas_call | solution.py:768
  650.9 13.4 %collective-permute-done.41 = bf16[256,2048]{1,0:T(8,128)(2,1)S(1)} collective-permute-done((bf16[256,2048]{1,0:T(8,128)(2,1)}, bf16[256,2048]{1,0:T(8,128)(2,1)S(1)}, u32[]{:S(2)}, u32[]{:S(2)}) %collective-permute-start.41) | collective-permute-done | bytes 1048608 | tf_op jit(solution)/shard_map/ppermute | solution.py:44
  (366 shorter events, 279.7 us)
Async XLA Ops:
  7.2 268.0 %all-gather.2.cloned.1.call-start = ((), (), s32[]{:S(2)}) async-start(), calls=%async_computation.3 | async-start | bytes 15728640 | tf_op jit(solution)/shard_map/all_gather | solution.py:883
  77.2 31.8 %collective-permute-start.14 = (bf16[128,2688]{1,0:T(8,128)(2,1)S(1)}, bf16[128,2688]{1,0:T(8,128)(2,1)S(1)}, u32[]{:S(2)}, u32[]{:S(2)}) collective-permute-start(bf16[128,2688]{1,0:T(8,128)(2,1)S(1)} %copy-done.48), channel_id=1, source_target_pairs={{0,16},{8,24},{16,0},{24,8},{1,17},{9,25},{17,1},{25,9},{2,18},{10... | collective-permute-start | bytes 2064392 | tf_op jit(solution)/shard_map/ppermute | solution.py:33
  77.7 46.1 %collective-permute-start.12 = (bf16[128,2688]{1,0:T(8,128)(2,1)}, bf16[128,2688]{1,0:T(8,128)(2,1)}, u32[]{:S(2)}, u32[]{:S(2)}) collective-permute-start(bf16[128,2688]{1,0:T(8,128)(2,1)} %collective-permute-done.5.refs_8_), channel_id=1, source_target_pairs={{0,16},{8,24},{16,0},{24,8},{1,17},{9,25},{17,1},{25,9},{2,18},{10... | collective-permute-start | bytes 2064392 | tf_op jit(solution)/shard_map/ppermute | solution.py:33
  90.7 33.1 %collective-permute-start.15 = (bf16[128,2688]{1,0:T(8,128)(2,1)}, bf16[128,2688]{1,0:T(8,128)(2,1)}, u32[]{:S(2)}, u32[]{:S(2)}) collective-permute-start(bf16[128,2688]{1,0:T(8,128)(2,1)} %collective-permute-done.7.refs_15_), channel_id=1, source_target_pairs={{0,8},{8,0},{16,24},{24,16},{1,9},{9,1},{17,25},{25,17},{2,10},{10... | collective-permute-start | bytes 2064392 | tf_op jit(solution)/shard_map/ppermute | solution.py:33
  94.3 39.9 %collective-permute-start.16 = (bf16[128,2688]{1,0:T(8,128)(2,1)}, bf16[128,2688]{1,0:T(8,128)(2,1)}, u32[]{:S(2)}, u32[]{:S(2)}) collective-permute-start(bf16[128,2688]{1,0:T(8,128)(2,1)} %collective-permute-done.9.refs_12_), channel_id=1, source_target_pairs={{0,16},{8,24},{16,0},{24,8},{1,17},{9,25},{17,1},{25,9},{2,18},{10... | collective-permute-start | bytes 2064392 | tf_op jit(solution)/shard_map/ppermute | solution.py:33
  95.9 38.3 %collective-permute-start.17 = (bf16[128,2688]{1,0:T(8,128)(2,1)}, bf16[128,2688]{1,0:T(8,128)(2,1)}, u32[]{:S(2)}, u32[]{:S(2)}) collective-permute-start(bf16[128,2688]{1,0:T(8,128)(2,1)} %collective-permute-done.13.refs_17_), channel_id=1, source_target_pairs={{0,8},{8,0},{16,24},{24,16},{1,9},{9,1},{17,25},{25,17},{2,10},{10... | collective-permute-start | bytes 2064392 | tf_op jit(solution)/shard_map/ppermute | solution.py:33
  134.2 577.9 %reduce-scatter.4.cloned.1.call-start = ((), (), s32[]{:S(2)}) async-start(), calls=%async_computation.4 | async-start | bytes 5242880 | tf_op jit(solution)/shard_map/reduce_scatter | solution.py:948
  190.1 28.6 %collective-permute-start.21 = (bf16[256,2048]{1,0:T(8,128)(2,1)S(1)}, bf16[256,2048]{1,0:T(8,128)(2,1)}, u32[]{:S(2)}, u32[]{:S(2)}) collective-permute-start(bf16[256,2048]{1,0:T(8,128)(2,1)S(1)} %copy-done.41), channel_id=1, source_target_pairs={{0,4},{1,5},{4,6},{5,7},{6,2},{7,3},{2,0},{3,1},{8,12},{9,13},{12,... | collective-permute-start | bytes 3145736 | tf_op jit(solution)/shard_map/ppermute | solution.py:44
  218.8 25.9 %collective-permute-start.24 = (bf16[256,2048]{1,0:T(8,128)(2,1)}, bf16[256,2048]{1,0:T(8,128)(2,1)}, u32[]{:S(2)}, u32[]{:S(2)}) collective-permute-start(bf16[256,2048]{1,0:T(8,128)(2,1)} %collective-permute-done.21.refs_1_), channel_id=1, source_target_pairs={{0,4},{1,5},{4,6},{5,7},{6,2},{7,3},{2,0},{3,1},{8,12},{9,13},{12,... | collective-permute-start | bytes 3145736 | tf_op jit(solution)/shard_map/ppermute | solution.py:44
  275.2 29.4 %collective-permute-start.27 = (bf16[2048,3072]{1,0:T(8,128)(2,1)}, bf16[2048,3072]{1,0:T(8,128)(2,1)}, u32[]{:S(2)}, u32[]{:S(2)}) collective-permute-start(bf16[2048,3072]{1,0:T(8,128)(2,1)} %all-gather.2.cloned.1.call-done.refs_4_.refs_5_.refs_6_), channel_id=1, source_target_pairs={{0,1},{1,0},{2,3},{3,2},{4,5},{5,4},{6,7},{7,6},{8,9},{9,8},{10,11... | collective-permute-start | bytes 37748744 | tf_op jit(solution)/shard_map/ppermute | solution.py:28
  275.2 26.4 %collective-permute-start.26 = (bf16[256,2048]{1,0:T(8,128)(2,1)S(1)}, bf16[256,2048]{1,0:T(8,128)(2,1)S(1)}, u32[]{:S(2)}, u32[]{:S(2)}) collective-permute-start(bf16[256,2048]{1,0:T(8,128)(2,1)S(1)} %collective-permute-done.25.refs_2_), channel_id=1, source_target_pairs={{0,4},{1,5},{4,6},{5,7},{6,2},{7,3},{2,0},{3,1},{8,12},{9,13},{12,... | collective-permute-start | bytes 3145736 | tf_op jit(solution)/shard_map/ppermute | solution.py:44
  301.7 37.5 %collective-permute-start.29 = (bf16[256,2048]{1,0:T(8,128)(2,1)S(1)}, bf16[256,2048]{1,0:T(8,128)(2,1)S(1)}, u32[]{:S(2)}, u32[]{:S(2)}) collective-permute-start(bf16[256,2048]{1,0:T(8,128)(2,1)S(1)} %collective-permute-done.26.refs_0_), channel_id=1, source_target_pairs={{0,4},{1,5},{4,6},{5,7},{6,2},{7,3},{2,0},{3,1},{8,12},{9,13},{12,... | collective-permute-start | bytes 3145736 | tf_op jit(solution)/shard_map/ppermute | solution.py:44
  339.1 27.6 %collective-permute-start.28 = (bf16[256,2048]{1,0:T(8,128)(2,1)S(1)}, bf16[256,2048]{1,0:T(8,128)(2,1)S(1)}, u32[]{:S(2)}, u32[]{:S(2)}) collective-permute-start(bf16[256,2048]{1,0:T(8,128)(2,1)S(1)} %slice.126), channel_id=1, source_target_pairs={{0,4},{1,5},{4,6},{5,7},{6,2},{7,3},{2,0},{3,1},{8,12},{9,13},{12,... | collective-permute-start | bytes 3145736 | tf_op jit(solution)/shard_map/ppermute | solution.py:44
  399.7 26.1 %collective-permute-start.30 = (bf16[256,2048]{1,0:T(8,128)(2,1)S(1)}, bf16[256,2048]{1,0:T(8,128)(2,1)}, u32[]{:S(2)}, u32[]{:S(2)}) collective-permute-start(bf16[256,2048]{1,0:T(8,128)(2,1)S(1)} %add_convert_fusion.9), channel_id=1, source_target_pairs={{0,4},{1,5},{4,6},{5,7},{6,2},{7,3},{2,0},{3,1},{8,12},{9,13},{12,... | collective-permute-start | bytes 3145736 | tf_op jit(solution)/shard_map/ppermute | solution.py:44
  422.4 292.6 %reduce-scatter.8.cloned.1.call-start = ((), (), s32[]{:S(2)}) async-start(), calls=%async_computation.6 | async-start | bytes 5242880 | tf_op jit(solution)/shard_map/reduce_scatter | solution.py:948
  427.4 25.8 %collective-permute-start.31 = (bf16[256,2048]{1,0:T(8,128)(2,1)S(1)}, bf16[256,2048]{1,0:T(8,128)(2,1)S(1)}, u32[]{:S(2)}, u32[]{:S(2)}) collective-permute-start(bf16[256,2048]{1,0:T(8,128)(2,1)S(1)} %add_convert_fusion.8), channel_id=1, source_target_pairs={{0,4},{1,5},{4,6},{5,7},{6,2},{7,3},{2,0},{3,1},{8,12},{9,13},{12,... | collective-permute-start | bytes 3145736 | tf_op jit(solution)/shard_map/ppermute | solution.py:44
  438.4 55.7 %collective-permute-start.36 = (bf16[1024,2048]{1,0:T(8,128)(2,1)}, bf16[1024,2048]{1,0:T(8,128)(2,1)}, u32[]{:S(2)}, u32[]{:S(2)}) collective-permute-start(bf16[1024,2048]{1,0:T(8,128)(2,1)} %convolution_convert_fusion.4), channel_id=1, source_target_pairs={{0,1},{1,0},{2,3},{3,2},{4,5},{5,4},{6,7},{7,6},{8,9},{9,8},{10,11... | collective-permute-start | bytes 12582920 | tf_op jit(solution)/shard_map/ppermute | solution.py:28
  444.8 59.4 %collective-permute-start.38 = (bf16[2048,1024]{1,0:T(8,128)(2,1)}, bf16[2048,1024]{1,0:T(8,128)(2,1)}, u32[]{:S(2)}, u32[]{:S(2)}) collective-permute-start(bf16[2048,1024]{1,0:T(8,128)(2,1)} %convolution_convert_fusion), channel_id=1, source_target_pairs={{0,1},{1,0},{2,3},{3,2},{4,5},{5,4},{6,7},{7,6},{8,9},{9,8},{10,11... | collective-permute-start | bytes 12582920 | tf_op jit(solution)/shard_map/ppermute | solution.py:28
  464.9 25.9 %collective-permute-start.32 = (bf16[256,2048]{1,0:T(8,128)(2,1)}, bf16[256,2048]{1,0:T(8,128)(2,1)S(1)}, u32[]{:S(2)}, u32[]{:S(2)}) collective-permute-start(bf16[256,2048]{1,0:T(8,128)(2,1)} %slice.125), channel_id=1, source_target_pairs={{0,4},{1,5},{4,6},{5,7},{6,2},{7,3},{2,0},{3,1},{8,12},{9,13},{12,... | collective-permute-start | bytes 3145736 | tf_op jit(solution)/shard_map/ppermute | solution.py:44
  484.0 82.4 %collective-permute-start.64 = (bf16[512,1024]{1,0:T(8,128)(2,1)}, bf16[512,1024]{1,0:T(8,128)(2,1)}, u32[]{:S(2)}, u32[]{:S(2)}) collective-permute-start(bf16[512,1024]{1,0:T(8,128)(2,1)} %get-tuple-element.172), channel_id=1, source_target_pairs={{0,16},{8,24},{16,0},{24,8},{1,17},{9,25},{17,1},{25,9},{2,18},{10... | collective-permute-start | bytes 3145736 | tf_op jit(solution)/shard_map/ppermute | solution.py:33
  490.8 62.5 %collective-permute-start.65 = (bf16[512,1024]{1,0:T(8,128)(2,1)}, bf16[512,1024]{1,0:T(8,128)(2,1)}, u32[]{:S(2)}, u32[]{:S(2)}) collective-permute-start(bf16[512,1024]{1,0:T(8,128)(2,1)} %get-tuple-element.175), channel_id=1, source_target_pairs={{0,16},{8,24},{16,0},{24,8},{1,17},{9,25},{17,1},{25,9},{2,18},{10... | collective-permute-start | bytes 3145736 | tf_op jit(solution)/shard_map/ppermute | solution.py:33
  494.2 52.3 %collective-permute-start.34 = (bf16[256,2048]{1,0:T(8,128)(2,1)}, bf16[256,2048]{1,0:T(8,128)(2,1)S(1)}, u32[]{:S(2)}, u32[]{:S(2)}) collective-permute-start(bf16[256,2048]{1,0:T(8,128)(2,1)} %add_convert_fusion.7), channel_id=1, source_target_pairs={{0,4},{1,5},{4,6},{5,7},{6,2},{7,3},{2,0},{3,1},{8,12},{9,13},{12,... | collective-permute-start | bytes 3145736 | tf_op jit(solution)/shard_map/ppermute | solution.py:44
  504.2 213.6 %reduce-scatter.6.cloned.1.call-start = ((), (), s32[]{:S(2)}) async-start(), calls=%async_computation.5 | async-start | bytes 5242880 | tf_op jit(solution)/shard_map/reduce_scatter | solution.py:948
  552.6 37.5 %collective-permute-start.51 = (bf16[512,1024]{1,0:T(8,128)(2,1)}, bf16[512,1024]{1,0:T(8,128)(2,1)S(1)}, u32[]{:S(2)}, u32[]{:S(2)}) collective-permute-start(bf16[512,1024]{1,0:T(8,128)(2,1)} %get-tuple-element.163), channel_id=1, source_target_pairs={{0,8},{8,0},{16,24},{24,16},{1,9},{9,1},{17,25},{25,17},{2,10},{10... | collective-permute-start | bytes 3145736 | tf_op jit(solution)/shard_map/ppermute | solution.py:33
  564.4 48.3 %collective-permute-start.66 = (bf16[512,1024]{1,0:T(8,128)(2,1)}, bf16[512,1024]{1,0:T(8,128)(2,1)}, u32[]{:S(2)}, u32[]{:S(2)}) collective-permute-start(bf16[512,1024]{1,0:T(8,128)(2,1)} %add_convert_fusion.3), channel_id=1, source_target_pairs={{0,8},{8,0},{16,24},{24,16},{1,9},{9,1},{17,25},{25,17},{2,10},{10... | collective-permute-start | bytes 3145736 | tf_op jit(solution)/shard_map/ppermute | solution.py:33
  564.5 73.1 %collective-permute-start.50 = (bf16[512,1024]{1,0:T(8,128)(2,1)}, bf16[512,1024]{1,0:T(8,128)(2,1)}, u32[]{:S(2)}, u32[]{:S(2)}) collective-permute-start(bf16[512,1024]{1,0:T(8,128)(2,1)} %get-tuple-element.161), channel_id=1, source_target_pairs={{0,8},{8,0},{16,24},{24,16},{1,9},{9,1},{17,25},{25,17},{2,10},{10... | collective-permute-start | bytes 3145736 | tf_op jit(solution)/shard_map/ppermute | solution.py:33
  572.9 44.0 %collective-permute-start.42 = (bf16[512,512]{1,0:T(8,128)(2,1)S(1)}, bf16[512,512]{1,0:T(8,128)(2,1)S(1)}, u32[]{:S(2)}, u32[]{:S(2)}) collective-permute-start(bf16[512,512]{1,0:T(8,128)(2,1)S(1)} %add_convert_fusion.11), channel_id=1, source_target_pairs={{0,4},{1,5},{4,6},{5,7},{6,2},{7,3},{2,0},{3,1},{8,12},{9,13},{12,... | collective-permute-start | bytes 1572872 | tf_op jit(solution)/shard_map/ppermute | solution.py:44
  591.5 55.6 %collective-permute-start.52 = (bf16[512,1024]{1,0:T(8,128)(2,1)}, bf16[512,1024]{1,0:T(8,128)(2,1)}, u32[]{:S(2)}, u32[]{:S(2)}) collective-permute-start(bf16[512,1024]{1,0:T(8,128)(2,1)} %add_convert_fusion.4), channel_id=1, source_target_pairs={{0,16},{8,24},{16,0},{24,8},{1,17},{9,25},{17,1},{25,9},{2,18},{10... | collective-permute-start | bytes 3145736 | tf_op jit(solution)/shard_map/ppermute | solution.py:33
  635.1 29.3 %collective-permute-start.41 = (bf16[256,2048]{1,0:T(8,128)(2,1)}, bf16[256,2048]{1,0:T(8,128)(2,1)S(1)}, u32[]{:S(2)}, u32[]{:S(2)}) collective-permute-start(bf16[256,2048]{1,0:T(8,128)(2,1)} %add_convert_fusion.6), channel_id=1, source_target_pairs={{0,4},{1,5},{4,6},{5,7},{6,2},{7,3},{2,0},{3,1},{8,12},{9,13},{12,... | collective-permute-start | bytes 3145736 | tf_op jit(solution)/shard_map/ppermute | solution.py:44
  637.6 30.0 %collective-permute-start.43 = (bf16[256,2048]{1,0:T(8,128)(2,1)}, bf16[256,2048]{1,0:T(8,128)(2,1)S(1)}, u32[]{:S(2)}, u32[]{:S(2)}) collective-permute-start(bf16[256,2048]{1,0:T(8,128)(2,1)} %get-tuple-element.159), channel_id=1, source_target_pairs={{0,1},{1,0},{2,3},{3,2},{4,5},{5,4},{6,7},{7,6},{8,9},{9,8},{10,11... | collective-permute-start | bytes 3145736 | tf_op jit(solution)/shard_map/ppermute | solution.py:28
  647.2 26.1 %collective-permute-start.59 = (bf16[512,512]{1,0:T(8,128)(2,1)S(1)}, bf16[512,512]{1,0:T(8,128)(2,1)S(1)}, u32[]{:S(2)}, u32[]{:S(2)}) collective-permute-start(bf16[512,512]{1,0:T(8,128)(2,1)S(1)} %add_convert_fusion.10), channel_id=1, source_target_pairs={{0,8},{8,0},{16,24},{24,16},{1,9},{9,1},{17,25},{25,17},{2,10},{10... | collective-permute-start | bytes 1572872 | tf_op jit(solution)/shard_map/ppermute | solution.py:33
  667.5 26.8 %collective-permute-start.70 = (f32[64,1024]{1,0:T(8,128)S(1)}, f32[64,1024]{1,0:T(8,128)S(1)}, u32[]{:S(2)}, u32[]{:S(2)}) collective-permute-start(f32[64,1024]{1,0:T(8,128)S(1)} %get-tuple-element.225), channel_id=1, source_target_pairs={{0,1},{1,0},{2,3},{3,2},{4,5},{5,4},{6,7},{7,6},{8,9},{9,8},{10,11... | collective-permute-start | bytes 786440 | tf_op jit(solution)/shard_map/ppermute | solution.py:28
  (106 other events, 1463.3 us)
Sparse Core Ops, SparseCore 0:
  134.4 120.7 all-gather.1
  422.5 52.1 reduce-scatter.3
  504.3 81.5 reduce-scatter.7
  637.7 60.2 reduce-scatter.5
